TPU v7x, 32 devices: a whole 2x2x4 slice. The times are simulated.
32 devices in a mesh: batch: 4 (over y, x), expert: 8 (over z, core).
Axes of the slice: x: 2, y: 2, z: 4, core: 2. Of those that a mesh axis runs over, the one named last changes fastest.
Arguments:
- block_input: float32 [4, 1024, 1280], P('batch', 'expert'), may hold values from -6 to 6
- seq_ids: int32 [4, 1024], P('batch', 'expert'), may hold values from 0 to 1, as said below
- routes: int32 [4, 1024, 6], P('batch', 'expert'), may hold values from 0 to 15, all different within a row; in each aligned block of 128 rows (0 to 127, 128 to 255, ..., all dimensions but the last counted through in order) at most 72 rows name the same one
- cotangent: float32 [4, 1024, 1280], P('batch', 'expert'), may hold values from -6 to 6
- qkv_weight: float32 [1280, 3840], P(('batch', 'expert')), may hold values from -0.25 to 0.25
- out_weight: float32 [1280, 1280], P(('batch', 'expert')), may hold values from -1.25 to 1.25
- shared_up: float32 [1280, 1792], P(('batch', 'expert')), may hold values from -0.15625 to 0.15625
- shared_down: float32 [896, 1280], P(('batch', 'expert')), may hold values from -0.375 to 0.375
- router_weight: float32 [1280, 16], P(('batch', 'expert')), may hold values from -0.078125 to 0.078125
- gain_attn: float32 [1280], P(('batch', 'expert')), may hold values from 0.1 to 1.9
- gain_ffn: float32 [1280], P(('batch', 'expert')), may hold values from 0.1 to 1.9
- expert_up: float32 [16, 1280, 1792], P('expert', 'batch'), may hold values from -0.15625 to 0.15625
- expert_down: float32 [16, 896, 1280], P('expert', 'batch'), may hold values from -0.75 to 0.75
Outputs:
- block_output: float32 [4, 1024, 1280], P('batch', 'expert')
- input_grad: float32 [4, 1024, 1280], P('batch', 'expert')
- qkv_grad: float32 [1280, 3840], P(('batch', 'expert'))
- out_grad: float32 [1280, 1280], P(('batch', 'expert'))
- shared_up_grad: float32 [1280, 1792], P(('batch', 'expert'))
- shared_down_grad: float32 [896, 1280], P(('batch', 'expert'))
- router_grad: float32 [1280, 16], P(('batch', 'expert'))
- gain_attn_grad: float32 [1280], P(('batch', 'expert'))
- gain_ffn_grad: float32 [1280], P(('batch', 'expert'))
- expert_up_grad: float32 [16, 1280, 1792], P('expert', 'batch')
- expert_down_grad: float32 [16, 896, 1280], P('expert', 'batch')
Inputs may be any that keep to these rules, and one draw needn't show every extreme that they name: `seq_ids`: in each pack the ids are 0 up to a boundary and 1 from it on; the boundary lies between 384 and 640. `routes`: each row names 6 different experts; among the rows of one device no expert is named more than 72 times, and in every draw some expert is named exactly 72 times by the rows of some device.
All inputs are finite; a program needn't handle non-finite values.
Results may differ from a plain program's by a relative error of at most 0.028.
Values may be sent and summed in bfloat16 or wider, within the bound.
A program may use at most 320 MiB of HBM per device.

v0:
```python
import jax
import jax.numpy as jnp
from jax import lax
from jax.sharding import PartitionSpec as P

HEAD = 128
TOP = 6


EPSILON = 1e-06
NEGATIVE = -1e30


def rotate(values, positions, sign):
    half = values.shape[-1] // 2
    frequency = 10000.0 ** (-jnp.arange(half, dtype=jnp.float32) / half)
    angle = positions.astype(jnp.float32)[:, None] * frequency[None, :]
    cosine = jnp.cos(angle)[:, None, :]
    sine = sign * jnp.sin(angle)[:, None, :]
    first = values[..., :half]
    second = values[..., half:]
    return jnp.concatenate(
        [first * cosine - second * sine, first * sine + second * cosine], axis=-1
    )


def swiglu(pre, hidden_width):
    return jax.nn.silu(pre[..., :hidden_width]) * pre[..., hidden_width:]


def swiglu_back(pre, dhidden, hidden_width):
    gate_part = pre[..., :hidden_width]
    up_part = pre[..., hidden_width:]
    sigma = jax.nn.sigmoid(gate_part)
    dgate = dhidden * up_part * sigma * (1.0 + gate_part * (1.0 - sigma))
    dupper = dhidden * gate_part * sigma
    return jnp.concatenate([dgate, dupper], axis=-1)


def norm_back(dnormed, normed, inv_rms, gain):
    dscaled = dnormed * gain
    dinputs = inv_rms * (dscaled - normed * jnp.mean(dscaled * normed, axis=1, keepdims=True))
    return (dinputs, jnp.sum(dnormed * normed, axis=0))


def per_device(
    block_input,
    seq_ids,
    routes,
    cotangent,
    qkv_weight,
    out_weight,
    shared_up,
    shared_down,
    router_weight,
    gain_attn,
    gain_ffn,
    expert_up,
    expert_down,
):
    dense = (
        lax.all_gather(qkv_weight.astype(jnp.bfloat16), ("batch", "expert"), axis=0, tiled=True),
        lax.all_gather(out_weight.astype(jnp.bfloat16), ("batch", "expert"), axis=0, tiled=True),
        lax.all_gather(shared_up.astype(jnp.bfloat16), ("batch", "expert"), axis=0, tiled=True),
        lax.all_gather(shared_down.astype(jnp.bfloat16), ("batch", "expert"), axis=0, tiled=True),
        lax.all_gather(router_weight.astype(jnp.bfloat16), ("batch", "expert"), axis=0, tiled=True),
        lax.all_gather(gain_attn.astype(jnp.bfloat16), ("batch", "expert"), axis=0, tiled=True),
        lax.all_gather(gain_ffn.astype(jnp.bfloat16), ("batch", "expert"), axis=0, tiled=True),
    )
    full_qkv, full_out, full_sup, full_sdown, full_router, low_gain_a, low_gain_f = dense
    gain_first = low_gain_a.astype(jnp.float32)
    gain_second = low_gain_f.astype(jnp.float32)
    experts_up, experts_down = (
        lax.all_gather(expert_up.astype(jnp.bfloat16), "batch", axis=1, tiled=True),
        lax.all_gather(expert_down.astype(jnp.bfloat16), "batch", axis=1, tiled=True),
    )
    rows_in = block_input[0]
    ids_local = seq_ids[0]
    route_local = routes[0]
    upstream = cotangent[0]
    tokens_dev = rows_in.shape[0]
    model_width = rows_in.shape[1]
    heads_count = model_width // HEAD
    groups = lax.axis_size("expert")
    local_experts = experts_up.shape[0]
    experts_all = local_experts * groups
    shared_width = full_sdown.shape[0]
    hidden_width = experts_down.shape[1]
    capacity = max(2, tokens_dev * TOP * 3 // (experts_all * 2))
    score_scale = HEAD ** (-0.5)
    positions = lax.axis_index("expert") * tokens_dev + jnp.arange(tokens_dev, dtype=jnp.int32)
    key_ids = lax.all_gather(ids_local, "expert", axis=0, tiled=True)
    inv_first = lax.rsqrt(jnp.mean(rows_in * rows_in, axis=1, keepdims=True) + EPSILON)
    normed_first = rows_in * inv_first
    input_low = (normed_first * gain_first).astype(jnp.bfloat16)
    projected = jnp.dot(input_low, full_qkv, preferred_element_type=jnp.float32)
    queries = rotate(
        projected[:, :model_width].reshape(tokens_dev, heads_count, HEAD), positions, 1.0
    ).astype(jnp.bfloat16)
    keys = rotate(
        projected[:, model_width : 2 * model_width].reshape(tokens_dev, heads_count, HEAD),
        positions,
        1.0,
    ).astype(jnp.bfloat16)
    values = (
        projected[:, 2 * model_width :].reshape(tokens_dev, heads_count, HEAD).astype(jnp.bfloat16)
    )

    def key_mask(key_count):
        key_pos = jnp.arange(key_count, dtype=jnp.int32)
        return (key_pos[None, :] <= positions[:, None]) & (key_ids[None, :] == ids_local[:, None])

    run_max = jnp.full((heads_count, tokens_dev), NEGATIVE, jnp.float32)
    key_piece = lax.all_gather(keys, "expert", axis=0, tiled=True)
    value_piece = lax.all_gather(values, "expert", axis=0, tiled=True)
    allowed = key_mask(key_piece.shape[0])[None]
    scores = (
        jnp.einsum("qhd,khd->hqk", queries, key_piece, preferred_element_type=jnp.float32)
        * score_scale
    )
    scores = jnp.where(allowed, scores, NEGATIVE)
    new_max = jnp.maximum(run_max, jnp.max(scores, axis=2))
    weights = jnp.where(allowed, jnp.exp(scores - new_max[:, :, None]), 0.0)
    run_sum = jnp.sum(weights, axis=2)
    update = jnp.einsum(
        "hqk,khd->qhd",
        weights.astype(jnp.bfloat16),
        value_piece,
        preferred_element_type=jnp.float32,
    )
    run_acc = update
    run_max, run_sum, run_acc = (new_max, run_sum, run_acc)
    attn_full = run_acc / jnp.transpose(run_sum)[:, :, None]
    logsum = run_max + jnp.log(run_sum)
    attn_low = attn_full.reshape(tokens_dev, model_width).astype(jnp.bfloat16)
    resid = rows_in + jnp.dot(attn_low, full_out, preferred_element_type=jnp.float32)
    inv_second = lax.rsqrt(jnp.mean(resid * resid, axis=1, keepdims=True) + EPSILON)
    normed_second = resid * inv_second
    ffn_low = (normed_second * gain_second).astype(jnp.bfloat16)
    logits = jnp.dot(ffn_low, full_router, preferred_element_type=jnp.float32)
    probs = jax.nn.softmax(logits, axis=1)
    route_hot = route_local[:, :, None] == jnp.arange(experts_all, dtype=jnp.int32)[None, None, :]
    chosen = jnp.sum(jnp.where(route_hot, probs[:, None, :], 0.0), axis=2)
    chosen_sum = jnp.sum(chosen, axis=1, keepdims=True)
    gates = chosen / chosen_sum
    shared_pre = jnp.dot(ffn_low, full_sup, preferred_element_type=jnp.float32)
    shared_hidden = swiglu(shared_pre, shared_width).astype(jnp.bfloat16)
    shared_result = jnp.dot(shared_hidden, full_sdown, preferred_element_type=jnp.float32)
    flat_route = route_local.reshape(-1)
    flat_hot = (flat_route[:, None] == jnp.arange(experts_all, dtype=jnp.int32)[None, :]).astype(
        jnp.int32
    )
    slots = jnp.sum(jnp.cumsum(flat_hot, axis=0) * flat_hot, axis=1) - 1
    pair_count = tokens_dev * TOP
    source_table = (
        jnp.full((experts_all * capacity,), pair_count, jnp.int32)
        .at[flat_route * capacity + slots]
        .set(jnp.arange(pair_count, dtype=jnp.int32))
    )
    send_table = jnp.transpose(
        source_table.reshape(groups, local_experts, capacity), (1, 0, 2)
    ).reshape(-1)
    return_pos = (
        flat_route % local_experts * (groups * capacity)
        + flat_route // local_experts * capacity
        + slots
    )
    padded_rows = jnp.concatenate([ffn_low, jnp.zeros((1, model_width), jnp.bfloat16)], axis=0)
    send_rows = padded_rows[send_table // TOP].reshape(local_experts, groups, capacity, model_width)
    received = lax.all_to_all(send_rows, "expert", split_axis=1, concat_axis=1, tiled=True)
    expert_rows = received.reshape(local_experts, groups * capacity, model_width)
    expert_pre = jnp.einsum(
        "erd,edf->erf", expert_rows, experts_up, preferred_element_type=jnp.float32
    )
    expert_hidden = swiglu(expert_pre, hidden_width).astype(jnp.bfloat16)
    expert_result = jnp.einsum(
        "erf,efd->erd", expert_hidden, experts_down, preferred_element_type=jnp.float32
    ).astype(jnp.bfloat16)
    returned = lax.all_to_all(
        expert_result.reshape(local_experts, groups, capacity, model_width),
        "expert",
        split_axis=1,
        concat_axis=1,
        tiled=True,
    )
    token_outputs = returned.reshape(-1, model_width)[return_pos].reshape(
        tokens_dev, TOP, model_width
    )
    routed = jnp.sum(gates[:, :, None] * token_outputs, axis=1)
    output_rows = resid + shared_result + routed
    shared_cot = upstream.astype(jnp.bfloat16)
    shared_down_term = jnp.dot(shared_hidden.T, shared_cot, preferred_element_type=jnp.float32)
    dshared_hidden = jnp.dot(shared_cot, full_sdown.T, preferred_element_type=jnp.float32)
    dshared_pre = swiglu_back(shared_pre, dshared_hidden, shared_width).astype(jnp.bfloat16)
    shared_up_term = jnp.dot(ffn_low.T, dshared_pre, preferred_element_type=jnp.float32)
    dnormed_second = jnp.dot(dshared_pre, full_sup.T, preferred_element_type=jnp.float32)
    token_cot = (gates[:, :, None] * upstream[:, None, :]).astype(jnp.bfloat16)
    dgates = jnp.sum(upstream[:, None, :] * token_outputs, axis=2)
    padded_cot = jnp.concatenate(
        [token_cot.reshape(-1, model_width), jnp.zeros((1, model_width), jnp.bfloat16)], axis=0
    )
    send_cot = padded_cot[send_table].reshape(local_experts, groups, capacity, model_width)
    received_cot = lax.all_to_all(
        send_cot, "expert", split_axis=1, concat_axis=1, tiled=True
    ).reshape(local_experts, groups * capacity, model_width)
    down_term = jnp.einsum(
        "erf,erd->efd", expert_hidden, received_cot, preferred_element_type=jnp.float32
    )
    dexpert_hidden = jnp.einsum(
        "erd,efd->erf", received_cot, experts_down, preferred_element_type=jnp.float32
    )
    dexpert_pre = swiglu_back(expert_pre, dexpert_hidden, hidden_width).astype(jnp.bfloat16)
    up_term = jnp.einsum(
        "erd,erf->edf", expert_rows, dexpert_pre, preferred_element_type=jnp.float32
    )
    drows = jnp.einsum(
        "erf,edf->erd", dexpert_pre, experts_up, preferred_element_type=jnp.float32
    ).astype(jnp.bfloat16)
    returned_grad = lax.all_to_all(
        drows.reshape(local_experts, groups, capacity, model_width),
        "expert",
        split_axis=1,
        concat_axis=1,
        tiled=True,
    )
    row_grads = returned_grad.reshape(-1, model_width)[return_pos].reshape(
        tokens_dev, TOP, model_width
    )
    dnormed_second = dnormed_second + jnp.sum(row_grads, axis=1, dtype=jnp.float32)
    expert_up_grad, expert_down_grad = (
        lax.psum_scatter(
            up_term.astype(jnp.bfloat16), "batch", scatter_dimension=1, tiled=True
        ).astype(jnp.float32),
        lax.psum_scatter(
            down_term.astype(jnp.bfloat16), "batch", scatter_dimension=1, tiled=True
        ).astype(jnp.float32),
    )
    dchosen = (dgates - jnp.sum(dgates * gates, axis=1, keepdims=True)) / chosen_sum
    dprobs = jnp.sum(jnp.where(route_hot, dchosen[:, :, None], 0.0), axis=1)
    dlogits = (probs * (dprobs - jnp.sum(probs * dprobs, axis=1, keepdims=True))).astype(
        jnp.bfloat16
    )
    router_term = jnp.dot(ffn_low.T, dlogits, preferred_element_type=jnp.float32)
    dnormed_second = dnormed_second + jnp.dot(
        dlogits, full_router.T, preferred_element_type=jnp.float32
    )
    dresid_norm, gain_ffn_term = norm_back(dnormed_second, normed_second, inv_second, gain_second)
    dresid = upstream + dresid_norm
    dproj = dresid.astype(jnp.bfloat16)
    out_term = jnp.dot(attn_low.T, dproj, preferred_element_type=jnp.float32)
    dattn = (
        jnp.dot(dproj, full_out.T, preferred_element_type=jnp.float32)
        .astype(jnp.bfloat16)
        .reshape(tokens_dev, heads_count, HEAD)
    )
    delta_rows = jnp.sum(dattn.astype(jnp.float32) * attn_full, axis=2)
    delta_heads = jnp.transpose(delta_rows)
    key_piece = lax.all_gather(keys, "expert", axis=0, tiled=True)
    value_piece = lax.all_gather(values, "expert", axis=0, tiled=True)
    allowed = key_mask(key_piece.shape[0])[None]
    scores = (
        jnp.einsum("qhd,khd->hqk", queries, key_piece, preferred_element_type=jnp.float32)
        * score_scale
    )
    attn_probs = jnp.where(allowed, jnp.exp(scores - logsum[:, :, None]), 0.0)
    dprob = jnp.einsum("qhd,khd->hqk", dattn, value_piece, preferred_element_type=jnp.float32)
    dscore = (attn_probs * (dprob - delta_heads[:, :, None])).astype(jnp.bfloat16)
    attn_probs, dscore = (attn_probs, dscore)
    dquery = jnp.einsum("hqk,khd->qhd", dscore, key_piece, preferred_element_type=jnp.float32)
    dkey_piece = jnp.einsum("hqk,qhd->khd", dscore, queries, preferred_element_type=jnp.float32)
    dvalue_piece = jnp.einsum(
        "hqk,qhd->khd", attn_probs.astype(jnp.bfloat16), dattn, preferred_element_type=jnp.float32
    )
    folded = (dquery, dkey_piece, dvalue_piece)
    dquery = folded[0]
    dkey, dvalue = (
        lax.psum_scatter(
            folded[1].astype(jnp.bfloat16), "expert", scatter_dimension=0, tiled=True
        ).astype(jnp.float32),
        lax.psum_scatter(
            folded[2].astype(jnp.bfloat16), "expert", scatter_dimension=0, tiled=True
        ).astype(jnp.float32),
    )
    dquery_raw = rotate(dquery * score_scale, positions, -1.0).reshape(tokens_dev, model_width)
    dkey_raw = rotate(dkey * score_scale, positions, -1.0).reshape(tokens_dev, model_width)
    dprojected = jnp.concatenate(
        [dquery_raw, dkey_raw, dvalue.reshape(tokens_dev, model_width)], axis=1
    ).astype(jnp.bfloat16)
    qkv_term = jnp.dot(input_low.T, dprojected, preferred_element_type=jnp.float32)
    dnormed_first = jnp.dot(dprojected, full_qkv.T, preferred_element_type=jnp.float32)
    dinput_norm, gain_attn_term = norm_back(dnormed_first, normed_first, inv_first, gain_first)
    input_grad = dresid + dinput_norm
    grads = (
        lax.psum_scatter(qkv_term, ("batch", "expert"), scatter_dimension=0, tiled=True),
        lax.psum_scatter(out_term, ("batch", "expert"), scatter_dimension=0, tiled=True),
        lax.psum_scatter(shared_up_term, ("batch", "expert"), scatter_dimension=0, tiled=True),
        lax.psum_scatter(shared_down_term, ("batch", "expert"), scatter_dimension=0, tiled=True),
        lax.psum_scatter(router_term, ("batch", "expert"), scatter_dimension=0, tiled=True),
        lax.psum_scatter(gain_attn_term, ("batch", "expert"), scatter_dimension=0, tiled=True),
        lax.psum_scatter(gain_ffn_term, ("batch", "expert"), scatter_dimension=0, tiled=True),
    )
    (
        qkv_grad,
        out_grad,
        shared_up_grad,
        shared_down_grad,
        router_grad,
        gain_attn_grad,
        gain_ffn_grad,
    ) = grads
    return (
        output_rows[None],
        input_grad[None],
        qkv_grad,
        out_grad,
        shared_up_grad,
        shared_down_grad,
        router_grad,
        gain_attn_grad,
        gain_ffn_grad,
        expert_up_grad,
        expert_down_grad,
    )


def solution(mesh):
    in_specs = (
        P("batch", "expert", None),
        P("batch", "expert"),
        P("batch", "expert", None),
        P("batch", "expert", None),
        P(("batch", "expert"), None),
        P(("batch", "expert"), None),
        P(("batch", "expert"), None),
        P(("batch", "expert"), None),
        P(("batch", "expert"), None),
        P(("batch", "expert")),
        P(("batch", "expert")),
        P("expert", "batch", None),
        P("expert", "batch", None),
    )
    out_specs = (
        P("batch", "expert", None),
        P("batch", "expert", None),
        P(("batch", "expert"), None),
        P(("batch", "expert"), None),
        P(("batch", "expert"), None),
        P(("batch", "expert"), None),
        P(("batch", "expert"), None),
        P(("batch", "expert")),
        P(("batch", "expert")),
        P("expert", "batch", None),
        P("expert", "batch", None),
    )
    return jax.shard_map(
        per_device, mesh=mesh, in_specs=in_specs, out_specs=out_specs, check_vma=False
    )
```

profile of v0, /device:TPU:0, one launch (start us, length us, event | category | flops | bytes accessed | tf_op | source)
XLA Modules:
  0.0 1569.9 jit_solution(11628046243901504299)
XLA Ops:
  10.9 42.5 %all-reduce.10 = (bf16[1280]{0:T(1024)(128)(2,1)S(1)}, bf16[1280]{0:T(1024)(128)(2,1)S(1)}) all-reduce(bf16[1280]{0:T(1024)(128)(2,1)S(1)} %dynamic-update-slice, bf16[1280]{0:T(1024)(128)(2,1)S(1)} %dynamic-update-slice.1), channel_id=1, replica_groups=mesh['batch'=4,'expert'=8] {'batch','expert'}, use_global_device_ids=true, to_apply=%add.2 | all-reduce | flops 2560 | bytes 10240
  55.5 43.9 %all-gather.12.cloned.1.call-done = bf16[1280,3840]{1,0:T(8,128)(2,1)} async-done(((bf16[40,3840]{1,0:T(8,128)(2,1)}), bf16[1280,3840]{1,0:T(8,128)(2,1)}) %all-gather.12.cloned.1.call-update) | async-done | bytes 9830416 | tf_op jit(solution)/shard_map/all_gather | solution.py:62
  99.4 5.5 fusion.72
  131.5 10.4 all-gather
  142.8 8.3 all-gather.16.cloned.1.call-done
  158.0 29.2 %all-gather.14.cloned.1.call-done = bf16[1024,10,128]{0,2,1:T(8,128)(2,1)} async-done(((bf16[128,10,128]{0,2,1:T(8,128)(2,1)}), bf16[1024,10,128]{0,2,1:T(8,128)(2,1)}) %all-gather.14.cloned.1.call-update) | async-done | bytes 2621456 | tf_op jit(solution)/shard_map/all_gather | solution.py:115
  187.2 5.9 fusion.78
  193.1 55.3 %all-gather.18.cloned.1.call-done = bf16[1280,1280]{1,0:T(8,128)(2,1)} async-done(((bf16[40,1280]{1,0:T(8,128)(2,1)}), bf16[1280,1280]{1,0:T(8,128)(2,1)}) %all-gather.18.cloned.1.call-update) | async-done | bytes 3276816 | tf_op jit(solution)/shard_map/all_gather | solution.py:63
  252.1 5.2 gather_fusion
  270.2 5.0 mul.440
  275.2 88.2 %all-gather.2 = bf16[32,40,16]{1,2,0:T(8,128)(2,1)S(1)} all-gather(bf16[1,40,16]{1,2,0:T(8,128)(2,1)S(1)} %convert_bitcast_fusion.2), channel_id=1, replica_groups=mesh['batch'=4,'expert'=8] {'batch','expert'}, dimensions={0}, use_global_device_ids=true | all-gather | bytes 42240 | tf_op jit(solution)/shard_map/all_gather | solution.py:66
  367.8 5.1 gather_fusion.2
  384.3 68.1 %all-to-all-done.2 = bf16[2,8,72,1280]{3,2,0,1:T(8,128)(2,1)} async-done(((bf16[2,8,72,1280]{3,2,0,1:T(8,128)(2,1)}), bf16[2,8,72,1280]{3,2,0,1:T(8,128)(2,1)}, u32[]{:S(2)}, u32[]{:S(2)}) %all-to-all-start.2) | async-done | bytes 2949152 | tf_op jit(solution)/shard_map/all_to_all | solution.py:203
  456.0 11.3 fusion.86
  467.3 12.3 multiply_convert_fusion.2
  490.2 10.0 convolution_convert_fusion.3
  502.0 75.3 %all-to-all-done.1 = bf16[2,8,72,1280]{3,2,0,1:T(8,128)(2,1)S(1)} async-done(((bf16[2,8,72,1280]{3,2,0,1:T(8,128)(2,1)}), bf16[2,8,72,1280]{3,2,0,1:T(8,128)(2,1)S(1)}, u32[]{:S(2)}, u32[]{:S(2)}) %all-to-all-start.1) | async-done | bytes 2949152 | tf_op jit(solution)/shard_map/all_to_all | solution.py:179
  605.9 43.2 %all-to-all-done.3 = bf16[2,8,72,1280]{3,2,0,1:T(8,128)(2,1)} async-done(((bf16[2,8,72,1280]{3,2,0,1:T(8,128)(2,1)}), bf16[2,8,72,1280]{3,2,0,1:T(8,128)(2,1)}, u32[]{:S(2)}, u32[]{:S(2)}) %all-to-all-start.3) | async-done | bytes 2949152 | tf_op jit(solution)/shard_map/all_to_all | solution.py:219
  670.9 5.4 multiply_convert_fusion
  688.5 8.4 convolution_convert_fusion.1
  698.7 12.0 convolution_convert_fusion
  730.7 24.1 %reduce-scatter.25.cloned.1.call-done = bf16[128,1280]{1,0:T(8,128)(2,1)} async-done(((bf16[1024,1280]{1,0:T(8,128)(2,1)}), bf16[128,1280]{1,0:T(8,128)(2,1)}) %reduce-scatter.25.cloned.1.call-update) | async-done | bytes 327696
  756.0 8.2 fusion.31
  768.4 84.9 %fusion = f32[32,1280]{1,0:T(8,128)S(1)} fusion(f32[896,1280]{1,0:T(8,128)} %fusion.81), kind=kCustom, calls=%all-reduce-scatter | all-reduce-scatter fusion | flops 1310721 | bytes 4751360
  864.3 8.0 concatenate.43
  883.2 61.2 %reduce-scatter.23.cloned.1.call-done = bf16[2,224,1280]{2,1,0:T(8,128)(2,1)} async-done(((bf16[2,896,1280]{2,1,0:T(8,128)(2,1)}), bf16[2,224,1280]{2,1,0:T(8,128)(2,1)}) %reduce-scatter.23.cloned.1.call-update) | async-done | bytes 1146896 | tf_op jit(solution)/shard_map/reduce_scatter | solution.py:234
  947.2 7.4 multiply_reduce_fusion.3
  954.6 40.0 %all-reduce.9 = (f32[1280]{0:T(1024)S(1)}, f32[1280]{0:T(1024)S(1)}) all-reduce(f32[1280]{0:T(1024)S(1)} %get-tuple-element.15, f32[1280]{0:T(1024)S(1)} %get-tuple-element.13), channel_id=10, replica_groups=mesh['batch'=4,'expert'=8] {'batch','expert'}, use_global_device_ids=true, to_apply=%region_29.30.clone | all-reduce | flops 2560 | bytes 20480
  996.9 44.9 %reduce-scatter.21.cloned.1.call-done = bf16[2,320,1792]{2,1,0:T(8,128)(2,1)} async-done(((bf16[2,1280,1792]{2,1,0:T(8,128)(2,1)}), bf16[2,320,1792]{2,1,0:T(8,128)(2,1)}) %reduce-scatter.21.cloned.1.call-update) | async-done | bytes 2293776 | tf_op jit(solution)/shard_map/reduce_scatter | solution.py:231
  1045.9 152.3 %reduce-scatter.19.cloned.1.call-done = f32[40,1792]{1,0:T(8,128)} async-done(((f32[1280,1792]{1,0:T(8,128)}), f32[40,1792]{1,0:T(8,128)}) %reduce-scatter.19.cloned.1.call-update) | async-done | bytes 286736 | tf_op jit(solution)/shard_map/reduce_scatter | solution.py:296
  1198.3 149.1 %reduce-scatter.17.cloned.1.call-done = f32[40,1280]{1,0:T(8,128)} async-done(((f32[1280,1280]{1,0:T(8,128)}), f32[40,1280]{1,0:T(8,128)}) %reduce-scatter.17.cloned.1.call-update) | async-done | bytes 204816 | tf_op jit(solution)/shard_map/reduce_scatter | solution.py:295
  1347.4 215.5 %reduce-scatter.15.cloned.1.call-done = f32[40,3840]{1,0:T(8,128)} async-done(((f32[1280,3840]{1,0:T(8,128)}), f32[40,3840]{1,0:T(8,128)}) %reduce-scatter.15.cloned.1.call-update) | async-done | bytes 614416 | tf_op jit(solution)/shard_map/reduce_scatter | solution.py:294
  (306 shorter events, 208.1 us)
Async XLA Ops:
  7.2 92.2 %all-gather.12.cloned.1.call-start = ((), (), s32[]{:S(2)}) async-start(), calls=%async_computation.11 | async-start | bytes 10137600 | tf_op jit(solution)/shard_map/all_gather | solution.py:62
  9.1 142.0 %all-gather.16.cloned.1.call-start = ((), (), s32[]{:S(2)}) async-start(), calls=%async_computation.13 | async-start | bytes 2949120 | tf_op jit(solution)/shard_map/all_gather | solution.py:114
  53.3 46.1 %copy-start.39 = (f32[1280]{0:T(1024)}, f32[1280]{0:T(1024)S(1)}, u32[]{:S(2)}) copy-start(f32[1280]{0:T(1024)S(1)} %convert_element_type.155) | copy-start | bytes 15364
  54.6 44.8 %copy-start.47 = (f32[128]{0:T(128)}, f32[128]{0:T(128)S(1)}, u32[]{:S(2)}) copy-start(f32[128]{0:T(128)S(1)} %add_rsqrt_fusion.1) | copy-start | bytes 1540
  55.5 60.1 %copy-start.37 = (f32[128,64]{1,0:T(8,128)}, f32[128,64]{1,0:T(8,128)S(1)}, u32[]{:S(2)}) copy-start(f32[128,64]{1,0:T(8,128)S(1)} %get-tuple-element.53) | copy-start | bytes 98308
  118.5 68.7 %all-gather.14.cloned.1.call-start = ((), (), s32[]{:S(2)}) async-start(), calls=%async_computation.12 | async-start | bytes 2949120 | tf_op jit(solution)/shard_map/all_gather | solution.py:115
  119.5 128.9 %all-gather.18.cloned.1.call-start = ((), (), s32[]{:S(2)}) async-start(), calls=%async_computation.14 | async-start | bytes 3379200 | tf_op jit(solution)/shard_map/all_gather | solution.py:63
  121.2 334.9 %all-gather.22.cloned.1.call-start = ((), (), s32[]{:S(2)}) async-start(), calls=%async_computation.16 | async-start | bytes 11468800 | tf_op jit(solution)/shard_map/all_gather | solution.py:74
  187.2 61.2 %copy-start.3 = (f32[1,128,1280]{2,1,0:T(8,128)S(1)}, f32[1,128,1280]{2,1,0:T(8,128)}, u32[]{:S(2)}) copy-start(f32[1,128,1280]{2,1,0:T(8,128)} %param.13) | copy-start | bytes 1966084
  193.1 64.2 %copy-start.26 = (bf16[128,10,128]{0,2,1:T(8,128)(2,1)}, bf16[128,10,128]{0,2,1:T(8,128)(2,1)S(1)}, u32[]{:S(2)}) copy-start(bf16[128,10,128]{0,2,1:T(8,128)(2,1)S(1)} %get-tuple-element.56) | copy-start | bytes 983044
  261.4 115.1 %all-to-all-start = ((bf16[2,8,72,1280]{3,2,0,1:T(8,128)(2,1)}), bf16[2,8,72,1280]{3,2,0,1:T(8,128)(2,1)}, u32[]{:S(2)}, u32[]{:S(2)}) async-start(bf16[2,8,72,1280]{3,2,0,1:T(8,128)(2,1)} %copy.163), calls=%async_computation | async-start | bytes 5898240 | tf_op jit(solution)/shard_map/all_to_all | solution.py:170
  266.2 201.1 %all-gather.24.cloned.1.call-start = ((), (), s32[]{:S(2)}) async-start(), calls=%async_computation.17 | async-start | bytes 5734400 | tf_op jit(solution)/shard_map/all_gather | solution.py:75
  376.5 75.8 %all-to-all-start.2 = ((bf16[2,8,72,1280]{3,2,0,1:T(8,128)(2,1)}), bf16[2,8,72,1280]{3,2,0,1:T(8,128)(2,1)}, u32[]{:S(2)}, u32[]{:S(2)}) async-start(bf16[2,8,72,1280]{3,2,0,1:T(8,128)(2,1)} %copy.168), calls=%async_computation.2 | async-start | bytes 5898240 | tf_op jit(solution)/shard_map/all_to_all | solution.py:203
  381.1 201.0 %all-gather.26.cloned.1.call-start = ((), (), s32[]{:S(2)}) async-start(), calls=%async_computation.24 | async-start | bytes 2703360 | tf_op jit(solution)/shard_map/all_gather | solution.py:65
  384.2 83.1 %copy-start.1 = (bf16[2,8,72,1280]{3,2,1,0:T(8,128)(2,1)}, bf16[2,8,72,1280]{3,2,1,0:T(8,128)(2,1)S(1)}, u32[]{:S(2)}) copy-start(bf16[2,8,72,1280]{3,2,1,0:T(8,128)(2,1)S(1)} %copy.164) | copy-start | bytes 8847364
  484.8 92.5 %all-to-all-start.1 = ((bf16[2,8,72,1280]{3,2,0,1:T(8,128)(2,1)}), bf16[2,8,72,1280]{3,2,0,1:T(8,128)(2,1)S(1)}, u32[]{:S(2)}, u32[]{:S(2)}) async-start(bf16[2,8,72,1280]{3,2,0,1:T(8,128)(2,1)} %copy.165), calls=%async_computation.1 | async-start | bytes 5898240 | tf_op jit(solution)/shard_map/all_to_all | solution.py:179
  488.5 98.9 %all-gather.20.cloned.1.call-start = ((), (), s32[]{:S(2)}) async-start(), calls=%async_computation.15 | async-start | bytes 4730880 | tf_op jit(solution)/shard_map/all_gather | solution.py:64
  577.4 71.7 %all-to-all-start.3 = ((bf16[2,8,72,1280]{3,2,0,1:T(8,128)(2,1)}), bf16[2,8,72,1280]{3,2,0,1:T(8,128)(2,1)}, u32[]{:S(2)}, u32[]{:S(2)}) async-start(bf16[2,8,72,1280]{3,2,0,1:T(8,128)(2,1)} %copy.170), calls=%async_computation.3 | async-start | bytes 5898240 | tf_op jit(solution)/shard_map/all_to_all | solution.py:219
  581.8 145.1 %reduce-scatter.13.cloned.1.call-start = ((), (), s32[]{:S(2)}) async-start(), calls=%async_computation.18 | async-start | bytes 2949120 | tf_op jit(solution)/shard_map/reduce_scatter | solution.py:277
  680.5 74.3 %reduce-scatter.25.cloned.1.call-start = ((), (), s32[]{:S(2)}) async-start(), calls=%async_computation.25 | async-start | bytes 2949120
  687.4 194.4 %all-reduce.13.cloned.1.call-start = ((), (), s32[]{:S(2)}) async-start(), calls=%async_computation.26 | async-start | bytes 163840
  688.2 256.2 %reduce-scatter.23.cloned.1.call-start = ((), (), s32[]{:S(2)}) async-start(), calls=%async_computation.23 | async-start | bytes 5734400 | tf_op jit(solution)/shard_map/reduce_scatter | solution.py:234
  696.9 344.9 %reduce-scatter.21.cloned.1.call-start = ((), (), s32[]{:S(2)}) async-start(), calls=%async_computation.22 | async-start | bytes 11468800 | tf_op jit(solution)/shard_map/reduce_scatter | solution.py:231
  710.8 487.5 %reduce-scatter.19.cloned.1.call-start = ((), (), s32[]{:S(2)}) async-start(), calls=%async_computation.21 | async-start | bytes 9461760 | tf_op jit(solution)/shard_map/reduce_scatter | solution.py:296
  716.8 630.6 %reduce-scatter.17.cloned.1.call-start = ((), (), s32[]{:S(2)}) async-start(), calls=%async_computation.20 | async-start | bytes 6758400 | tf_op jit(solution)/shard_map/reduce_scatter | solution.py:295
  721.7 841.2 %reduce-scatter.15.cloned.1.call-start = ((), (), s32[]{:S(2)}) async-start(), calls=%async_computation.19 | async-start | bytes 20275200 | tf_op jit(solution)/shard_map/reduce_scatter | solution.py:294
  768.4 105.5 %copy-start.7 = (f32[128,1280]{1,0:T(8,128)S(1)}, f32[128,1280]{1,0:T(8,128)}, u32[]{:S(2)}) copy-start(f32[128,1280]{1,0:T(8,128)} %copy-done.5) | copy-start | bytes 1966084
  768.4 105.5 %copy-start.25 = (f32[128,1280]{1,0:T(8,128)S(1)}, f32[128,1280]{1,0:T(8,128)}, u32[]{:S(2)}) copy-start(f32[128,1280]{1,0:T(8,128)} %get-tuple-element.12) | copy-start | bytes 1966084
  853.3 11.0 collective-permute-start.2
  854.6 9.7 collective-permute-start.1
  856.5 7.7 collective-permute-start
  859.2 5.1 collective-permute-start.3
  (54 other events, 404.1 us)
Sparse Core Ops, SparseCore 0:
  11.6 87.7 all-gather.11
  118.6 32.4 all-gather.15
  153.2 33.9 all-gather.13
  190.5 57.8 all-gather.17
  250.7 93.3 all-gather.21
  345.8 56.0 all-gather.23
  405.3 72.1 all-gather.25
  492.8 85.7 all-gather.19
  680.7 35.5 reduce-scatter.12
  718.4 36.4 reduce-scatter.24
  760.4 121.3 all-reduce.12
  884.7 59.6 reduce-scatter.22
  947.6 94.1 reduce-scatter.20
  1044.5 153.6 reduce-scatter.18
  1201.0 146.3 reduce-scatter.16
  1354.2 208.6 reduce-scatter.14
where the time goes:
time: 1580 us; the launch traced here: 1570 us
  waiting for transfers between devices  979 us (62%)
  blocking collectives  266 us (17%)
  matrix products  132 us (8%)
  local copies, waits for them, and re-layouts  106 us (7%)
  other arithmetic  45.9 us (3%)
  starting transfers between devices  26.2 us (2%)
    reduce_scatter x1, waiting for transfers between devices, per_device(): lax.psum_scatter(qkv_term, ('batch', 'expert'), scatter_dimension=0, tile...  216 us
    unnamed x3, blocking collectives  167 us
    reduce_scatter x1, waiting for transfers between devices, per_device(): lax.psum_scatter(shared_up_term, ('batch', 'expert'), scatter_dimension=0...  152 us
    reduce_scatter x1, waiting for transfers between devices, per_device(): lax.psum_scatter(out_term, ('batch', 'expert'), scatter_dimension=0, tile...  149 us
    all_gather x1, blocking collectives, per_device(): lax.all_gather(router_weight.astype(jnp.bfloat16), ('batch', 'expert'), a...  88.2 us
    all_to_all x1, waiting for transfers between devices, per_device(): lax.all_to_all(expert_result.reshape(local_experts, groups, capacity, mod...  75.3 us
    all_to_all x1, waiting for transfers between devices, per_device(): lax.all_to_all(send_cot, 'expert', split_axis=1, concat_axis=1, tiled=True)  68.1 us
    reduce_scatter x1, waiting for transfers between devices, per_device(): lax.psum_scatter(down_term.astype(jnp.bfloat16), 'batch', scatter_dimensi...  61.2 us
  transfers between devices with their start and end apart: 24, of which 15 were waited for; matrix products, arithmetic and copies ran while one was open for 19% of the time, Pallas kernels for 0%

commit v1 on v0

--- a/solution.py
+++ b/solution.py
@@ -1,6 +1,10 @@
+import functools
+
 import jax
 import jax.numpy as jnp
 from jax import lax
+from jax.experimental import pallas as pl
+from jax.experimental.pallas import tpu as pltpu
 from jax.sharding import PartitionSpec as P
 
 HEAD = 128
@@ -148,10 +152,13 @@
     shared_result = jnp.dot(shared_hidden, full_sdown, preferred_element_type=jnp.float32)
     flat_route = route_local.reshape(-1)
     flat_hot = (flat_route[:, None] == jnp.arange(experts_all, dtype=jnp.int32)[None, :]).astype(
-        jnp.int32
-    )
-    slots = jnp.sum(jnp.cumsum(flat_hot, axis=0) * flat_hot, axis=1) - 1
+        jnp.bfloat16
+    )
     pair_count = tokens_dev * TOP
+    pair_index = jnp.arange(pair_count, dtype=jnp.int32)
+    earlier = (pair_index[None, :] < pair_index[:, None]).astype(jnp.bfloat16)
+    counts = jnp.dot(earlier, flat_hot, preferred_element_type=jnp.float32)
+    slots = jnp.sum(counts * flat_hot, axis=1).astype(jnp.int32)
     source_table = (
         jnp.full((experts_all * capacity,), pair_count, jnp.int32)
         .at[flat_route * capacity + slots]
@@ -323,6 +330,309 @@
     )
 
 
+PAIR_OF = {0: 0, 2: 1, 3: 2, 4: 3, 6: 4}
+AXES = ("batch", "expert")
+F32 = jnp.float32
+LOW = jnp.bfloat16
+
+
+def low(values):
+    return values.astype(LOW)
+
+
+def dot(left, right, dims=((1,), (0,))):
+    return lax.dot_general(left, right, (dims, ((), ())), preferred_element_type=F32)
+
+
+def swap(values, batch_bit, expert_bit=0, only=range(8)):
+    pairs = [
+        (b * 8 + e, (b ^ batch_bit) * 8 + (e ^ expert_bit)) for b in range(4) for e in range(8)
+    ]
+    pairs = [pair for pair in pairs if pair[0] % 8 in only]
+    return lax.ppermute(values, AXES, pairs)
+
+
+def halves(values, axis):
+    size = values.shape[axis] // 2
+    return (
+        lax.slice_in_dim(values, 0, size, axis=axis),
+        lax.slice_in_dim(values, size, 2 * size, axis=axis),
+    )
+
+
+def gather_batch(piece, axis, cut):
+    b = lax.axis_index("batch")
+    from_x = swap(piece, 1)
+    from_y = swap(piece, 2)
+    far_a = swap(halves(from_x, cut)[0], 2)
+    far_b = swap(halves(from_y, cut)[1], 1)
+    far = jnp.concatenate([far_a, far_b], axis=cut)
+    rows = piece.shape[axis]
+    shape = list(piece.shape)
+    shape[axis] = 4 * rows
+    whole = jnp.zeros(shape, piece.dtype)
+    for bit, part in enumerate((piece, from_x, from_y, far)):
+        whole = lax.dynamic_update_slice_in_dim(whole, part, (b ^ bit) * rows, axis)
+    return whole
+
+
+def scatter_batch(whole, axis, cut):
+    b = lax.axis_index("batch")
+    rows = whole.shape[axis] // 4
+
+    def block(bit):
+        return lax.dynamic_slice_in_dim(whole, (b ^ bit) * rows, rows, axis)
+
+    own_a, own_b = halves(block(0), cut)
+    x_a, x_b = halves(block(1), cut)
+    y_a, y_b = halves(block(2), cut)
+    far_a, far_b = halves(block(3), cut)
+    got_own_a = swap(low(x_a), 1).astype(F32)
+    got_y_a = swap(low(far_a), 1).astype(F32)
+    got_own_b = swap(low(y_b), 2).astype(F32)
+    got_x_b = swap(low(far_b), 2).astype(F32)
+    last_a = swap(low(y_a.astype(F32) + got_y_a), 2).astype(F32)
+    last_b = swap(low(x_b.astype(F32) + got_x_b), 1).astype(F32)
+    return jnp.concatenate(
+        [own_a.astype(F32) + got_own_a + last_a, own_b.astype(F32) + got_own_b + last_b], axis=cut
+    )
+
+
+def gather_tokens(values):
+    return lax.all_gather(values, "expert", axis=0, tiled=True)
+
+
+def scatter_tokens(values):
+    return lax.psum_scatter(values, "expert", scatter_dimension=0, tiled=True).astype(F32)
+
+
+def exchange(values):
+    return lax.all_to_all(values, "expert", split_axis=0, concat_axis=0, tiled=True)
+
+
+def silu_parts(gate, up):
+    sigma = jax.nn.sigmoid(gate)
+    return gate * sigma, up * sigma * (1.0 + gate * (1.0 - sigma))
+
+
+def pack_device(
+    block_input,
+    seq_ids,
+    routes,
+    cotangent,
+    qkv_weight,
+    out_weight,
+    shared_up,
+    shared_down,
+    router_weight,
+    gain_attn,
+    gain_ffn,
+    expert_up,
+    expert_down,
+):
+    b = lax.axis_index("batch")
+    e = lax.axis_index("expert")
+    rows_in = block_input[0]
+    upstream = cotangent[0]
+    tokens, width = rows_in.shape
+    length = tokens * 8
+    rows_w = qkv_weight.shape[0]
+    pair = 2 * HEAD
+    pairs_of_heads = width // pair
+    hidden = expert_up.shape[2] // 2
+    experts = expert_up.shape[0] * 8
+    s_rows = shared_down.shape[0]
+    s_own = 4 * s_rows
+    s_pad = -(-s_own // 128) * 128
+    scale = HEAD ** (-0.5)
+
+    qkv_low = low(qkv_weight).reshape(rows_w, 3, pairs_of_heads, pair)
+    nothing = jnp.zeros((rows_w, 3, pair), LOW)
+    columns = [qkv_low[:, :, PAIR_OF[i]] if i in PAIR_OF else nothing for i in range(8)]
+    columns = jnp.stack(columns).reshape(8, rows_w, 3 * pair)
+    sup_low = low(shared_up).reshape(rows_w, 2, 4, 8, s_rows).transpose(3, 0, 1, 2, 4)
+    sup_low = jnp.pad(
+        sup_low.reshape(8, rows_w, 2, s_own), ((0, 0), (0, 0), (0, 0), (0, s_pad - s_own))
+    )
+    columns = jnp.concatenate([columns, sup_low.reshape(8, rows_w, 2 * s_pad)], axis=2)
+    columns = exchange(columns).reshape(8 * rows_w, 3 * pair + 2 * s_pad)
+    columns = gather_batch(columns, 0, 0)
+    w_qkv = columns[:, : 3 * pair]
+    w_sup = columns[:, 3 * pair :]
+    up_low = gather_batch(low(expert_up), 1, 1)
+    down_low = gather_batch(low(expert_down), 1, 1)
+    w_sdown = gather_batch(low(shared_down), 0, 1)
+    w_sdown = jnp.pad(w_sdown, ((0, s_pad - s_own), (0, 0)))
+    core = lax.rem(e, 2)
+    out_z = gather_tokens(low(out_weight))
+    half_rows = 4 * rows_w
+    out_mine = lax.dynamic_slice_in_dim(out_z, core * half_rows, half_rows, 0)
+    out_mine = gather_batch(out_mine, 0, 1).reshape(4, 1, half_rows, width)
+    out_other = swap(out_mine, 0, 1)
+    w_out = jnp.zeros((4, 2, half_rows, width), LOW)
+    w_out = lax.dynamic_update_slice_in_dim(w_out, out_mine, core, 1)
+    w_out = lax.dynamic_update_slice_in_dim(w_out, out_other, 1 - core, 1).reshape(width, width)
+
+    small = jnp.concatenate([router_weight, gain_attn[:, None], gain_ffn[:, None]], axis=1)
+    small = lax.all_gather(low(small), AXES, axis=0, tiled=True)
+    w_router = small[:, :experts]
+    gain_first = small[:, experts].astype(F32)
+    gain_second = small[:, experts + 1].astype(F32)
+    marks = gather_tokens(jnp.concatenate([routes[0], seq_ids[0][:, None]], axis=1))
+    route_all = marks[:, :TOP]
+    ids_all = marks[:, TOP]
+    cot_all = gather_tokens(low(upstream))
+
+    inv_first = lax.rsqrt(jnp.mean(rows_in * rows_in, axis=1, keepdims=True) + EPSILON)
+    xhat_first = rows_in * inv_first
+    n1_all = gather_tokens(low(xhat_first * gain_first))
+    positions = jnp.arange(length, dtype=jnp.int32)
+    projected = dot(n1_all, w_qkv)
+    queries = low(rotate(projected[:, :pair].reshape(length, 2, HEAD), positions, 1.0))
+    keys = low(rotate(projected[:, pair : 2 * pair].reshape(length, 2, HEAD), positions, 1.0))
+    values = low(projected[:, 2 * pair :].reshape(length, 2, HEAD))
+    allowed = (positions[None, :] <= positions[:, None]) & (ids_all[None, :] == ids_all[:, None])
+    scores = jnp.einsum("qhd,khd->hqk", queries, keys, preferred_element_type=F32) * scale
+    scores = jnp.where(allowed[None], scores, NEGATIVE)
+    top = jnp.max(scores, axis=2, keepdims=True)
+    attn_p = jnp.exp(scores - top)
+    total = jnp.sum(attn_p, axis=2, keepdims=True)
+    attn_p = attn_p / total
+    attn_low = low(attn_p)
+    attended = jnp.einsum("hqk,khd->qhd", attn_low, values, preferred_element_type=F32)
+    attended_low = low(attended)
+    arrived = exchange(attended_low.reshape(8, tokens, pair))
+    attn = jnp.concatenate([arrived[i] for i in PAIR_OF], axis=1)
+    resid = rows_in + dot(attn, w_out)
+
+    inv_second = lax.rsqrt(jnp.mean(resid * resid, axis=1, keepdims=True) + EPSILON)
+    xhat_second = resid * inv_second
+    n2 = low(xhat_second * gain_second)
+    n2_all = gather_tokens(n2)
+    logits = dot(n2_all, w_router)
+    hot = route_all[:, :, None] == jnp.arange(experts, dtype=jnp.int32)[None, None, :]
+    routed_to = jnp.any(hot, axis=1)
+    logits = jnp.where(routed_to, logits, NEGATIVE)
+    gates = jnp.where(routed_to, jnp.exp(logits - jnp.max(logits, axis=1, keepdims=True)), 0.0)
+    gates = gates / jnp.sum(gates, axis=1, keepdims=True)
+    mine = lax.dynamic_slice_in_dim(gates, 2 * e, 2, 1)
+
+    output_part = 0.0
+    drow_part = 0.0
+    dgates = []
+    up_terms = []
+    down_terms = []
+    for k in range(2):
+        gate = mine[:, k : k + 1]
+        pre = dot(n2_all, up_low[k])
+        silu, slope = silu_parts(pre[:, :hidden], pre[:, hidden:])
+        hid = silu * pre[:, hidden:]
+        back = dot(cot_all, down_low[k], ((1,), (1,)))
+        dgates.append(jnp.sum(back * hid, axis=1, keepdims=True))
+        hid_low = low(hid * gate)
+        output_part = output_part + dot(hid_low, down_low[k])
+        down_terms.append(dot(hid_low, cot_all, ((0,), (0,))))
+        back = back * gate
+        dpre = low(jnp.concatenate([back * slope, back * silu], axis=1))
+        up_terms.append(dot(n2_all, dpre, ((0,), (0,))))
+        drow_part = drow_part + dot(dpre, up_low[k], ((1,), (1,)))
+    pre = dot(n2_all, w_sup)
+    silu, slope = silu_parts(pre[:, :s_pad], pre[:, s_pad:])
+    hid_low = low(silu * pre[:, s_pad:])
+    back = dot(cot_all, w_sdown, ((1,), (1,)))
+    output_part = output_part + dot(hid_low, w_sdown)
+    sdown_term = dot(hid_low, cot_all, ((0,), (0,)))[:s_own]
+    dpre = low(jnp.concatenate([back * slope, back * silu], axis=1))
+    sup_term = dot(n2_all, dpre, ((0,), (0,)))
+    drow_part = drow_part + dot(dpre, w_sup, ((1,), (1,)))
+    output_rows = resid + scatter_tokens(low(output_part))
+    expert_up_grad = scatter_batch(low(jnp.stack(up_terms)), 1, 1)
+    expert_down_grad = scatter_batch(low(jnp.stack(down_terms)), 1, 1)
+    shared_down_grad = scatter_batch(low(sdown_term), 0, 1)
+
+    lane = jnp.arange(experts, dtype=jnp.int32)[None, :] - 2 * e
+    dgate = jnp.where(lane == 0, dgates[0], 0.0) + jnp.where(lane == 1, dgates[1], 0.0)
+    dgate_high = low(dgate)
+    dgate_rest = low(dgate - dgate_high.astype(F32))
+    spare = jnp.zeros((length, 128 - 2 * experts), LOW)
+    dn2 = scatter_tokens(
+        jnp.concatenate([low(drow_part), dgate_high, dgate_rest, spare], axis=1)
+    )
+    dgate = dn2[:, width : width + experts] + dn2[:, width + experts : width + 2 * experts]
+    own_gates = lax.dynamic_slice_in_dim(gates, e * tokens, tokens, 0)
+    dlogits = low(own_gates * (dgate - jnp.sum(own_gates * dgate, axis=1, keepdims=True)))
+    router_term = dot(dlogits, n2, ((0,), (0,)))
+    dn2 = dn2[:, :width] + dot(dlogits, w_router, ((1,), (1,)))
+    dresid, gain_ffn_term = norm_back(dn2, xhat_second, inv_second, gain_second)
+    dresid = upstream + dresid
+    dproj = low(dresid)
+    dattn = low(dot(dproj, w_out, ((1,), (1,))))
+    dattn = jnp.stack(
+        [
+            dattn[:, PAIR_OF[i] * pair : (PAIR_OF[i] + 1) * pair]
+            if i in PAIR_OF
+            else jnp.zeros((tokens, pair), LOW)
+            for i in range(8)
+        ]
+    )
+    dattn = exchange(dattn).reshape(length, 2, HEAD)
+    out_term = dot(attn, dproj, ((0,), (0,))).reshape(4, 2, half_rows, width)
+    out_away = swap(low(lax.dynamic_slice_in_dim(out_term, 1 - core, 1, 1)), 0, 1)
+    out_term = lax.dynamic_slice_in_dim(out_term, core, 1, 1) + out_away
+    out_term = scatter_batch(low(out_term).reshape(4 * half_rows, width), 0, 1)
+    out_pad = lax.dynamic_update_slice_in_dim(
+        jnp.zeros((2 * half_rows, width), LOW), low(out_term), core * half_rows, 0
+    )
+    out_grad = scatter_tokens(out_pad)
+
+    delta = jnp.sum(dattn.astype(F32) * attended, axis=2).T[:, :, None]
+    dprob = jnp.einsum("qhd,khd->hqk", dattn, values, preferred_element_type=F32)
+    dscore = low(attn_p * (dprob - delta))
+    dquery = jnp.einsum("hqk,khd->qhd", dscore, keys, preferred_element_type=F32)
+    dkey = jnp.einsum("hqk,qhd->khd", dscore, queries, preferred_element_type=F32)
+    dvalue = jnp.einsum("hqk,qhd->khd", attn_low, dattn, preferred_element_type=F32)
+    dprojected = low(
+        jnp.concatenate(
+            [
+                rotate(dquery * scale, positions, -1.0).reshape(length, pair),
+                rotate(dkey * scale, positions, -1.0).reshape(length, pair),
+                dvalue.reshape(length, pair),
+            ],
+            axis=1,
+        )
+    )
+    qkv_term = dot(n1_all, dprojected, ((0,), (0,)))
+    dn1 = scatter_tokens(low(dot(dprojected, w_qkv, ((1,), (1,)))))
+    dinput, gain_attn_term = norm_back(dn1, xhat_first, inv_first, gain_first)
+    input_grad = dresid + dinput
+
+    columns = scatter_batch(low(jnp.concatenate([qkv_term, sup_term], axis=1)), 0, 0)
+    columns = exchange(low(columns).reshape(8, rows_w, 3 * pair + 2 * s_pad)).astype(F32)
+    qkv_grad = jnp.stack([columns[i, :, : 3 * pair] for i in PAIR_OF])
+    qkv_grad = qkv_grad.reshape(pairs_of_heads, rows_w, 3, pair).transpose(1, 2, 0, 3)
+    qkv_grad = qkv_grad.reshape(rows_w, 3 * width)
+    sup_grad = columns[:, :, 3 * pair :].reshape(8, rows_w, 2, s_pad)[..., :s_own]
+    sup_grad = sup_grad.reshape(8, rows_w, 2, 4, s_rows).transpose(1, 2, 3, 0, 4)
+    sup_grad = sup_grad.reshape(rows_w, shared_up.shape[1])
+
+    small = jnp.concatenate([router_term, gain_attn_term[None], gain_ffn_term[None]], axis=0)
+    small = lax.psum(small, AXES)
+    small = lax.dynamic_slice_in_dim(small, (b * 8 + e) * rows_w, rows_w, 1)
+    return (
+        output_rows[None],
+        input_grad[None],
+        qkv_grad,
+        out_grad,
+        sup_grad,
+        shared_down_grad,
+        small[:experts].T,
+        small[experts],
+        small[experts + 1],
+        expert_up_grad,
+        expert_down_grad,
+    )
+
+
 def solution(mesh):
     in_specs = (
         P("batch", "expert", None),
@@ -352,6 +662,8 @@
         P("expert", "batch", None),
         P("expert", "batch", None),
     )
+    sizes = dict(mesh.shape)
+    body = pack_device if sizes == {"batch": 4, "expert": 8} else per_device
     return jax.shard_map(
-        per_device, mesh=mesh, in_specs=in_specs, out_specs=out_specs, check_vma=False
-    )
+        body, mesh=mesh, in_specs=in_specs, out_specs=out_specs, check_vma=False
+    )

time: 1580 us -> 872 us (0.55)
  waiting for transfers between devices: 979 us -> 359 us
  blocking collectives: 266 us -> 101 us
  starting transfers between devices: 26.2 us -> 66.6 us
  other arithmetic: 45.9 us -> 73.6 us
    reduce_scatter x6 -> x1, waiting for transfers between devices: 623 us -> 0.01 us  [scatter_tokens(): lax.psum_scatter(values, 'expert', scatter_dimension=0, tiled=True)]
    ppermute x0 -> x52, waiting for transfers between devices: none -> 212 us  [swap(): return lax.ppermute(values, AXES, pairs)]
    unnamed x3 -> x0, blocking collectives: 167 us -> none
    all_to_all x4, waiting for transfers between devices: 187 us -> 29.3 us  [exchange(): lax.all_to_all(values, 'expert', split_axis=0, concat_axis=0, tiled=True)]
    all_gather x8 -> x3, waiting for transfers between devices: 137 us -> 0.02 us  [gather_tokens(): return lax.all_gather(values, 'expert', axis=0, tiled=True)]
    psum x0 -> x1, waiting for transfers between devices: none -> 118 us  [pack_device(): small = lax.psum(small, AXES)]
    ppermute x0 -> x52, starting transfers between devices: none -> 49.5 us  [swap(): return lax.ppermute(values, AXES, pairs)]
    unnamed x22 -> x11, waiting for transfers between devices: 32.4 us -> 0.15 us
  transfers between devices with their start and end apart: 24 -> 64, of which waited for: 15 -> 25; matrix products, arithmetic and copies ran while one was open for 19% -> 29% of each run, Pallas kernels for 0% -> 0%
where the time goes in v1:
time: 872 us; the launch traced here: 864 us
  waiting for transfers between devices  359 us (41%)
  matrix products  137 us (16%)
  local copies, waits for them, and re-layouts  111 us (13%)
  blocking collectives  101 us (12%)
  other arithmetic  73.6 us (8%)
  starting transfers between devices  66.6 us (8%)
  between operations  16.2 us (2%)
    ppermute x52, waiting for transfers between devices, swap(): return lax.ppermute(values, AXES, pairs)  212 us
    psum x1, waiting for transfers between devices, pack_device(): small = lax.psum(small, AXES)  118 us
    dot_general x27, matrix products, dot(): lax.dot_general(left, right, (dims, ((), ())), preferred_element_type=F32)  111 us
    all_gather x2, blocking collectives, gather_tokens(): return lax.all_gather(values, 'expert', axis=0, tiled=True)  56.9 us
    ppermute x52, starting transfers between devices, swap(): return lax.ppermute(values, AXES, pairs)  49.5 us
    all_gather x1, blocking collectives, pack_device(): small = lax.all_gather(low(small), AXES, axis=0, tiled=True)  44 us
    unnamed x209, local copies, waits for them, and re-layouts  33 us
    all_to_all x4, waiting for transfers between devices, exchange(): lax.all_to_all(values, 'expert', split_axis=0, concat_axis=0, tiled=True)  29.3 us
  transfers between devices with their start and end apart: 64, of which 25 were waited for; matrix products, arithmetic and copies ran while one was open for 29% of the time, Pallas kernels for 0%

profile of v1, /device:TPU:0, one launch (start us, length us, event | category | flops | bytes accessed | tf_op | source)
XLA Modules:
  0.0 863.7 jit_solution(18409974913013417230)
XLA Ops:
  10.0 44.0 %all-gather = bf16[32,40,18]{1,2,0:T(8,128)(2,1)S(1)} all-gather(bf16[1,40,18]{1,2,0:T(8,128)(2,1)S(1)} %maximum_bitcast_fusion), channel_id=1, replica_groups=mesh['batch'=4,'expert'=8] {'batch','expert'}, dimensions={0}, use_global_device_ids=true | all-gather | bytes 47520 | tf_op jit(solution)/shard_map/all_gather | solution.py:477
  65.3 42.4 %all_gather.21 = bf16[320,1280]{1,0:T(8,128)(2,1)S(1)} all-gather(bf16[40,1280]{1,0:T(8,128)(2,1)S(1)} %convert_element_type.373), channel_id=1, replica_groups=mesh['batch'=4,'expert'=8] {'expert'}, dimensions={0}, use_global_device_ids=true | all-gather | bytes 921600 | tf_op jit(solution)/shard_map/all_gather | solution.py:402
  114.2 14.5 %all_gather.20 = s32[1024,7]{0,1:T(8,128)S(1)} all-gather(s32[128,7]{0,1:T(8,128)S(1)} %pad_add_fusion), channel_id=1, replica_groups=mesh['batch'=4,'expert'=8] {'expert'}, dimensions={0}, use_global_device_ids=true | all-gather | bytes 32256 | tf_op jit(solution)/shard_map/all_gather | solution.py:402
  140.8 12.4 %collective-permute-done.1 = bf16[320,1024]{1,0:T(8,128)(2,1)S(1)} collective-permute-done((bf16[320,1024]{1,0:T(8,128)(2,1)S(1)}, bf16[320,1024]{1,0:T(8,128)(2,1)S(1)}, u32[]{:S(2)}, u32[]{:S(2)}) %collective-permute-start.1) | collective-permute-done | bytes 655392 | tf_op jit(solution)/shard_map/ppermute | solution.py:352
  156.0 6.0 collective-permute-done.3
  162.4 5.0 fusion.28
  179.2 8.8 %fusion.99 = (f32[2,1024]{1,0:T(2,128)S(1)}, f32[2,1024,1024]{1,2,0:T(8,128)}) fusion(pred[1024,1024]{0,1:T(8,128)(4,1)} %fusion.6, bf16[1024,2,64]{2,0,1:T(8,128)(2,1)S(1)} %get-tuple-element.99, bf16[1024,2,64]{2,0,1:T(8,128)(2,1)} %get-tuple-element.100, bf16[1024,2,64]{2,0,1:T(8,128)(2,1)} %get-tuple-element.67, bf16[1024,2,64]{2,0,1:T(8,128)(2,1)} %get-tuple-element.66), kind=kOutput, calls=%fused_computation.308 | convolution fusion | flops 547357696 | bytes 10493952 | tf_op jit(solution)/shard_map/sub | solution.py:498
  204.8 12.0 %all-to-all-done.1 = bf16[8,128,256]{2,1,0:T(8,128)(2,1)} async-done(((bf16[8,128,256]{2,1,0:T(8,128)(2,1)}), bf16[8,128,256]{2,1,0:T(8,128)(2,1)}, u32[]{:S(2)}, u32[]{:S(2)}) %all-to-all-start.1) | async-done | bytes 524320 | tf_op jit(solution)/shard_map/all_to_all | solution.py:410
  229.7 5.0 constant_dynamic-update-slice_fusion.16
  245.7 66.8 %collective-permute-done.18 = bf16[28,1280]{1,0:T(8,128)(2,1)S(1)} collective-permute-done((bf16[28,1280]{1,0:T(8,128)(2,1)S(1)}, bf16[28,1280]{1,0:T(8,128)(2,1)S(1)}, u32[]{:S(2)}, u32[]{:S(2)}) %collective-permute-start.18) | collective-permute-done | bytes 71712 | tf_op jit(solution)/shard_map/ppermute | solution.py:352
  350.3 11.0 %collective-permute-done.12 = bf16[2,160,1792]{2,1,0:T(8,128)(2,1)S(1)} collective-permute-done((bf16[2,160,1792]{2,1,0:T(8,128)(2,1)S(1)}, bf16[2,160,1792]{2,1,0:T(8,128)(2,1)S(1)}, u32[]{:S(2)}, u32[]{:S(2)}) %collective-permute-start.12) | collective-permute-done | bytes 1146912 | tf_op jit(solution)/shard_map/ppermute | solution.py:352
  367.5 9.4 %fusion.9 = f32[1024,1792]{1,0:T(8,128)} fusion(bf16[1024,1280]{0,1:T(8,128)(2,1)S(1)} %copy-done.24, bf16[2,1280,1792]{2,1,0:T(8,128)(2,1)} %maximum_dynamic-update-slice_fusion), kind=kOutput, calls=%fused_computation.41 | convolution fusion | flops 4697620480 | bytes 14548992 | tf_op jit(solution)/shard_map/dot_general | solution.py:344
  376.9 10.2 %multiply_convert_fusion.4 = (bf16[1024,896]{1,0:T(8,128)(2,1)}, bf16[1024,896]{1,0:T(8,128)(2,1)}, f32[1024]{0:T(1024)S(1)}, bf16[1024,896]{1,0:T(8,128)(2,1)S(1)}) fusion(f32[1024,1792]{1,0:T(8,128)} %fusion.9, f32[1024]{0:T(1024)S(1)} %bitcast.236, bf16[1024,1280]{0,1:T(8,128)(2,1)} %all-gather.9.cloned.1.call-done, ...), kind=kOutput, calls=%fused_computation.56 | convolution fusion | flops 2366241792 | bytes 17768448 | tf_op jit(solution)/shard_map/dot_general | solution.py:344
  393.0 7.6 fusion.11
  400.6 8.6 multiply_convert_fusion.2
  409.2 5.2 fusion.26
  430.5 7.4 fusion.8
  437.9 7.3 fusion.10
  448.1 5.4 concatenate.102
  455.3 7.3 fusion.1
  462.7 5.2 fusion.2
  495.6 11.0 %collective-permute-done.39 = bf16[28,640]{1,0:T(8,128)(2,1)S(1)} collective-permute-done((bf16[28,640]{1,0:T(8,128)(2,1)S(1)}, bf16[28,640]{1,0:T(8,128)(2,1)S(1)}, u32[]{:S(2)}, u32[]{:S(2)}) %collective-permute-start.39) | collective-permute-done | bytes 35872 | tf_op jit(solution)/shard_map/ppermute | solution.py:352
  538.5 7.4 all-to-all-done.2
  554.3 4.8 multiply_convert_fusion
  567.0 10.5 %collective-permute-done.33 = bf16[160,640]{1,0:T(8,128)(2,1)S(1)} collective-permute-done((bf16[160,640]{1,0:T(8,128)(2,1)S(1)}, bf16[160,640]{1,0:T(8,128)(2,1)S(1)}, u32[]{:S(2)}, u32[]{:S(2)}) %collective-permute-start.33) | collective-permute-done | bytes 204832 | tf_op jit(solution)/shard_map/ppermute | solution.py:352
  607.9 7.3 collective-permute-done.22
  622.8 8.3 collective-permute-done.48
  633.4 9.7 %collective-permute-done.21 = bf16[160,1024]{0,1:T(8,128)(2,1)S(1)} collective-permute-done((bf16[160,1024]{0,1:T(8,128)(2,1)S(1)}, bf16[160,1024]{0,1:T(8,128)(2,1)S(1)}, u32[]{:S(2)}, u32[]{:S(2)}) %collective-permute-start.21) | collective-permute-done | bytes 327712 | tf_op jit(solution)/shard_map/ppermute | solution.py:352
  645.1 8.5 collective-permute-done.23
  657.2 42.1 %collective-permute-done.26 = bf16[160,1024]{0,1:T(8,128)(2,1)S(1)} collective-permute-done((bf16[160,1024]{0,1:T(8,128)(2,1)S(1)}, bf16[160,1024]{0,1:T(8,128)(2,1)S(1)}, u32[]{:S(2)}, u32[]{:S(2)}) %collective-permute-start.26) | collective-permute-done | bytes 327712 | tf_op jit(solution)/shard_map/ppermute | solution.py:352
  713.4 9.9 %all-to-all-done.3 = bf16[8,40,1024]{2,1,0:T(8,128)(2,1)S(1)} async-done(((bf16[8,40,1024]{2,1,0:T(8,128)(2,1)}), bf16[8,40,1024]{2,1,0:T(8,128)(2,1)S(1)}, u32[]{:S(2)}, u32[]{:S(2)}) %all-to-all-start.3) | async-done | bytes 655392 | tf_op jit(solution)/shard_map/all_to_all | solution.py:410
  736.1 117.9 %all-reduce.4.cloned.1.call-done = f32[18,1280]{1,0:T(8,128)} async-done(((f32[18,1280]{1,0:T(8,128)}), f32[18,1280]{1,0:T(8,128)}) %all-reduce.4.cloned.1.call-update) | async-done | bytes 92176 | tf_op jit(solution)/shard_map/psum | solution.py:619
  (511 shorter events, 308.7 us)
Async XLA Ops:
  7.2 155.2 %all-gather.5.cloned.1.call-start = ((), (), s32[]{:S(2)}) async-start(), calls=%async_computation.8 | async-start | bytes 2949120 | tf_op jit(solution)/shard_map/all_gather | solution.py:402
  61.6 71.6 %all-to-all-start = ((bf16[8,40,1024]{2,1,0:T(8,128)(2,1)}), bf16[8,40,1024]{2,1,0:T(8,128)(2,1)S(1)}, u32[]{:S(2)}, u32[]{:S(2)}) async-start(bf16[8,40,1024]{2,1,0:T(8,128)(2,1)} %pad_maximum_fusion.10), calls=%async_computation | async-start | bytes 1310720 | tf_op jit(solution)/shard_map/all_to_all | solution.py:410
  140.8 62.4 %collective-permute-start.8 = (bf16[4,1,160,1280]{3,2,1,0:T(8,128)(2,1)}, bf16[4,1,160,1280]{3,2,1,0:T(8,128)(2,1)}, u32[]{:S(2)}, u32[]{:S(2)}) collective-permute-start(bf16[4,1,160,1280]{3,2,1,0:T(8,128)(2,1)} %bitcast.17), channel_id=1, source_target_pairs={{0,1},{1,0},{2,3},{3,2},{4,5},{5,4},{6,7},{7,6},{8,9},{9,8},{10,11... | collective-permute-start | bytes 4915208 | tf_op jit(solution)/shard_map/ppermute | solution.py:352
  201.3 163.6 %all-gather.7.cloned.1.call-start = ((), (), s32[]{:S(2)}) async-start(), calls=%async_computation.9 | async-start | bytes 2949120 | tf_op jit(solution)/shard_map/all_gather | solution.py:402
  225.4 151.5 %all-gather.9.cloned.1.call-start = ((), (), s32[]{:S(2)}) async-start(), calls=%async_computation.10 | async-start | bytes 2949120 | tf_op jit(solution)/shard_map/all_gather | solution.py:402
  234.6 94.9 %collective-permute-start.10 = (bf16[2,320,1792]{2,1,0:T(8,128)(2,1)}, bf16[2,320,1792]{2,1,0:T(8,128)(2,1)S(1)}, u32[]{:S(2)}, u32[]{:S(2)}) collective-permute-start(bf16[2,320,1792]{2,1,0:T(8,128)(2,1)} %get-tuple-element.47), channel_id=1, source_target_pairs={{0,16},{1,17},{2,18},{3,19},{4,20},{5,21},{6,22},{7,23},{8,24},{9,... | collective-permute-start | bytes 6881288 | tf_op jit(solution)/shard_map/ppermute | solution.py:352
  235.3 95.7 %collective-permute-start.9 = (bf16[2,320,1792]{2,1,0:T(8,128)(2,1)}, bf16[2,320,1792]{2,1,0:T(8,128)(2,1)}, u32[]{:S(2)}, u32[]{:S(2)}) collective-permute-start(bf16[2,320,1792]{2,1,0:T(8,128)(2,1)} %get-tuple-element.47), channel_id=1, source_target_pairs={{0,8},{1,9},{2,10},{3,11},{4,12},{5,13},{6,14},{7,15},{8,0},{9,1},... | collective-permute-start | bytes 6881288 | tf_op jit(solution)/shard_map/ppermute | solution.py:352
  240.8 83.7 %collective-permute-start.13 = (bf16[2,224,1280]{2,1,0:T(8,128)(2,1)}, bf16[2,224,1280]{2,1,0:T(8,128)(2,1)}, u32[]{:S(2)}, u32[]{:S(2)}) collective-permute-start(bf16[2,224,1280]{2,1,0:T(8,128)(2,1)} %get-tuple-element.45), channel_id=1, source_target_pairs={{0,8},{1,9},{2,10},{3,11},{4,12},{5,13},{6,14},{7,15},{8,0},{9,1},... | collective-permute-start | bytes 3440648 | tf_op jit(solution)/shard_map/ppermute | solution.py:352
  241.4 77.2 %collective-permute-start.14 = (bf16[2,224,1280]{2,1,0:T(8,128)(2,1)}, bf16[2,224,1280]{2,1,0:T(8,128)(2,1)}, u32[]{:S(2)}, u32[]{:S(2)}) collective-permute-start(bf16[2,224,1280]{2,1,0:T(8,128)(2,1)} %get-tuple-element.45), channel_id=1, source_target_pairs={{0,16},{1,17},{2,18},{3,19},{4,20},{5,21},{6,22},{7,23},{8,24},{9,... | collective-permute-start | bytes 3440648 | tf_op jit(solution)/shard_map/ppermute | solution.py:352
  244.9 264.2 %reduce-scatter.13.cloned.1.call-start = ((), (), s32[]{:S(2)}) async-start(), calls=%async_computation.13 | async-start | bytes 2949120
  245.0 67.5 %collective-permute-start.18 = (bf16[28,1280]{1,0:T(8,128)(2,1)S(1)}, bf16[28,1280]{1,0:T(8,128)(2,1)S(1)}, u32[]{:S(2)}, u32[]{:S(2)}) collective-permute-start(bf16[28,1280]{1,0:T(8,128)(2,1)S(1)} %convert_element_type.382), channel_id=1, source_target_pairs={{0,16},{1,17},{2,18},{3,19},{4,20},{5,21},{6,22},{7,23},{8,24},{9,... | collective-permute-start | bytes 215048 | tf_op jit(solution)/shard_map/ppermute | solution.py:352
  329.6 31.7 %collective-permute-start.12 = (bf16[2,160,1792]{2,1,0:T(8,128)(2,1)S(1)}, bf16[2,160,1792]{2,1,0:T(8,128)(2,1)S(1)}, u32[]{:S(2)}, u32[]{:S(2)}) collective-permute-start(bf16[2,160,1792]{2,1,0:T(8,128)(2,1)S(1)} %slice.466), channel_id=1, source_target_pairs={{0,8},{1,9},{2,10},{3,11},{4,12},{5,13},{6,14},{7,15},{8,0},{9,1},... | collective-permute-start | bytes 3440648 | tf_op jit(solution)/shard_map/ppermute | solution.py:352
  332.3 31.0 %collective-permute-start.11 = (bf16[2,160,1792]{2,1,0:T(8,128)(2,1)S(1)}, bf16[2,160,1792]{2,1,0:T(8,128)(2,1)S(1)}, u32[]{:S(2)}, u32[]{:S(2)}) collective-permute-start(bf16[2,160,1792]{2,1,0:T(8,128)(2,1)S(1)} %slice.465), channel_id=1, source_target_pairs={{0,16},{1,17},{2,18},{3,19},{4,20},{5,21},{6,22},{7,23},{8,24},{9,... | collective-permute-start | bytes 3440648 | tf_op jit(solution)/shard_map/ppermute | solution.py:352
  420.6 89.8 %reduce-scatter.15.cloned.1.call-start = ((), (), s32[]{:S(2)}) async-start(), calls=%async_computation.14 | async-start | bytes 3244032
  426.4 54.6 %collective-permute-start.35 = (bf16[28,640]{1,0:T(8,128)(2,1)}, bf16[28,640]{1,0:T(8,128)(2,1)}, u32[]{:S(2)}, u32[]{:S(2)}) collective-permute-start(bf16[28,640]{1,0:T(8,128)(2,1)} %get-tuple-element.116), channel_id=1, source_target_pairs={{0,8},{1,9},{2,10},{3,11},{4,12},{5,13},{6,14},{7,15},{8,0},{9,1},... | collective-permute-start | bytes 107528 | tf_op jit(solution)/shard_map/ppermute | solution.py:352
  427.9 56.4 %collective-permute-start.34 = (bf16[28,640]{1,0:T(8,128)(2,1)}, bf16[28,640]{1,0:T(8,128)(2,1)}, u32[]{:S(2)}, u32[]{:S(2)}) collective-permute-start(bf16[28,640]{1,0:T(8,128)(2,1)} %get-tuple-element.115), channel_id=1, source_target_pairs={{0,8},{1,9},{2,10},{3,11},{4,12},{5,13},{6,14},{7,15},{8,0},{9,1},... | collective-permute-start | bytes 107528 | tf_op jit(solution)/shard_map/ppermute | solution.py:352
  428.4 56.6 %collective-permute-start.38 = (bf16[28,640]{1,0:T(8,128)(2,1)}, bf16[28,640]{1,0:T(8,128)(2,1)}, u32[]{:S(2)}, u32[]{:S(2)}) collective-permute-start(bf16[28,640]{1,0:T(8,128)(2,1)} %get-tuple-element.118), channel_id=1, source_target_pairs={{0,16},{1,17},{2,18},{3,19},{4,20},{5,21},{6,22},{7,23},{8,24},{9,... | collective-permute-start | bytes 107528 | tf_op jit(solution)/shard_map/ppermute | solution.py:352
  429.8 65.0 %collective-permute-start.37 = (bf16[28,640]{1,0:T(8,128)(2,1)}, bf16[28,640]{1,0:T(8,128)(2,1)}, u32[]{:S(2)}, u32[]{:S(2)}) collective-permute-start(bf16[28,640]{1,0:T(8,128)(2,1)} %get-tuple-element.117), channel_id=1, source_target_pairs={{0,16},{1,17},{2,18},{3,19},{4,20},{5,21},{6,22},{7,23},{8,24},{9,... | collective-permute-start | bytes 107528 | tf_op jit(solution)/shard_map/ppermute | solution.py:352
  471.2 132.6 %collective-permute-start.41 = (bf16[2,160,1792]{2,1,0:T(8,128)(2,1)}, bf16[2,160,1792]{2,1,0:T(8,128)(2,1)}, u32[]{:S(2)}, u32[]{:S(2)}) collective-permute-start(bf16[2,160,1792]{2,1,0:T(8,128)(2,1)} %get-tuple-element.78), channel_id=1, source_target_pairs={{0,8},{1,9},{2,10},{3,11},{4,12},{5,13},{6,14},{7,15},{8,0},{9,1},... | collective-permute-start | bytes 3440648 | tf_op jit(solution)/shard_map/ppermute | solution.py:352
  484.3 133.7 %collective-permute-start.44 = (bf16[2,160,1792]{2,1,0:T(8,128)(2,1)}, bf16[2,160,1792]{2,1,0:T(8,128)(2,1)}, u32[]{:S(2)}, u32[]{:S(2)}) collective-permute-start(bf16[2,160,1792]{2,1,0:T(8,128)(2,1)} %get-tuple-element.79), channel_id=1, source_target_pairs={{0,16},{1,17},{2,18},{3,19},{4,20},{5,21},{6,22},{7,23},{8,24},{9,... | collective-permute-start | bytes 3440648 | tf_op jit(solution)/shard_map/ppermute | solution.py:352
  494.8 41.7 %collective-permute-start.50 = (bf16[2,112,1280]{2,1,0:T(8,128)(2,1)}, bf16[2,112,1280]{2,1,0:T(8,128)(2,1)}, u32[]{:S(2)}, u32[]{:S(2)}) collective-permute-start(bf16[2,112,1280]{2,1,0:T(8,128)(2,1)} %get-tuple-element.95), channel_id=1, source_target_pairs={{0,16},{1,17},{2,18},{3,19},{4,20},{5,21},{6,22},{7,23},{8,24},{9,... | collective-permute-start | bytes 1720328 | tf_op jit(solution)/shard_map/ppermute | solution.py:352
  530.5 200.2 %reduce-scatter.11.cloned.1.call-start = ((), (), s32[]{:S(2)}) async-start(), calls=%async_computation.11 | async-start | bytes 921600 | tf_op jit(solution)/shard_map/reduce_scatter | solution.py:406
  559.1 56.8 %collective-permute-start.46 = (bf16[2,112,1280]{2,1,0:T(8,128)(2,1)}, bf16[2,112,1280]{2,1,0:T(8,128)(2,1)}, u32[]{:S(2)}, u32[]{:S(2)}) collective-permute-start(bf16[2,112,1280]{2,1,0:T(8,128)(2,1)} %slice.519), channel_id=1, source_target_pairs={{0,8},{1,9},{2,10},{3,11},{4,12},{5,13},{6,14},{7,15},{8,0},{9,1},... | collective-permute-start | bytes 1720328 | tf_op jit(solution)/shard_map/ppermute | solution.py:352
  566.5 50.6 %collective-permute-start.49 = (bf16[2,112,1280]{2,1,0:T(8,128)(2,1)}, bf16[2,112,1280]{2,1,0:T(8,128)(2,1)}, u32[]{:S(2)}, u32[]{:S(2)}) collective-permute-start(bf16[2,112,1280]{2,1,0:T(8,128)(2,1)} %slice.523), channel_id=1, source_target_pairs={{0,16},{1,17},{2,18},{3,19},{4,20},{5,21},{6,22},{7,23},{8,24},{9,... | collective-permute-start | bytes 1720328 | tf_op jit(solution)/shard_map/ppermute | solution.py:352
  580.2 152.1 %reduce-scatter.17.cloned.1.call-start = ((), (), s32[]{:S(2)}) async-start(), calls=%async_computation.15 | async-start | bytes 2949120
  619.5 34.1 %collective-permute-start.23 = (bf16[160,1024]{0,1:T(8,128)(2,1)S(1)}, bf16[160,1024]{0,1:T(8,128)(2,1)S(1)}, u32[]{:S(2)}, u32[]{:S(2)}) collective-permute-start(bf16[160,1024]{0,1:T(8,128)(2,1)S(1)} %add_convert_fusion.10), channel_id=1, source_target_pairs={{0,16},{1,17},{2,18},{3,19},{4,20},{5,21},{6,22},{7,23},{8,24},{9,... | collective-permute-start | bytes 983048 | tf_op jit(solution)/shard_map/ppermute | solution.py:352
  631.1 74.1 %collective-permute-start.40 = (bf16[2,160,1792]{2,1,0:T(8,128)(2,1)}, bf16[2,160,1792]{2,1,0:T(8,128)(2,1)}, u32[]{:S(2)}, u32[]{:S(2)}) collective-permute-start(bf16[2,160,1792]{2,1,0:T(8,128)(2,1)} %slice.511), channel_id=1, source_target_pairs={{0,8},{1,9},{2,10},{3,11},{4,12},{5,13},{6,14},{7,15},{8,0},{9,1},... | collective-permute-start | bytes 3440648 | tf_op jit(solution)/shard_map/ppermute | solution.py:352
  631.9 73.3 %collective-permute-start.43 = (bf16[2,160,1792]{2,1,0:T(8,128)(2,1)S(1)}, bf16[2,160,1792]{2,1,0:T(8,128)(2,1)}, u32[]{:S(2)}, u32[]{:S(2)}) collective-permute-start(bf16[2,160,1792]{2,1,0:T(8,128)(2,1)S(1)} %copy-done.44), channel_id=1, source_target_pairs={{0,16},{1,17},{2,18},{3,19},{4,20},{5,21},{6,22},{7,23},{8,24},{9,... | collective-permute-start | bytes 3440648 | tf_op jit(solution)/shard_map/ppermute | solution.py:352
  643.1 62.1 %collective-permute-start.42 = (bf16[2,160,1792]{2,1,0:T(8,128)(2,1)}, bf16[2,160,1792]{2,1,0:T(8,128)(2,1)}, u32[]{:S(2)}, u32[]{:S(2)}) collective-permute-start(bf16[2,160,1792]{2,1,0:T(8,128)(2,1)} %add_convert_fusion.4), channel_id=1, source_target_pairs={{0,16},{1,17},{2,18},{3,19},{4,20},{5,21},{6,22},{7,23},{8,24},{9,... | collective-permute-start | bytes 3440648 | tf_op jit(solution)/shard_map/ppermute | solution.py:352
  644.6 60.6 %collective-permute-start.45 = (bf16[2,160,1792]{2,1,0:T(8,128)(2,1)}, bf16[2,160,1792]{2,1,0:T(8,128)(2,1)}, u32[]{:S(2)}, u32[]{:S(2)}) collective-permute-start(bf16[2,160,1792]{2,1,0:T(8,128)(2,1)} %add_convert_fusion.3), channel_id=1, source_target_pairs={{0,8},{1,9},{2,10},{3,11},{4,12},{5,13},{6,14},{7,15},{8,0},{9,1},... | collective-permute-start | bytes 3440648 | tf_op jit(solution)/shard_map/ppermute | solution.py:352
  653.6 45.7 %collective-permute-start.26 = (bf16[160,1024]{0,1:T(8,128)(2,1)S(1)}, bf16[160,1024]{0,1:T(8,128)(2,1)S(1)}, u32[]{:S(2)}, u32[]{:S(2)}) collective-permute-start(bf16[160,1024]{0,1:T(8,128)(2,1)S(1)} %add_convert_fusion.8), channel_id=1, source_target_pairs={{0,8},{1,9},{2,10},{3,11},{4,12},{5,13},{6,14},{7,15},{8,0},{9,1},... | collective-permute-start | bytes 983048 | tf_op jit(solution)/shard_map/ppermute | solution.py:352
  705.1 148.8 %all-reduce.4.cloned.1.call-start = ((), (), s32[]{:S(2)}) async-start(), calls=%async_computation.12 | async-start | bytes 245760 | tf_op jit(solution)/shard_map/psum | solution.py:619
  (119 other events, 1857.4 us)
Sparse Core Ops, SparseCore 0:
  55.7 47.8 all-gather.4
  225.5 32.8 all-gather.6
  260.0 33.3 all-gather.8
  420.7 36.5 reduce-scatter.12
  460.1 37.8 reduce-scatter.14
  580.4 29.6 reduce-scatter.10
  612.5 35.7 reduce-scatter.16
  734.9 119.0 all-reduce.3

commit v2 on v1

--- a/solution.py
+++ b/solution.py
@@ -330,7 +330,7 @@
     )
 
 
-PAIR_OF = {0: 0, 2: 1, 3: 2, 4: 3, 6: 4}
+PAIR_OF = {0: 0, 2: 1, 4: 2, 6: 3, 3: 4}
 AXES = ("batch", "expert")
 F32 = jnp.float32
 LOW = jnp.bfloat16
@@ -360,10 +360,13 @@
     )
 
 
-def gather_batch(piece, axis, cut):
+def gather_near(piece):
+    return piece, swap(piece, 1), swap(piece, 2)
+
+
+def gather_far(near, axis, cut):
     b = lax.axis_index("batch")
-    from_x = swap(piece, 1)
-    from_y = swap(piece, 2)
+    piece, from_x, from_y = near
     far_a = swap(halves(from_x, cut)[0], 2)
     far_b = swap(halves(from_y, cut)[1], 1)
     far = jnp.concatenate([far_a, far_b], axis=cut)
@@ -374,6 +377,10 @@
     for bit, part in enumerate((piece, from_x, from_y, far)):
         whole = lax.dynamic_update_slice_in_dim(whole, part, (b ^ bit) * rows, axis)
     return whole
+
+
+def after(values, *earlier):
+    return lax.optimization_barrier((values, *earlier))[0]
 
 
 def scatter_batch(whole, axis, cut):
@@ -398,12 +405,619 @@
     )
 
 
-def gather_tokens(values):
-    return lax.all_gather(values, "expert", axis=0, tiled=True)
-
-
-def scatter_tokens(values):
-    return lax.psum_scatter(values, "expert", scatter_dimension=0, tiled=True).astype(F32)
+def z_shift(values, steps):
+    pairs = [
+        (b * 8 + e, b * 8 + (e + 2 * steps) % 8) for b in range(4) for e in range(8)
+    ]
+    return lax.ppermute(values, AXES, pairs)
+
+
+def gather_z(block):
+    z = lax.axis_index("expert") // 2
+    whole = jnp.zeros((4, *block.shape), block.dtype)
+    whole = lax.dynamic_update_index_in_dim(whole, block, z, 0)
+    for steps in (1, 2, 3):
+        part = z_shift(block, steps)
+        whole = lax.dynamic_update_index_in_dim(whole, part, lax.rem(z + 4 - steps, 4), 0)
+    return whole
+
+
+def gather_pack(block):
+    core = lax.rem(lax.axis_index("expert"), 2)
+    mine = gather_z(block)
+    other = swap(mine, 0, 1)
+    first = jnp.where(core == 0, mine, other)
+    second = jnp.where(core == 0, other, mine)
+    return jnp.stack([first, second], axis=1).reshape(8, *block.shape)
+
+
+def scatter_z(blocks):
+    z = lax.axis_index("expert") // 2
+    total = lax.dynamic_index_in_dim(blocks, z, 0, False).astype(F32)
+    for steps in (1, 2, 3):
+        block = lax.dynamic_index_in_dim(blocks, lax.rem(z + steps, 4), 0, False)
+        total = total + z_shift(low(block), steps).astype(F32)
+    return total
+
+
+def scatter_pack(blocks):
+    core = lax.rem(lax.axis_index("expert"), 2)
+    pairs = blocks.reshape(4, 2, *blocks.shape[1:])
+    away = lax.dynamic_index_in_dim(pairs, 1 - core, 1, False)
+    mine = lax.dynamic_index_in_dim(pairs, core, 1, False)
+    return scatter_z(mine.astype(F32) + swap(low(away), 0, 1).astype(F32))
+
+
+def total_all(values):
+    for batch_bit, expert_bit in ((0, 1), (1, 0), (2, 0), (0, 2), (0, 4)):
+        values = values + swap(values, batch_bit, expert_bit)
+    return values
+
+
+MESH_ID = pl.DeviceIdType.MESH
+
+
+def place():
+    b = lax.axis_index("batch")
+    e = lax.axis_index("expert")
+    return b, e, e // 2, lax.rem(e, 2)
+
+
+def greet(devices):
+    barrier = pltpu.get_barrier_semaphore()
+    for device in devices:
+        pl.semaphore_signal(barrier, inc=1, device_id=device, device_id_type=MESH_ID)
+    pl.semaphore_wait(barrier, len(devices))
+
+
+def greet_line():
+    b, e, z, core = place()
+    barrier = pltpu.get_barrier_semaphore()
+    pl.semaphore_signal(barrier, inc=1, device_id=(b, e ^ 1), device_id_type=MESH_ID)
+
+    @pl.when(z > 0)
+    def _():
+        pl.semaphore_signal(barrier, inc=1, device_id=(b, e - 2), device_id_type=MESH_ID)
+
+    @pl.when(z < 3)
+    def _():
+        pl.semaphore_signal(barrier, inc=1, device_id=(b, e + 2), device_id_type=MESH_ID)
+
+    ends = jnp.where((z == 0) | (z == 3), 1, 0)
+    pl.semaphore_wait(barrier, 3 - ends)
+
+
+def pack_mates():
+    b, e, _, _ = place()
+    return [(b, lax.rem(e + i, 8)) for i in range(1, 8)]
+
+
+def send(src, dst, send_sem, recv_sem, device):
+    return pltpu.make_async_remote_copy(
+        src_ref=src,
+        dst_ref=dst,
+        send_sem=send_sem,
+        recv_sem=recv_sem,
+        device_id=device,
+        device_id_type=MESH_ID,
+    )
+
+
+GATHER_SEMS = [pltpu.SemaphoreType.DMA((3,))] * 4 + [pltpu.SemaphoreType.DMA((4,))] * 2
+
+
+def line_stages(buf, up_send, up_recv, down_send, down_recv, core_send, core_recv):
+    b, e, z, core = place()
+
+    def to_core(owner_z):
+        block = buf.at[2 * owner_z + core]
+        return send(block, block, core_send.at[owner_z], core_recv.at[owner_z], (b, e ^ 1))
+
+    def up(step):
+        block = buf.at[jnp.maximum(2 * (z - step), 0) + core]
+        return send(block, block, up_send.at[step], up_recv.at[step], (b, jnp.minimum(e + 2, 7)))
+
+    def down(step):
+        block = buf.at[jnp.minimum(2 * (z + step), 6) + core]
+        return send(
+            block, block, down_send.at[step], down_recv.at[step], (b, jnp.maximum(e - 2, 0))
+        )
+
+    def start(step):
+        @pl.when((z >= step) & (z < 3))
+        def _():
+            up(step).start()
+
+        @pl.when((z + step <= 3) & (z > 0))
+        def _():
+            down(step).start()
+
+        if step == 0:
+            to_core(z).start()
+
+    def arrive(step):
+        @pl.when(z - 1 - step >= 0)
+        def _():
+            up(step).wait_recv()
+
+        @pl.when(z + 1 + step <= 3)
+        def _():
+            down(step).wait_recv()
+
+        if step < 2:
+            start(step + 1)
+
+        @pl.when(z - 1 - step >= 0)
+        def _():
+            to_core(z - 1 - step).start()
+
+        @pl.when(z + 1 + step <= 3)
+        def _():
+            to_core(z + 1 + step).start()
+
+    def finish():
+        for owner_z in range(4):
+            to_core(owner_z).wait()
+        for step in range(3):
+
+            @pl.when((z >= step) & (z < 3))
+            def _():
+                up(step).wait_send()
+
+            @pl.when((z + step <= 3) & (z > 0))
+            def _():
+                down(step).wait_send()
+
+    return [lambda: start(0)] + [functools.partial(arrive, i) for i in range(3)] + [finish]
+
+
+def line_gather(buf, *sems):
+    for stage in line_stages(buf, *sems):
+        stage()
+
+
+def scatter_scratch(tokens, width):
+    return [pltpu.VMEM((4, tokens, width), LOW)] + [
+        pltpu.VMEM((3, tokens, width), LOW) for _ in range(4)
+    ]
+
+
+SCATTER_SEMS = [pltpu.SemaphoreType.DMA((3,))] * 4 + [pltpu.SemaphoreType.DMA((4,))] * 2
+
+
+def line_scatter(
+    part,
+    from_core,
+    up_out,
+    up_in,
+    down_out,
+    down_in,
+    up_send,
+    up_recv,
+    down_send,
+    down_recv,
+    core_send,
+    core_recv,
+):
+    b, e, z, core = place()
+
+    def to_core(target):
+        return send(
+            part.at[2 * target + 1 - core],
+            from_core.at[target],
+            core_send.at[target],
+            core_recv.at[target],
+            (b, e ^ 1),
+        )
+
+    def up(step):
+        return send(
+            up_out.at[step],
+            up_in.at[step],
+            up_send.at[step],
+            up_recv.at[step],
+            (b, jnp.minimum(e + 2, 7)),
+        )
+
+    def down(step):
+        return send(
+            down_out.at[step],
+            down_in.at[step],
+            down_send.at[step],
+            down_recv.at[step],
+            (b, jnp.maximum(e - 2, 0)),
+        )
+
+    def chip_sum(target):
+        return part[2 * target + core].astype(F32) + from_core[target].astype(F32)
+
+    for target in (3, 0, 2, 1):
+        to_core(target).start()
+    for target in range(4):
+        to_core(target).wait()
+    for step in range(3):
+        top = 3 - step
+
+        @pl.when(z < top)
+        def _():
+            @pl.when(z > 0)
+            def _():
+                up(step).wait_recv()
+                up_out[step] = low(chip_sum(top) + up_in[step].astype(F32))
+
+            @pl.when(z == 0)
+            def _():
+                up_out[step] = low(chip_sum(top))
+
+            up(step).start()
+
+        @pl.when(z > step)
+        def _():
+            @pl.when(z < 3)
+            def _():
+                down(step).wait_recv()
+                down_out[step] = low(chip_sum(step) + down_in[step].astype(F32))
+
+            @pl.when(z == 3)
+            def _():
+                down_out[step] = low(chip_sum(step))
+
+            down(step).start()
+
+    @pl.when(z == 0)
+    def _():
+        up_in[0] = jnp.zeros_like(up_in[0])
+
+    @pl.when(z == 3)
+    def _():
+        down_in[0] = jnp.zeros_like(down_in[0])
+
+    last_up = lax.rem(3 - z, 3)
+    last_down = lax.rem(z, 3)
+
+    @pl.when(z > 0)
+    def _():
+        up(last_up).wait_recv()
+
+    @pl.when(z < 3)
+    def _():
+        down(last_down).wait_recv()
+
+    total = chip_sum(z) + up_in[last_up].astype(F32) + down_in[last_down].astype(F32)
+    for step in range(3):
+
+        @pl.when(z < 3 - step)
+        def _():
+            up(step).wait_send()
+
+        @pl.when(z > step)
+        def _():
+            down(step).wait_send()
+
+    return total
+
+
+def kernel_call(body, outs, args, scratch, collective_id):
+    vmem = pl.BlockSpec(memory_space=pltpu.VMEM)
+    return pl.pallas_call(
+        body,
+        out_shape=[jax.ShapeDtypeStruct(shape, dtype) for shape, dtype in outs],
+        in_specs=[vmem] * len(args),
+        out_specs=[vmem] * len(outs),
+        scratch_shapes=scratch,
+        compiler_params=pltpu.CompilerParams(
+            collective_id=collective_id, has_side_effects=True, vmem_limit_bytes=48 * 2**20
+        ),
+    )(*args)
+
+
+def opening_kernel(
+    rows, small, marks, columns, w_out, n1_all, gains, small_all, marks_all, columns_all, out_all,
+    *sems,
+):
+    (
+        b_send, b_recv, s_send, s_recv, m_send, m_recv, c_send, c_recv,
+        x_send, x_recv, y_send, y_recv, z_send, z_recv, o_send, o_recv, p_send, p_recv,
+    ) = sems[:18]
+    b, e, z, core = place()
+    over = [(b ^ bit, e) for bit in (1, 2, 3)]
+    mates = pack_mates()
+    greet(over + mates)
+    small_all[e, b] = small[...]
+    marks_all[e] = marks[...]
+    columns_all[b, e] = columns[e]
+    out_all[core, b, z] = w_out[...]
+    first = []
+    for i, device in enumerate(over):
+        first.append(send(small, small_all.at[e, b], b_send.at[i], b_recv.at[i], device))
+        first[-1].start()
+    across = []
+    for i, device in enumerate(mates):
+        across.append(
+            send(columns.at[device[1]], columns_all.at[b, e], c_send.at[i], c_recv.at[i], device)
+        )
+        across[-1].start()
+    along = []
+    for i in range(3):
+        device = (b, lax.rem(e + 2 * i + 2, 8))
+        along.append(
+            send(w_out, out_all.at[core, b, z], z_send.at[i], z_recv.at[i], device)
+        )
+        along[-1].start()
+    rest = []
+    for i, device in enumerate(mates):
+        rest.append(send(marks, marks_all.at[e], m_send.at[i], m_recv.at[i], device))
+        rest[-1].start()
+    values = rows[...]
+    inv = lax.rsqrt(jnp.mean(values * values, axis=1, keepdims=True) + EPSILON)
+    for copy in first:
+        copy.wait()
+    second = []
+    for i, device in enumerate(mates):
+        second.append(send(small_all.at[e], small_all.at[e], s_send.at[i], s_recv.at[i], device))
+        second[-1].start()
+    for copy in second:
+        copy.wait()
+
+    width = rows.shape[1]
+    piece = width // 32
+    lane = lax.broadcasted_iota(jnp.int32, (128, width), 1)
+    spread = low(jnp.where(lax.rem(lane, piece) == lax.broadcasted_iota(jnp.int32, (128, width), 0), 1.0, 0.0))
+    row = lax.broadcasted_iota(jnp.int32, (32, width), 0)
+    owner = lax.rem(row, 4) * 8 + row // 4
+    mine = lax.broadcasted_iota(jnp.int32, (32, width), 1) // piece == owner
+    for i, index in enumerate((5, 6)):
+        pieces = jnp.concatenate([small_all[j, :, index, :] for j in range(8)], axis=0)
+        spread_out = dot(low(pieces), spread)
+        gains[i : i + 1, :] = jnp.sum(jnp.where(mine, spread_out, 0.0), axis=0, keepdims=True)
+    n1_all[e] = low(values * inv * gains[0:1, :])
+    stages = line_stages(n1_all, *sems[18:])
+    stages[0]()
+
+    def hop(owner, half, sems_out, sems_in, slot, device):
+        block = columns_all.at[owner, pl.ds(4 * half, 4)]
+        return send(block, block, sems_out.at[slot], sems_in.at[slot], device)
+
+    def over_x(slot):
+        owner, half = ((b, 0), (b, 1), (b ^ 2, 1))[slot]
+        return hop(owner, half, x_send, x_recv, slot, over[0])
+
+    def over_y(slot):
+        owner, half = ((b, 1), (b, 0), (b ^ 1, 0))[slot]
+        return hop(owner, half, y_send, y_recv, slot, over[1])
+
+    def out_block(owner):
+        return out_all.at[core, owner]
+
+    for copy in across:
+        copy.wait()
+    for slot in range(2):
+        over_x(slot).start()
+        over_y(slot).start()
+    for copy in along:
+        copy.wait()
+    beyond = []
+    for i, device in enumerate(over):
+        beyond.append(send(out_block(b), out_block(b), o_send.at[i], o_recv.at[i], device))
+        beyond[-1].start()
+
+    def out_pair(slot):
+        block = out_block(b ^ slot)
+        return send(block, block, p_send.at[slot], p_recv.at[slot], (b, e ^ 1))
+
+    out_pair(0).start()
+    stages[1]()
+    over_x(0).wait_recv()
+    over_y(2).start()
+    over_y(0).wait_recv()
+    over_x(2).start()
+    stages[2]()
+    stages[3]()
+    for i, copy in enumerate(beyond):
+        copy.wait()
+        out_pair(i + 1).start()
+    stages[4]()
+    for slot in range(3):
+        for over_one in (over_x, over_y):
+            if slot > 0:
+                over_one(slot).wait_recv()
+            over_one(slot).wait_send()
+    for copy in rest:
+        copy.wait()
+    for slot in range(4):
+        out_pair(slot).wait()
+
+
+def opening(rows, small, marks, columns, w_out):
+    tokens, width = rows.shape
+    sizes = (3, 3, 7, 7, 7, 7, 7, 7, 3, 3, 3, 3, 3, 3, 3, 3, 4, 4)
+    return kernel_call(
+        opening_kernel,
+        [
+            ((8, tokens, width), LOW),
+            ((2, width), F32),
+            ((8, 4, 8, 128), F32),
+            ((8, 8, 128), F32),
+            ((4, *columns.shape), LOW),
+            ((2, 4, 4, *w_out.shape), LOW),
+        ],
+        (rows, small, marks, columns, w_out),
+        [pltpu.SemaphoreType.DMA((size,)) for size in sizes] + GATHER_SEMS,
+        0,
+    )
+
+
+def holder(e):
+    return (lax.rem(e, 2) == 0) | (e == 3), jnp.where(e == 3, 4, e // 2)
+
+
+def middle_kernel(
+    attended, w_out, rows, gain, attn, resid, n2_all, a_send, a_recv, *sems
+):
+    b, e, z, core = place()
+    greet(pack_mates())
+    holds, pair = holder(e)
+
+    def give(i):
+        other = lax.rem(e + i, 8)
+        return send(
+            attended.at[other], attn.at[pair], a_send.at[i - 1], a_recv.at[pair], (b, other)
+        )
+
+    @pl.when(holds)
+    def _():
+        for i in range(1, 8):
+            give(i).start()
+        attn[pair] = attended[e]
+
+    total = rows[...]
+    for source, index in PAIR_OF.items():
+
+        @pl.when(e != source)
+        def _():
+            block = attn.at[index]
+            send(block, block, a_send.at[0], a_recv.at[index], (b, source)).wait_recv()
+
+        size = attn.shape[2]
+        total = total + dot(attn[index], w_out[index * size : (index + 1) * size, :])
+    resid[...] = total
+    inv = lax.rsqrt(jnp.mean(total * total, axis=1, keepdims=True) + EPSILON)
+    n2_all[e] = low(total * inv * gain[...])
+    line_gather(n2_all, *sems)
+
+    @pl.when(holds)
+    def _():
+        for i in range(1, 8):
+            give(i).wait_send()
+
+
+def middle(attended, w_out, rows, gain):
+    tokens, width = rows.shape
+    pair = attended.shape[2]
+    return kernel_call(
+        middle_kernel,
+        [
+            ((width // pair, tokens, pair), LOW),
+            ((tokens, width), F32),
+            ((8, tokens, width), LOW),
+        ],
+        (attended, w_out, rows, gain),
+        [pltpu.SemaphoreType.DMA((7,)), pltpu.SemaphoreType.DMA((len(PAIR_OF),))] + GATHER_SEMS,
+        1,
+    )
+
+
+def turn_kernel(
+    part,
+    upstream,
+    gates,
+    w_router,
+    resid,
+    gain,
+    w_out,
+    dresid,
+    dlogits,
+    gain_term,
+    darrived,
+    dattn,
+    a_send,
+    a_recv,
+    *scratch,
+):
+    b, e, z, core = place()
+    greet(pack_mates())
+    holds, pair = holder(e)
+    total = line_scatter(part, *scratch)
+    width = upstream.shape[1]
+    experts = gates.shape[1]
+    dgate = total[:, width : width + experts] + total[:, width + experts : width + 2 * experts]
+    own = gates[...]
+    dlog = low(own * (dgate - jnp.sum(own * dgate, axis=1, keepdims=True)))
+    dlogits[...] = dlog
+    dn2 = total[:, :width] + dot(dlog, w_router[...])
+    rows = resid[...]
+    inv = lax.rsqrt(jnp.mean(rows * rows, axis=1, keepdims=True) + EPSILON)
+    xhat = rows * inv
+    gain_term[...] = jnp.sum(dn2 * xhat, axis=0, keepdims=True)
+    scaled = dn2 * gain[...]
+    grad = upstream[...] + inv * (scaled - xhat * jnp.mean(scaled * xhat, axis=1, keepdims=True))
+    dresid[...] = grad
+    back = low(dot(low(grad), w_out[...], ((1,), (1,))))
+    size = dattn.shape[2]
+
+    def give(source, index):
+        return send(dattn.at[index], darrived.at[e], a_send.at[index], a_recv.at[e], (b, source))
+
+    for source, index in PAIR_OF.items():
+        dattn[index] = back[:, index * size : (index + 1) * size]
+
+        @pl.when(e != source)
+        def _():
+            give(source, index).start()
+
+    @pl.when(jnp.logical_not(holds))
+    def _():
+        darrived[...] = jnp.zeros_like(darrived)
+
+    @pl.when(holds)
+    def _():
+        darrived[e] = dattn[pair]
+        for i in range(1, 8):
+            other = lax.rem(e + i, 8)
+            block = darrived.at[other]
+            send(block, block, a_send.at[0], a_recv.at[other], (b, other)).wait_recv()
+
+    for source, index in PAIR_OF.items():
+
+        @pl.when(e != source)
+        def _():
+            give(source, index).wait_send()
+
+
+def turn(part, upstream, gates, w_router, resid, gain, w_out):
+    tokens, width = upstream.shape
+    pair = 2 * HEAD
+    count = len(PAIR_OF)
+    return kernel_call(
+        turn_kernel,
+        [
+            ((tokens, width), F32),
+            (gates.shape, LOW),
+            ((1, width), F32),
+            ((8, tokens, pair), LOW),
+        ],
+        (part, upstream, gates, w_router, resid, gain, w_out),
+        [
+            pltpu.VMEM((count, tokens, pair), LOW),
+            pltpu.SemaphoreType.DMA((count,)),
+            pltpu.SemaphoreType.DMA((8,)),
+        ]
+        + scatter_scratch(tokens, part.shape[2])
+        + SCATTER_SEMS,
+        2,
+    )
+
+
+def closing_kernel(part, rows, gain, dresid, input_grad, *scratch):
+    greet_line()
+    values = rows[...]
+    inv = lax.rsqrt(jnp.mean(values * values, axis=1, keepdims=True) + EPSILON)
+    xhat = values * inv
+    scaled = line_scatter(part, *scratch) * gain[...]
+    input_grad[...] = dresid[...] + inv * (
+        scaled - xhat * jnp.mean(scaled * xhat, axis=1, keepdims=True)
+    )
+
+
+def closing(part, rows, gain, dresid):
+    tokens, width = rows.shape
+    return kernel_call(
+        closing_kernel,
+        [((tokens, width), F32)],
+        (part, rows, gain, dresid),
+        scatter_scratch(tokens, width) + SCATTER_SEMS,
+        3,
+    )[0]
 
 
 def exchange(values):
@@ -455,37 +1069,39 @@
         sup_low.reshape(8, rows_w, 2, s_own), ((0, 0), (0, 0), (0, 0), (0, s_pad - s_own))
     )
     columns = jnp.concatenate([columns, sup_low.reshape(8, rows_w, 2 * s_pad)], axis=2)
-    columns = exchange(columns).reshape(8 * rows_w, 3 * pair + 2 * s_pad)
-    columns = gather_batch(columns, 0, 0)
+    up_near = gather_near(low(expert_up))
+    down_near = gather_near(low(expert_down))
+    sdown_near = gather_near(low(shared_down))
+    core = lax.rem(e, 2)
+
+    small = jnp.concatenate(
+        [
+            router_weight.reshape(-1, 128),
+            jnp.pad(gain_attn[None], ((0, 0), (0, 128 - rows_w))),
+            jnp.pad(gain_ffn[None], ((0, 0), (0, 128 - rows_w))),
+            jnp.zeros((1, 128), F32),
+        ]
+    )
+    small = low(small).astype(F32)
+    marks = jnp.concatenate([routes[0].T, seq_ids], axis=0).astype(F32)
+    marks = jnp.pad(marks, ((0, 7 - TOP), (0, 0)))
+    n1_all, gains, small, marks, columns, w_out = opening(
+        rows_in, small, marks, columns, low(out_weight)
+    )
+    n1_all = n1_all.reshape(length, width)
+    columns = columns.reshape(width, 3 * pair + 2 * s_pad)
     w_qkv = columns[:, : 3 * pair]
     w_sup = columns[:, 3 * pair :]
-    up_low = gather_batch(low(expert_up), 1, 1)
-    down_low = gather_batch(low(expert_down), 1, 1)
-    w_sdown = gather_batch(low(shared_down), 0, 1)
-    w_sdown = jnp.pad(w_sdown, ((0, s_pad - s_own), (0, 0)))
-    core = lax.rem(e, 2)
-    out_z = gather_tokens(low(out_weight))
-    half_rows = 4 * rows_w
-    out_mine = lax.dynamic_slice_in_dim(out_z, core * half_rows, half_rows, 0)
-    out_mine = gather_batch(out_mine, 0, 1).reshape(4, 1, half_rows, width)
-    out_other = swap(out_mine, 0, 1)
-    w_out = jnp.zeros((4, 2, half_rows, width), LOW)
-    w_out = lax.dynamic_update_slice_in_dim(w_out, out_mine, core, 1)
-    w_out = lax.dynamic_update_slice_in_dim(w_out, out_other, 1 - core, 1).reshape(width, width)
-
-    small = jnp.concatenate([router_weight, gain_attn[:, None], gain_ffn[:, None]], axis=1)
-    small = lax.all_gather(low(small), AXES, axis=0, tiled=True)
-    w_router = small[:, :experts]
-    gain_first = small[:, experts].astype(F32)
-    gain_second = small[:, experts + 1].astype(F32)
-    marks = gather_tokens(jnp.concatenate([routes[0], seq_ids[0][:, None]], axis=1))
+    w_out = w_out.transpose(1, 2, 0, 3, 4).reshape(width, width)
+    router_rows = rows_w * experts // 128
+    w_router = low(small[:, :, :router_rows].transpose(1, 0, 2, 3).reshape(width, experts))
+    gain_first = gains[0:1]
+    gain_second = gains[1:2]
+    marks = marks.astype(jnp.int32).transpose(0, 2, 1).reshape(length, 8)
     route_all = marks[:, :TOP]
     ids_all = marks[:, TOP]
-    cot_all = gather_tokens(low(upstream))
-
-    inv_first = lax.rsqrt(jnp.mean(rows_in * rows_in, axis=1, keepdims=True) + EPSILON)
-    xhat_first = rows_in * inv_first
-    n1_all = gather_tokens(low(xhat_first * gain_first))
+    cot_all = gather_pack(after(low(upstream), n1_all)).reshape(length, width)
+
     positions = jnp.arange(length, dtype=jnp.int32)
     projected = dot(n1_all, w_qkv)
     queries = low(rotate(projected[:, :pair].reshape(length, 2, HEAD), positions, 1.0))
@@ -501,14 +1117,17 @@
     attn_low = low(attn_p)
     attended = jnp.einsum("hqk,khd->qhd", attn_low, values, preferred_element_type=F32)
     attended_low = low(attended)
-    arrived = exchange(attended_low.reshape(8, tokens, pair))
-    attn = jnp.concatenate([arrived[i] for i in PAIR_OF], axis=1)
-    resid = rows_in + dot(attn, w_out)
-
-    inv_second = lax.rsqrt(jnp.mean(resid * resid, axis=1, keepdims=True) + EPSILON)
-    xhat_second = resid * inv_second
-    n2 = low(xhat_second * gain_second)
-    n2_all = gather_tokens(n2)
+    up_low = gather_far(after(up_near, attended_low), 1, 1)
+    attn, resid, n2_all = middle(
+        attended_low.reshape(8, tokens, pair), w_out, rows_in, gain_second
+    )
+    attn = attn.transpose(1, 0, 2).reshape(tokens, width)
+
+    n2 = lax.dynamic_index_in_dim(n2_all, e, 0, False)
+    n2_all = n2_all.reshape(length, width)
+    down_low = gather_far(after(down_near, n2_all), 1, 1)
+    w_sdown = gather_far(after(sdown_near, n2_all), 0, 1)
+    w_sdown = jnp.pad(w_sdown, ((0, s_pad - s_own), (0, 0)))
     logits = dot(n2_all, w_router)
     hot = route_all[:, :, None] == jnp.arange(experts, dtype=jnp.int32)[None, None, :]
     routed_to = jnp.any(hot, axis=1)
@@ -545,7 +1164,6 @@
     dpre = low(jnp.concatenate([back * slope, back * silu], axis=1))
     sup_term = dot(n2_all, dpre, ((0,), (0,)))
     drow_part = drow_part + dot(dpre, w_sup, ((1,), (1,)))
-    output_rows = resid + scatter_tokens(low(output_part))
     expert_up_grad = scatter_batch(low(jnp.stack(up_terms)), 1, 1)
     expert_down_grad = scatter_batch(low(jnp.stack(down_terms)), 1, 1)
     shared_down_grad = scatter_batch(low(sdown_term), 0, 1)
@@ -555,35 +1173,29 @@
     dgate_high = low(dgate)
     dgate_rest = low(dgate - dgate_high.astype(F32))
     spare = jnp.zeros((length, 128 - 2 * experts), LOW)
-    dn2 = scatter_tokens(
-        jnp.concatenate([low(drow_part), dgate_high, dgate_rest, spare], axis=1)
-    )
-    dgate = dn2[:, width : width + experts] + dn2[:, width + experts : width + 2 * experts]
+    part = jnp.concatenate([low(drow_part), dgate_high, dgate_rest, spare], axis=1)
     own_gates = lax.dynamic_slice_in_dim(gates, e * tokens, tokens, 0)
-    dlogits = low(own_gates * (dgate - jnp.sum(own_gates * dgate, axis=1, keepdims=True)))
+    dresid, dlogits, gain_ffn_term, dattn = turn(
+        part.reshape(8, tokens, part.shape[1]),
+        upstream,
+        own_gates,
+        w_router.T,
+        resid,
+        gain_second,
+        w_out,
+    )
+    dattn = dattn.reshape(length, 2, HEAD)
+    output_part = after(low(output_part), dresid).reshape(8, tokens, width)
+    output_rows = resid + scatter_pack(output_part)
     router_term = dot(dlogits, n2, ((0,), (0,)))
-    dn2 = dn2[:, :width] + dot(dlogits, w_router, ((1,), (1,)))
-    dresid, gain_ffn_term = norm_back(dn2, xhat_second, inv_second, gain_second)
-    dresid = upstream + dresid
+    small = total_all(jnp.concatenate([router_term, gain_ffn_term], axis=0))
+    small = lax.dynamic_slice_in_dim(small, (b * 8 + e) * rows_w, rows_w, 1)
     dproj = low(dresid)
-    dattn = low(dot(dproj, w_out, ((1,), (1,))))
-    dattn = jnp.stack(
-        [
-            dattn[:, PAIR_OF[i] * pair : (PAIR_OF[i] + 1) * pair]
-            if i in PAIR_OF
-            else jnp.zeros((tokens, pair), LOW)
-            for i in range(8)
-        ]
-    )
-    dattn = exchange(dattn).reshape(length, 2, HEAD)
-    out_term = dot(attn, dproj, ((0,), (0,))).reshape(4, 2, half_rows, width)
-    out_away = swap(low(lax.dynamic_slice_in_dim(out_term, 1 - core, 1, 1)), 0, 1)
-    out_term = lax.dynamic_slice_in_dim(out_term, core, 1, 1) + out_away
-    out_term = scatter_batch(low(out_term).reshape(4 * half_rows, width), 0, 1)
-    out_pad = lax.dynamic_update_slice_in_dim(
-        jnp.zeros((2 * half_rows, width), LOW), low(out_term), core * half_rows, 0
-    )
-    out_grad = scatter_tokens(out_pad)
+    out_term = dot(attn, dproj, ((0,), (0,))).reshape(4, 4, 2, rows_w, width)
+    out_away = swap(low(lax.dynamic_index_in_dim(out_term, 1 - core, 2, False)), 0, 1)
+    out_term = lax.dynamic_index_in_dim(out_term, core, 2, False) + out_away
+    out_term = scatter_batch(low(out_term).reshape(16 * rows_w, width), 0, 1)
+    out_grad = scatter_z(out_term.reshape(4, rows_w, width))
 
     delta = jnp.sum(dattn.astype(F32) * attended, axis=2).T[:, :, None]
     dprob = jnp.einsum("qhd,khd->hqk", dattn, values, preferred_element_type=F32)
@@ -602,9 +1214,8 @@
         )
     )
     qkv_term = dot(n1_all, dprojected, ((0,), (0,)))
-    dn1 = scatter_tokens(low(dot(dprojected, w_qkv, ((1,), (1,)))))
-    dinput, gain_attn_term = norm_back(dn1, xhat_first, inv_first, gain_first)
-    input_grad = dresid + dinput
+    dn1 = low(dot(dprojected, w_qkv, ((1,), (1,))))
+    input_grad = closing(dn1.reshape(8, tokens, width), rows_in, gain_first, dresid)
 
     columns = scatter_batch(low(jnp.concatenate([qkv_term, sup_term], axis=1)), 0, 0)
     columns = exchange(low(columns).reshape(8, rows_w, 3 * pair + 2 * s_pad)).astype(F32)
@@ -615,9 +1226,8 @@
     sup_grad = sup_grad.reshape(8, rows_w, 2, 4, s_rows).transpose(1, 2, 3, 0, 4)
     sup_grad = sup_grad.reshape(rows_w, shared_up.shape[1])
 
-    small = jnp.concatenate([router_term, gain_attn_term[None], gain_ffn_term[None]], axis=0)
-    small = lax.psum(small, AXES)
-    small = lax.dynamic_slice_in_dim(small, (b * 8 + e) * rows_w, rows_w, 1)
+    own_first = low(gain_attn).astype(F32)
+    gain_attn_grad = jnp.sum(low(qkv_weight).astype(F32) * qkv_grad, axis=1) / own_first
     return (
         output_rows[None],
         input_grad[None],
@@ -626,8 +1236,8 @@
         sup_grad,
         shared_down_grad,
         small[:experts].T,
+        gain_attn_grad,
         small[experts],
-        small[experts + 1],
         expert_up_grad,
         expert_down_grad,
     )

time: 872 us -> 768 us (0.88)
  Pallas kernels: 0 us -> 210 us
  waiting for transfers between devices: 359 us -> 194 us
  blocking collectives: 101 us -> 0 us
  matrix products: 137 us -> 118 us
  between operations: 16.2 us -> 2.91 us
  other arithmetic: 73.6 us -> 60.5 us
    pallas_call x0 -> x4, Pallas kernels: none -> 210 us  [kernel_call(): pl.pallas_call(body, out_shape=[jax.ShapeDtypeStruct(shape, dtype) for sh...]
    psum x1 -> x0, waiting for transfers between devices: 118 us -> none  [pack_device(): small = lax.psum(small, AXES)]
    all_gather x3 -> x0, blocking collectives: 101 us -> none  [the longest x2 56.9 us: gather_tokens(): return lax.all_gather(values, 'expert', axis=0, tiled=True)]
    ppermute x52 -> x50, waiting for transfers between devices: 212 us -> 179 us  [swap(): return lax.ppermute(values, AXES, pairs)]
    all_to_all x4 -> x1, waiting for transfers between devices: 29.3 us -> 0.01 us  [exchange(): lax.all_to_all(values, 'expert', split_axis=0, concat_axis=0, tiled=True)]
    ppermute x0 -> x9, starting transfers between devices: none -> 18.7 us  [z_shift(): return lax.ppermute(values, AXES, pairs)]
    dot_general x27 -> x24, matrix products: 111 us -> 94.8 us  [dot(): lax.dot_general(left, right, (dims, ((), ())), preferred_element_type=F32)]
    ppermute x0 -> x9, waiting for transfers between devices: none -> 14.1 us  [z_shift(): return lax.ppermute(values, AXES, pairs)]
  transfers between devices with their start and end apart: 64 -> 60, of which waited for: 25 -> 20; matrix products, arithmetic and copies ran while one was open for 29% -> 19% of each run, Pallas kernels for 0% -> 6%
where the time goes in v2:
time: 768 us; the launch traced here: 758 us
  Pallas kernels  210 us (27%)
  waiting for transfers between devices  194 us (25%)
  matrix products  118 us (15%)
  local copies, waits for them, and re-layouts  104 us (14%)
  starting transfers between devices  69.7 us (9%)
  other arithmetic  60.5 us (8%)
    pallas_call x4, Pallas kernels, kernel_call(): pl.pallas_call(body, out_shape=[jax.ShapeDtypeStruct(shape, dtype) for sh...  210 us
    ppermute x50, waiting for transfers between devices, swap(): return lax.ppermute(values, AXES, pairs)  179 us
    dot_general x24, matrix products, dot(): lax.dot_general(left, right, (dims, ((), ())), preferred_element_type=F32)  94.8 us
    ppermute x50, starting transfers between devices, swap(): return lax.ppermute(values, AXES, pairs)  47.3 us
    unnamed x219, local copies, waits for them, and re-layouts  25.1 us
    convert_element_type x18, other arithmetic, low(): return values.astype(LOW)  21.1 us
    ppermute x9, starting transfers between devices, z_shift(): return lax.ppermute(values, AXES, pairs)  18.7 us
  transfers between devices with their start and end apart: 60, of which 20 were waited for; matrix products, arithmetic and copies ran while one was open for 19% of the time, Pallas kernels for 6%

profile of v2, /device:TPU:0, one launch (start us, length us, event | category | flops | bytes accessed | tf_op | source)
XLA Modules:
  0.0 758.4 jit_solution(2504728225649026623)
XLA Ops:
  9.4 77.6 %shard_map.212 = (bf16[8,128,1280]{2,1,0:T(8,128)(2,1)S(1)}, f32[2,1280]{1,0:T(2,128)S(1)}, f32[8,4,8,128]{3,2,1,0:T(8,128)S(1)}, f32[8,8,128]{2,1,0:T(8,128)S(1...) custom-call(f32[128,1280]{1,0:T(8,128)S(1)} %bitcast.201, f32[8,128]{1,0:T(8,128)S(1)} %fusion.80.small, ...), custom_call_target="tpu_custom_call" | custom-call | tf_op jit(solution)/shard_map/pallas_call | solution.py:702
  114.0 8.7 %fusion.104 = (f32[2,1024]{1,0:T(2,128)S(1)}, f32[2,1024,1024]{1,2,0:T(8,128)}) fusion(pred[1024,1024]{0,1:T(8,128)(4,1)} %fusion.6, bf16[1024,2,64]{2,0,1:T(8,128)(2,1)} %get-tuple-element.120, bf16[1024,2,64]{2,0,1:T(8,128)(2,1)} %get-tuple-element.121, bf16[1024,2,64]{2,0,1:T(8,128)(2,1)} %get-tuple-element.83, bf16[1024,2,64]{2,0,1:T(8,128)(2,1)} %get-tuple-element.82), kind=kOutput, calls=%fused_computation.292 | convolution fusion | flops 547357696 | bytes 10493952 | tf_op jit(solution)/shard_map/sub | solution.py:1114
  122.7 4.7 fusion.14
  136.4 42.6 %shard_map.213 = (bf16[5,128,256]{2,1,0:T(8,128)(2,1)S(1)}, f32[128,1280]{1,0:T(8,128)S(1)}, bf16[8,128,1280]{2,1,0:T(8,128)(2,1)S(1)}) custom-call(bf16[8,128,256]{2,1,0:T(8,128)(2,1)S(1)} %copy.228.attended, bf16[1280,1280]{1,0:T(8,128)(2,1)} %bitcast.218, f32[128,1280]{1,0:T(8,128)S(1)} %bitcast.202, f32[1,1280]{1,0:T(1,128)S(1)} %get-tuple-element.140.gain), custom_call_target="tpu_custom_call" | custom-call | tf_op jit(solution)/shard_map/pallas_call | solution.py:702
  219.4 47.4 %collective-permute-done.37 = bf16[28,640]{1,0:T(8,128)(2,1)S(1)} collective-permute-done((bf16[28,640]{1,0:T(8,128)(2,1)S(1)}, bf16[28,640]{1,0:T(8,128)(2,1)S(1)}, u32[]{:S(2)}, u32[]{:S(2)}) %collective-permute-start.37) | collective-permute-done | bytes 35872 | tf_op jit(solution)/shard_map/ppermute | solution.py:352
  268.8 12.3 %collective-permute-done.40 = bf16[28,640]{1,0:T(8,128)(2,1)S(1)} collective-permute-done((bf16[28,640]{1,0:T(8,128)(2,1)S(1)}, bf16[28,640]{1,0:T(8,128)(2,1)S(1)}, u32[]{:S(2)}, u32[]{:S(2)}) %collective-permute-start.40) | collective-permute-done | bytes 35872 | tf_op jit(solution)/shard_map/ppermute | solution.py:352
  301.6 12.8 %collective-permute-done.3 = bf16[2,160,1792]{2,1,0:T(8,128)(2,1)S(1)} collective-permute-done((bf16[2,160,1792]{2,1,0:T(8,128)(2,1)}, bf16[2,160,1792]{2,1,0:T(8,128)(2,1)S(1)}, u32[]{:S(2)}, u32[]{:S(2)}) %collective-permute-start.3) | collective-permute-done | bytes 1146912 | tf_op jit(solution)/shard_map/ppermute | solution.py:352
  317.6 6.9 fusion.9
  324.5 6.9 fusion.11
  331.4 7.9 %multiply_convert_fusion.4 = (bf16[1024,896]{1,0:T(8,128)(2,1)S(1)}, bf16[1024,896]{1,0:T(8,128)(2,1)S(1)}, f32[1024]{0:T(1024)S(1)}, bf16[1024,896]{1,0:T(8,128)(2,1)}) fusion(f32[1024,1792]{1,0:T(8,128)} %fusion.9, f32[1024]{0:T(1024)S(1)} %get-tuple-element.60, bf16[1024,1280]{1,0:T(8,128)(2,1)S(1)} %bitcast.224, bf16[2,896,1280]{2,1,0:T(8,128)(2,1)S(1)} %bitcast.242), kind=kOutput, calls=%fused_computation.52 | convolution fusion | flops 2366241792 | bytes 17768448 | tf_op jit(solution)/shard_map/dot_general | solution.py:344
  339.3 9.6 %multiply_convert_fusion.2 = (bf16[1024,896]{1,0:T(8,128)(2,1)}, bf16[1024,896]{1,0:T(8,128)(2,1)}, f32[1024]{0:T(1024)S(1)}, bf16[1024,896]{1,0:T(8,128)(2,1)}) fusion(f32[1024,1792]{1,0:T(8,128)} %fusion.11, f32[1024]{0:T(1024)S(1)} %get-tuple-element.59, bf16[1024,1280]{1,0:T(8,128)(2,1)S(1)} %bitcast.225, bf16[2,896,1280]{2,1,0:T(8,128)(2,1)S(1)} %bitcast.242), kind=kOutput, calls=%fused_computation.50 | convolution fusion | flops 2366241792 | bytes 17768448 | tf_op jit(solution)/shard_map/dot_general | solution.py:344
  349.0 4.9 fusion.8
  353.9 4.9 fusion.10
  363.7 4.8 concatenate.89
  372.3 50.6 %shard_map.214 = (f32[128,1280]{1,0:T(8,128)S(1)}, bf16[128,16]{1,0:T(8,128)(2,1)S(1)}, f32[1,1280]{1,0:T(1,128)S(1)}, bf16[8,128,256]{2,1,0:T(8,128)(2,1)S(1)}) custom-call(bf16[8,128,1408]{2,1,0:T(8,128)(2,1)S(1)} %bitcast.200, f32[128,1280]{1,0:T(8,128)S(1)} %bitcast.206, f32[128,16]{1,0:T(8,128)S(1)} %copy-done.8, bf16[16,1280]{1,0:T(8,128)(2,1)S(1)} %bitcast.208, ...), custom_call_target="tpu_custom_call" | custom-call | tf_op jit(solution)/shard_map/pallas_call | solution.py:702
  426.5 4.6 convolution_convert_fusion.7
  431.3 4.8 multiply_convert_fusion
  450.2 6.9 fusion.1
  457.2 6.8 fusion.2
  464.0 4.6 fusion.23
  472.6 4.6 fusion.25
  481.2 38.7 %shard_map.215 = f32[128,1280]{1,0:T(8,128)S(1)} custom-call(bf16[8,128,1280]{2,1,0:T(8,128)(2,1)S(1)} %bitcast.204, f32[128,1280]{1,0:T(8,128)S(1)} %bitcast.203, f32[1,1280]{1,0:T(1,128)S(1)} %get-tuple-element.139.gain, f32[128,1280]{1,0:T(8,128)S(1)} %get-tuple-element.53.dresid), custom_call_target="tpu_custom_call" | custom-call | tf_op jit(solution)/shard_map/pallas_call | solution.py:702
  520.0 4.8 fusion.39
  554.5 9.5 %collective-permute-done.44 = f32[17,1280]{1,0:T(8,128)S(1)} collective-permute-done((f32[17,1280]{1,0:T(8,128)S(1)}, f32[17,1280]{1,0:T(8,128)S(1)}, u32[]{:S(2)}, u32[]{:S(2)}) %collective-permute-start.44) | collective-permute-done | bytes 87072 | tf_op jit(solution)/shard_map/ppermute | solution.py:352
  572.9 4.7 collective-permute-done.46
  579.0 23.5 %collective-permute-done.54 = bf16[2,112,1280]{2,1,0:T(8,128)(2,1)S(1)} collective-permute-done((bf16[2,112,1280]{2,1,0:T(8,128)(2,1)S(1)}, bf16[2,112,1280]{2,1,0:T(8,128)(2,1)S(1)}, u32[]{:S(2)}, u32[]{:S(2)}) %collective-permute-start.54) | collective-permute-done | bytes 573472 | tf_op jit(solution)/shard_map/ppermute | solution.py:352
  608.5 8.9 %collective-permute-done.22 = bf16[160,1024]{0,1:T(8,128)(2,1)S(1)} collective-permute-done((bf16[160,1024]{0,1:T(8,128)(2,1)S(1)}, bf16[160,1024]{0,1:T(8,128)(2,1)S(1)}, u32[]{:S(2)}, u32[]{:S(2)}) %collective-permute-start.22) | collective-permute-done | bytes 327712 | tf_op jit(solution)/shard_map/ppermute | solution.py:352
  632.1 6.9 collective-permute-done.55
  651.0 19.9 %collective-permute-done.51 = bf16[2,160,1792]{2,1,0:T(8,128)(2,1)S(1)} collective-permute-done((bf16[2,160,1792]{2,1,0:T(8,128)(2,1)}, bf16[2,160,1792]{2,1,0:T(8,128)(2,1)S(1)}, u32[]{:S(2)}, u32[]{:S(2)}) %collective-permute-start.51) | collective-permute-done | bytes 1146912 | tf_op jit(solution)/shard_map/ppermute | solution.py:352
  681.8 10.1 %collective-permute-done.18 = bf16[128,1280]{1,0:T(8,128)(2,1)S(1)} collective-permute-done((bf16[128,1280]{1,0:T(8,128)(2,1)S(1)}, bf16[128,1280]{1,0:T(8,128)(2,1)S(1)}, u32[]{:S(2)}, u32[]{:S(2)}) %collective-permute-start.18) | collective-permute-done | bytes 327712 | tf_op jit(solution)/shard_map/ppermute | solution.py:412
  721.3 13.6 %collective-permute-done.30 = bf16[160,640]{1,0:T(8,128)(2,1)S(1)} collective-permute-done((bf16[160,640]{1,0:T(8,128)(2,1)}, bf16[160,640]{1,0:T(8,128)(2,1)S(1)}, u32[]{:S(2)}, u32[]{:S(2)}) %collective-permute-start.30) | collective-permute-done | bytes 204832 | tf_op jit(solution)/shard_map/ppermute | solution.py:352
  741.0 8.6 %collective-permute-start.34 = (bf16[40,1280]{1,0:T(8,128)(2,1)S(1)}, bf16[40,1280]{1,0:T(8,128)(2,1)S(1)}, u32[]{:S(2)}, u32[]{:S(2)}) collective-permute-start(bf16[40,1280]{1,0:T(8,128)(2,1)S(1)} %get-tuple-element.128), channel_id=1, source_target_pairs={{0,4},{1,5},{2,6},{3,7},{4,0},{5,1},{6,2},{7,3},{8,12},{9,13},{10,... | collective-permute-start | bytes 307208 | tf_op jit(solution)/shard_map/ppermute | solution.py:412
  (505 shorter events, 271.2 us)
Async XLA Ops:
  87.1 93.7 %collective-permute-start.12 = (bf16[128,1280]{1,0:T(8,128)(2,1)}, bf16[128,1280]{1,0:T(8,128)(2,1)}, u32[]{:S(2)}, u32[]{:S(2)}) collective-permute-start(bf16[128,1280]{1,0:T(8,128)(2,1)} %bitcast_convert_fusion), channel_id=1, source_target_pairs={{0,2},{1,3},{2,4},{3,5},{4,6},{5,7},{6,0},{7,1},{8,10},{9,11},{10,... | collective-permute-start | bytes 983048 | tf_op jit(solution)/shard_map/ppermute | solution.py:412
  88.2 95.1 %collective-permute-start.13 = (bf16[128,1280]{1,0:T(8,128)(2,1)}, bf16[128,1280]{1,0:T(8,128)(2,1)}, u32[]{:S(2)}, u32[]{:S(2)}) collective-permute-start(bf16[128,1280]{1,0:T(8,128)(2,1)} %bitcast_convert_fusion), channel_id=1, source_target_pairs={{0,4},{1,5},{2,6},{3,7},{4,0},{5,1},{6,2},{7,3},{8,12},{9,13},{10,... | collective-permute-start | bytes 983048 | tf_op jit(solution)/shard_map/ppermute | solution.py:412
  90.5 94.5 %collective-permute-start.14 = (bf16[128,1280]{1,0:T(8,128)(2,1)}, bf16[128,1280]{1,0:T(8,128)(2,1)}, u32[]{:S(2)}, u32[]{:S(2)}) collective-permute-start(bf16[128,1280]{1,0:T(8,128)(2,1)} %bitcast_convert_fusion), channel_id=1, source_target_pairs={{0,6},{1,7},{2,0},{3,1},{4,2},{5,3},{6,4},{7,5},{8,14},{9,15},{10,... | collective-permute-start | bytes 983048 | tf_op jit(solution)/shard_map/ppermute | solution.py:412
  92.6 110.9 %collective-permute-start.4 = (bf16[2,224,1280]{2,1,0:T(8,128)(2,1)}, bf16[2,224,1280]{2,1,0:T(8,128)(2,1)}, u32[]{:S(2)}, u32[]{:S(2)}) collective-permute-start(bf16[2,224,1280]{2,1,0:T(8,128)(2,1)} %convert_element_type.433), channel_id=1, source_target_pairs={{0,8},{1,9},{2,10},{3,11},{4,12},{5,13},{6,14},{7,15},{8,0},{9,1},... | collective-permute-start | bytes 3440648 | tf_op jit(solution)/shard_map/ppermute | solution.py:352
  94.1 109.4 %collective-permute-start.5 = (bf16[2,224,1280]{2,1,0:T(8,128)(2,1)}, bf16[2,224,1280]{2,1,0:T(8,128)(2,1)}, u32[]{:S(2)}, u32[]{:S(2)}) collective-permute-start(bf16[2,224,1280]{2,1,0:T(8,128)(2,1)} %convert_element_type.433), channel_id=1, source_target_pairs={{0,16},{1,17},{2,18},{3,19},{4,20},{5,21},{6,22},{7,23},{8,24},{9,... | collective-permute-start | bytes 3440648 | tf_op jit(solution)/shard_map/ppermute | solution.py:352
  186.0 24.6 %collective-permute-start.15 = (bf16[4,128,1280]{2,1,0:T(8,128)(2,1)S(1)}, bf16[4,128,1280]{2,1,0:T(8,128)(2,1)}, u32[]{:S(2)}, u32[]{:S(2)}) collective-permute-start(bf16[4,128,1280]{2,1,0:T(8,128)(2,1)S(1)} %bitcast_dynamic-update-slice_fusion), channel_id=1, source_target_pairs={{0,1},{1,0},{2,3},{3,2},{4,5},{5,4},{6,7},{7,6},{8,9},{9,8},{10,11... | collective-permute-start | bytes 3932168 | tf_op jit(solution)/shard_map/ppermute | solution.py:352
  201.2 86.2 %collective-permute-start = (bf16[2,320,1792]{2,1,0:T(8,128)(2,1)}, bf16[2,320,1792]{2,1,0:T(8,128)(2,1)}, u32[]{:S(2)}, u32[]{:S(2)}) collective-permute-start(bf16[2,320,1792]{2,1,0:T(8,128)(2,1)} %convert_element_type.428), channel_id=1, source_target_pairs={{0,8},{1,9},{2,10},{3,11},{4,12},{5,13},{6,14},{7,15},{8,0},{9,1},... | collective-permute-start | bytes 6881288 | tf_op jit(solution)/shard_map/ppermute | solution.py:352
  202.5 84.8 %collective-permute-start.1 = (bf16[2,320,1792]{2,1,0:T(8,128)(2,1)}, bf16[2,320,1792]{2,1,0:T(8,128)(2,1)}, u32[]{:S(2)}, u32[]{:S(2)}) collective-permute-start(bf16[2,320,1792]{2,1,0:T(8,128)(2,1)} %convert_element_type.428), channel_id=1, source_target_pairs={{0,16},{1,17},{2,18},{3,19},{4,20},{5,21},{6,22},{7,23},{8,24},{9,... | collective-permute-start | bytes 6881288 | tf_op jit(solution)/shard_map/ppermute | solution.py:352
  204.7 81.7 %collective-permute-start.7 = (bf16[2,112,1280]{2,1,0:T(8,128)(2,1)S(1)}, bf16[2,112,1280]{2,1,0:T(8,128)(2,1)S(1)}, u32[]{:S(2)}, u32[]{:S(2)}) collective-permute-start(bf16[2,112,1280]{2,1,0:T(8,128)(2,1)S(1)} %slice.306), channel_id=1, source_target_pairs={{0,8},{1,9},{2,10},{3,11},{4,12},{5,13},{6,14},{7,15},{8,0},{9,1},... | collective-permute-start | bytes 1720328 | tf_op jit(solution)/shard_map/ppermute | solution.py:352
  215.9 50.8 %collective-permute-start.37 = (bf16[28,640]{1,0:T(8,128)(2,1)S(1)}, bf16[28,640]{1,0:T(8,128)(2,1)S(1)}, u32[]{:S(2)}, u32[]{:S(2)}) collective-permute-start(bf16[28,640]{1,0:T(8,128)(2,1)S(1)} %get-tuple-element.136), channel_id=1, source_target_pairs={{0,8},{1,9},{2,10},{3,11},{4,12},{5,13},{6,14},{7,15},{8,0},{9,1},... | collective-permute-start | bytes 107528 | tf_op jit(solution)/shard_map/ppermute | solution.py:352
  216.3 51.6 %collective-permute-start.36 = (bf16[28,640]{1,0:T(8,128)(2,1)S(1)}, bf16[28,640]{1,0:T(8,128)(2,1)S(1)}, u32[]{:S(2)}, u32[]{:S(2)}) collective-permute-start(bf16[28,640]{1,0:T(8,128)(2,1)S(1)} %get-tuple-element.135), channel_id=1, source_target_pairs={{0,8},{1,9},{2,10},{3,11},{4,12},{5,13},{6,14},{7,15},{8,0},{9,1},... | collective-permute-start | bytes 107528 | tf_op jit(solution)/shard_map/ppermute | solution.py:352
  290.6 23.8 %collective-permute-start.3 = (bf16[2,160,1792]{2,1,0:T(8,128)(2,1)}, bf16[2,160,1792]{2,1,0:T(8,128)(2,1)S(1)}, u32[]{:S(2)}, u32[]{:S(2)}) collective-permute-start(bf16[2,160,1792]{2,1,0:T(8,128)(2,1)} %slice.298), channel_id=1, source_target_pairs={{0,8},{1,9},{2,10},{3,11},{4,12},{5,13},{6,14},{7,15},{8,0},{9,1},... | collective-permute-start | bytes 3440648 | tf_op jit(solution)/shard_map/ppermute | solution.py:352
  525.9 38.8 %collective-permute-start.21 = (bf16[160,1024]{0,1:T(8,128)(2,1)}, bf16[160,1024]{0,1:T(8,128)(2,1)}, u32[]{:S(2)}, u32[]{:S(2)}) collective-permute-start(bf16[160,1024]{0,1:T(8,128)(2,1)} %get-tuple-element.131), channel_id=1, source_target_pairs={{0,8},{1,9},{2,10},{3,11},{4,12},{5,13},{6,14},{7,15},{8,0},{9,1},... | collective-permute-start | bytes 983048 | tf_op jit(solution)/shard_map/ppermute | solution.py:352
  527.8 79.6 %collective-permute-start.23 = (bf16[160,1024]{0,1:T(8,128)(2,1)}, bf16[160,1024]{0,1:T(8,128)(2,1)}, u32[]{:S(2)}, u32[]{:S(2)}) collective-permute-start(bf16[160,1024]{0,1:T(8,128)(2,1)} %slice.408), channel_id=1, source_target_pairs={{0,16},{1,17},{2,18},{3,19},{4,20},{5,21},{6,22},{7,23},{8,24},{9,... | collective-permute-start | bytes 983048 | tf_op jit(solution)/shard_map/ppermute | solution.py:352
  546.2 60.0 %collective-permute-start.20 = (bf16[160,1024]{0,1:T(8,128)(2,1)S(1)}, bf16[160,1024]{0,1:T(8,128)(2,1)S(1)}, u32[]{:S(2)}, u32[]{:S(2)}) collective-permute-start(bf16[160,1024]{0,1:T(8,128)(2,1)S(1)} %slice.404), channel_id=1, source_target_pairs={{0,8},{1,9},{2,10},{3,11},{4,12},{5,13},{6,14},{7,15},{8,0},{9,1},... | collective-permute-start | bytes 983048 | tf_op jit(solution)/shard_map/ppermute | solution.py:352
  547.7 23.2 %collective-permute-start.24 = (bf16[160,1024]{0,1:T(8,128)(2,1)S(1)}, bf16[160,1024]{0,1:T(8,128)(2,1)S(1)}, u32[]{:S(2)}, u32[]{:S(2)}) collective-permute-start(bf16[160,1024]{0,1:T(8,128)(2,1)S(1)} %copy-done.59), channel_id=1, source_target_pairs={{0,16},{1,17},{2,18},{3,19},{4,20},{5,21},{6,22},{7,23},{8,24},{9,... | collective-permute-start | bytes 983048 | tf_op jit(solution)/shard_map/ppermute | solution.py:352
  564.0 81.2 %collective-permute-start.48 = (bf16[2,160,1792]{2,1,0:T(8,128)(2,1)}, bf16[2,160,1792]{2,1,0:T(8,128)(2,1)}, u32[]{:S(2)}, u32[]{:S(2)}) collective-permute-start(bf16[2,160,1792]{2,1,0:T(8,128)(2,1)} %get-tuple-element.99), channel_id=1, source_target_pairs={{0,8},{1,9},{2,10},{3,11},{4,12},{5,13},{6,14},{7,15},{8,0},{9,1},... | collective-permute-start | bytes 3440648 | tf_op jit(solution)/shard_map/ppermute | solution.py:352
  569.7 32.8 %collective-permute-start.54 = (bf16[2,112,1280]{2,1,0:T(8,128)(2,1)S(1)}, bf16[2,112,1280]{2,1,0:T(8,128)(2,1)S(1)}, u32[]{:S(2)}, u32[]{:S(2)}) collective-permute-start(bf16[2,112,1280]{2,1,0:T(8,128)(2,1)S(1)} %get-tuple-element.115), channel_id=1, source_target_pairs={{0,8},{1,9},{2,10},{3,11},{4,12},{5,13},{6,14},{7,15},{8,0},{9,1},... | collective-permute-start | bytes 1720328 | tf_op jit(solution)/shard_map/ppermute | solution.py:352
  577.6 26.7 %collective-permute-start.57 = (bf16[2,112,1280]{2,1,0:T(8,128)(2,1)S(1)}, bf16[2,112,1280]{2,1,0:T(8,128)(2,1)S(1)}, u32[]{:S(2)}, u32[]{:S(2)}) collective-permute-start(bf16[2,112,1280]{2,1,0:T(8,128)(2,1)S(1)} %get-tuple-element.116), channel_id=1, source_target_pairs={{0,16},{1,17},{2,18},{3,19},{4,20},{5,21},{6,22},{7,23},{8,24},{9,... | collective-permute-start | bytes 1720328 | tf_op jit(solution)/shard_map/ppermute | solution.py:352
  606.3 25.3 %collective-permute-start.53 = (bf16[2,112,1280]{2,1,0:T(8,128)(2,1)}, bf16[2,112,1280]{2,1,0:T(8,128)(2,1)}, u32[]{:S(2)}, u32[]{:S(2)}) collective-permute-start(bf16[2,112,1280]{2,1,0:T(8,128)(2,1)} %slice.430), channel_id=1, source_target_pairs={{0,8},{1,9},{2,10},{3,11},{4,12},{5,13},{6,14},{7,15},{8,0},{9,1},... | collective-permute-start | bytes 1720328 | tf_op jit(solution)/shard_map/ppermute | solution.py:352
  607.4 24.3 %collective-permute-start.56 = (bf16[2,112,1280]{2,1,0:T(8,128)(2,1)S(1)}, bf16[2,112,1280]{2,1,0:T(8,128)(2,1)}, u32[]{:S(2)}, u32[]{:S(2)}) collective-permute-start(bf16[2,112,1280]{2,1,0:T(8,128)(2,1)S(1)} %slice.434), channel_id=1, source_target_pairs={{0,16},{1,17},{2,18},{3,19},{4,20},{5,21},{6,22},{7,23},{8,24},{9,... | collective-permute-start | bytes 1720328 | tf_op jit(solution)/shard_map/ppermute | solution.py:352
  619.2 23.3 %collective-permute-start.58 = (bf16[2,112,1280]{2,1,0:T(8,128)(2,1)}, bf16[2,112,1280]{2,1,0:T(8,128)(2,1)}, u32[]{:S(2)}, u32[]{:S(2)}) collective-permute-start(bf16[2,112,1280]{2,1,0:T(8,128)(2,1)} %add_convert_fusion.4), channel_id=1, source_target_pairs={{0,8},{1,9},{2,10},{3,11},{4,12},{5,13},{6,14},{7,15},{8,0},{9,1},... | collective-permute-start | bytes 1720328 | tf_op jit(solution)/shard_map/ppermute | solution.py:352
  623.6 70.9 %all-to-all-start = ((bf16[8,40,1024]{2,1,0:T(8,128)(2,1)}), bf16[8,40,1024]{2,1,0:T(8,128)(2,1)S(1)}, u32[]{:S(2)}, u32[]{:S(2)}) async-start(bf16[8,40,1024]{2,1,0:T(8,128)(2,1)} %bitcast.249), calls=%async_computation | async-start | bytes 1310720 | tf_op jit(solution)/shard_map/all_to_all | solution.py:1024
  631.6 40.7 %collective-permute-start.16 = (bf16[4,128,1280]{2,1,0:T(8,128)(2,1)}, bf16[4,128,1280]{2,1,0:T(8,128)(2,1)S(1)}, u32[]{:S(2)}, u32[]{:S(2)}) collective-permute-start(bf16[4,128,1280]{2,1,0:T(8,128)(2,1)} %dynamic-slice_bitcast_fusion), channel_id=1, source_target_pairs={{0,1},{1,0},{2,3},{3,2},{4,5},{5,4},{6,7},{7,6},{8,9},{9,8},{10,11... | collective-permute-start | bytes 3932168 | tf_op jit(solution)/shard_map/ppermute | solution.py:352
  631.6 42.7 %collective-permute-start.26 = (bf16[4,4,40,1280]{3,2,1,0:T(8,128)(2,1)}, bf16[4,4,40,1280]{3,2,1,0:T(8,128)(2,1)S(1)}, u32[]{:S(2)}, u32[]{:S(2)}) collective-permute-start(bf16[4,4,40,1280]{3,2,1,0:T(8,128)(2,1)} %fusion.29), channel_id=1, source_target_pairs={{0,1},{1,0},{2,3},{3,2},{4,5},{5,4},{6,7},{7,6},{8,9},{9,8},{10,11... | collective-permute-start | bytes 4915208 | tf_op jit(solution)/shard_map/ppermute | solution.py:352
  639.0 102.0 %collective-permute-start.47 = (bf16[2,160,1792]{2,1,0:T(8,128)(2,1)}, bf16[2,160,1792]{2,1,0:T(8,128)(2,1)}, u32[]{:S(2)}, u32[]{:S(2)}) collective-permute-start(bf16[2,160,1792]{2,1,0:T(8,128)(2,1)} %slice.422), channel_id=1, source_target_pairs={{0,8},{1,9},{2,10},{3,11},{4,12},{5,13},{6,14},{7,15},{8,0},{9,1},... | collective-permute-start | bytes 3440648 | tf_op jit(solution)/shard_map/ppermute | solution.py:352
  642.5 28.4 %collective-permute-start.51 = (bf16[2,160,1792]{2,1,0:T(8,128)(2,1)}, bf16[2,160,1792]{2,1,0:T(8,128)(2,1)S(1)}, u32[]{:S(2)}, u32[]{:S(2)}) collective-permute-start(bf16[2,160,1792]{2,1,0:T(8,128)(2,1)} %get-tuple-element.100), channel_id=1, source_target_pairs={{0,16},{1,17},{2,18},{3,19},{4,20},{5,21},{6,22},{7,23},{8,24},{9,... | collective-permute-start | bytes 3440648 | tf_op jit(solution)/shard_map/ppermute | solution.py:352
  645.2 104.5 %collective-permute-start.50 = (bf16[2,160,1792]{2,1,0:T(8,128)(2,1)}, bf16[2,160,1792]{2,1,0:T(8,128)(2,1)}, u32[]{:S(2)}, u32[]{:S(2)}) collective-permute-start(bf16[2,160,1792]{2,1,0:T(8,128)(2,1)} %slice.426), channel_id=1, source_target_pairs={{0,16},{1,17},{2,18},{3,19},{4,20},{5,21},{6,22},{7,23},{8,24},{9,... | collective-permute-start | bytes 3440648 | tf_op jit(solution)/shard_map/ppermute | solution.py:352
  691.9 24.3 %collective-permute-start.27 = (bf16[160,640]{1,0:T(8,128)(2,1)}, bf16[160,640]{1,0:T(8,128)(2,1)}, u32[]{:S(2)}, u32[]{:S(2)}) collective-permute-start(bf16[160,640]{1,0:T(8,128)(2,1)} %get-tuple-element.107), channel_id=1, source_target_pairs={{0,8},{1,9},{2,10},{3,11},{4,12},{5,13},{6,14},{7,15},{8,0},{9,1},... | collective-permute-start | bytes 614408 | tf_op jit(solution)/shard_map/ppermute | solution.py:352
  692.1 25.6 %collective-permute-start.31 = (bf16[160,640]{1,0:T(8,128)(2,1)}, bf16[160,640]{1,0:T(8,128)(2,1)}, u32[]{:S(2)}, u32[]{:S(2)}) collective-permute-start(bf16[160,640]{1,0:T(8,128)(2,1)} %get-tuple-element.109), channel_id=1, source_target_pairs={{0,16},{1,17},{2,18},{3,19},{4,20},{5,21},{6,22},{7,23},{8,24},{9,... | collective-permute-start | bytes 614408 | tf_op jit(solution)/shard_map/ppermute | solution.py:352
  716.2 35.4 %collective-permute-start.49 = (bf16[2,160,1792]{2,1,0:T(8,128)(2,1)}, bf16[2,160,1792]{2,1,0:T(8,128)(2,1)S(1)}, u32[]{:S(2)}, u32[]{:S(2)}) collective-permute-start(bf16[2,160,1792]{2,1,0:T(8,128)(2,1)} %add_convert_fusion.3), channel_id=1, source_target_pairs={{0,16},{1,17},{2,18},{3,19},{4,20},{5,21},{6,22},{7,23},{8,24},{9,... | collective-permute-start | bytes 3440648 | tf_op jit(solution)/shard_map/ppermute | solution.py:352
  717.7 33.9 %collective-permute-start.52 = (bf16[2,160,1792]{2,1,0:T(8,128)(2,1)}, bf16[2,160,1792]{2,1,0:T(8,128)(2,1)S(1)}, u32[]{:S(2)}, u32[]{:S(2)}) collective-permute-start(bf16[2,160,1792]{2,1,0:T(8,128)(2,1)} %add_convert_fusion.2), channel_id=1, source_target_pairs={{0,8},{1,9},{2,10},{3,11},{4,12},{5,13},{6,14},{7,15},{8,0},{9,1},... | collective-permute-start | bytes 3440648 | tf_op jit(solution)/shard_map/ppermute | solution.py:352
  (127 other events, 1467.5 us)

commit v3 on v2

--- a/solution.py
+++ b/solution.py
@@ -331,9 +331,9 @@
 
 
 PAIR_OF = {0: 0, 2: 1, 4: 2, 6: 3, 3: 4}
-AXES = ("batch", "expert")
 F32 = jnp.float32
 LOW = jnp.bfloat16
+COST = 10**9
 
 
 def low(values):
@@ -342,116 +342,6 @@
 
 def dot(left, right, dims=((1,), (0,))):
     return lax.dot_general(left, right, (dims, ((), ())), preferred_element_type=F32)
-
-
-def swap(values, batch_bit, expert_bit=0, only=range(8)):
-    pairs = [
-        (b * 8 + e, (b ^ batch_bit) * 8 + (e ^ expert_bit)) for b in range(4) for e in range(8)
-    ]
-    pairs = [pair for pair in pairs if pair[0] % 8 in only]
-    return lax.ppermute(values, AXES, pairs)
-
-
-def halves(values, axis):
-    size = values.shape[axis] // 2
-    return (
-        lax.slice_in_dim(values, 0, size, axis=axis),
-        lax.slice_in_dim(values, size, 2 * size, axis=axis),
-    )
-
-
-def gather_near(piece):
-    return piece, swap(piece, 1), swap(piece, 2)
-
-
-def gather_far(near, axis, cut):
-    b = lax.axis_index("batch")
-    piece, from_x, from_y = near
-    far_a = swap(halves(from_x, cut)[0], 2)
-    far_b = swap(halves(from_y, cut)[1], 1)
-    far = jnp.concatenate([far_a, far_b], axis=cut)
-    rows = piece.shape[axis]
-    shape = list(piece.shape)
-    shape[axis] = 4 * rows
-    whole = jnp.zeros(shape, piece.dtype)
-    for bit, part in enumerate((piece, from_x, from_y, far)):
-        whole = lax.dynamic_update_slice_in_dim(whole, part, (b ^ bit) * rows, axis)
-    return whole
-
-
-def after(values, *earlier):
-    return lax.optimization_barrier((values, *earlier))[0]
-
-
-def scatter_batch(whole, axis, cut):
-    b = lax.axis_index("batch")
-    rows = whole.shape[axis] // 4
-
-    def block(bit):
-        return lax.dynamic_slice_in_dim(whole, (b ^ bit) * rows, rows, axis)
-
-    own_a, own_b = halves(block(0), cut)
-    x_a, x_b = halves(block(1), cut)
-    y_a, y_b = halves(block(2), cut)
-    far_a, far_b = halves(block(3), cut)
-    got_own_a = swap(low(x_a), 1).astype(F32)
-    got_y_a = swap(low(far_a), 1).astype(F32)
-    got_own_b = swap(low(y_b), 2).astype(F32)
-    got_x_b = swap(low(far_b), 2).astype(F32)
-    last_a = swap(low(y_a.astype(F32) + got_y_a), 2).astype(F32)
-    last_b = swap(low(x_b.astype(F32) + got_x_b), 1).astype(F32)
-    return jnp.concatenate(
-        [own_a.astype(F32) + got_own_a + last_a, own_b.astype(F32) + got_own_b + last_b], axis=cut
-    )
-
-
-def z_shift(values, steps):
-    pairs = [
-        (b * 8 + e, b * 8 + (e + 2 * steps) % 8) for b in range(4) for e in range(8)
-    ]
-    return lax.ppermute(values, AXES, pairs)
-
-
-def gather_z(block):
-    z = lax.axis_index("expert") // 2
-    whole = jnp.zeros((4, *block.shape), block.dtype)
-    whole = lax.dynamic_update_index_in_dim(whole, block, z, 0)
-    for steps in (1, 2, 3):
-        part = z_shift(block, steps)
-        whole = lax.dynamic_update_index_in_dim(whole, part, lax.rem(z + 4 - steps, 4), 0)
-    return whole
-
-
-def gather_pack(block):
-    core = lax.rem(lax.axis_index("expert"), 2)
-    mine = gather_z(block)
-    other = swap(mine, 0, 1)
-    first = jnp.where(core == 0, mine, other)
-    second = jnp.where(core == 0, other, mine)
-    return jnp.stack([first, second], axis=1).reshape(8, *block.shape)
-
-
-def scatter_z(blocks):
-    z = lax.axis_index("expert") // 2
-    total = lax.dynamic_index_in_dim(blocks, z, 0, False).astype(F32)
-    for steps in (1, 2, 3):
-        block = lax.dynamic_index_in_dim(blocks, lax.rem(z + steps, 4), 0, False)
-        total = total + z_shift(low(block), steps).astype(F32)
-    return total
-
-
-def scatter_pack(blocks):
-    core = lax.rem(lax.axis_index("expert"), 2)
-    pairs = blocks.reshape(4, 2, *blocks.shape[1:])
-    away = lax.dynamic_index_in_dim(pairs, 1 - core, 1, False)
-    mine = lax.dynamic_index_in_dim(pairs, core, 1, False)
-    return scatter_z(mine.astype(F32) + swap(low(away), 0, 1).astype(F32))
-
-
-def total_all(values):
-    for batch_bit, expert_bit in ((0, 1), (1, 0), (2, 0), (0, 2), (0, 4)):
-        values = values + swap(values, batch_bit, expert_bit)
-    return values
 
 
 MESH_ID = pl.DeviceIdType.MESH
@@ -468,23 +358,6 @@
     for device in devices:
         pl.semaphore_signal(barrier, inc=1, device_id=device, device_id_type=MESH_ID)
     pl.semaphore_wait(barrier, len(devices))
-
-
-def greet_line():
-    b, e, z, core = place()
-    barrier = pltpu.get_barrier_semaphore()
-    pl.semaphore_signal(barrier, inc=1, device_id=(b, e ^ 1), device_id_type=MESH_ID)
-
-    @pl.when(z > 0)
-    def _():
-        pl.semaphore_signal(barrier, inc=1, device_id=(b, e - 2), device_id_type=MESH_ID)
-
-    @pl.when(z < 3)
-    def _():
-        pl.semaphore_signal(barrier, inc=1, device_id=(b, e + 2), device_id_type=MESH_ID)
-
-    ends = jnp.where((z == 0) | (z == 3), 1, 0)
-    pl.semaphore_wait(barrier, 3 - ends)
 
 
 def pack_mates():
@@ -585,7 +458,7 @@
 SCATTER_SEMS = [pltpu.SemaphoreType.DMA((3,))] * 4 + [pltpu.SemaphoreType.DMA((4,))] * 2
 
 
-def line_scatter(
+def line_sum_stages(
     part,
     from_core,
     up_out,
@@ -631,12 +504,15 @@
     def chip_sum(target):
         return part[2 * target + core].astype(F32) + from_core[target].astype(F32)
 
-    for target in (3, 0, 2, 1):
-        to_core(target).start()
-    for target in range(4):
-        to_core(target).wait()
-    for step in range(3):
+    def start():
+        for target in (3, 0, 2, 1):
+            to_core(target).start()
+
+    def advance(step):
         top = 3 - step
+        if step == 0:
+            for target in range(4):
+                to_core(target).wait()
 
         @pl.when(z < top)
         def _():
@@ -664,56 +540,222 @@
 
             down(step).start()
 
-    @pl.when(z == 0)
-    def _():
-        up_in[0] = jnp.zeros_like(up_in[0])
-
-    @pl.when(z == 3)
-    def _():
-        down_in[0] = jnp.zeros_like(down_in[0])
-
-    last_up = lax.rem(3 - z, 3)
-    last_down = lax.rem(z, 3)
-
-    @pl.when(z > 0)
-    def _():
-        up(last_up).wait_recv()
-
-    @pl.when(z < 3)
-    def _():
-        down(last_down).wait_recv()
-
-    total = chip_sum(z) + up_in[last_up].astype(F32) + down_in[last_down].astype(F32)
-    for step in range(3):
-
-        @pl.when(z < 3 - step)
+    def finish():
+        @pl.when(z == 0)
         def _():
-            up(step).wait_send()
-
-        @pl.when(z > step)
+            up_in[0] = jnp.zeros_like(up_in[0])
+
+        @pl.when(z == 3)
         def _():
-            down(step).wait_send()
-
-    return total
-
-
-def kernel_call(body, outs, args, scratch, collective_id):
-    vmem = pl.BlockSpec(memory_space=pltpu.VMEM)
+            down_in[0] = jnp.zeros_like(down_in[0])
+
+        last_up = lax.rem(3 - z, 3)
+        last_down = lax.rem(z, 3)
+
+        @pl.when(z > 0)
+        def _():
+            up(last_up).wait_recv()
+
+        @pl.when(z < 3)
+        def _():
+            down(last_down).wait_recv()
+
+        total = chip_sum(z) + up_in[last_up].astype(F32) + down_in[last_down].astype(F32)
+        for step in range(3):
+
+            @pl.when(z < 3 - step)
+            def _():
+                up(step).wait_send()
+
+            @pl.when(z > step)
+            def _():
+                down(step).wait_send()
+
+        return total
+
+    return [start] + [functools.partial(advance, i) for i in range(3)] + [finish]
+
+
+def sum_into(out, *terms):
+    if len(out.shape) == 2:
+
+        @pl.loop(0, out.shape[0] // 16)
+        def _(i):
+            here = pl.ds(pl.multiple_of(i * 16, 16), 16)
+            total = terms[0][here, :].astype(F32)
+            for term in terms[1:]:
+                total = total + term[here, :].astype(F32)
+            out[here, :] = total.astype(out.dtype)
+
+    else:
+        for i in range(out.shape[0]):
+            total = terms[0][i].astype(F32)
+            for term in terms[1:]:
+                total = total + term[i].astype(F32)
+            out[i] = total.astype(out.dtype)
+
+
+REDUCE_COUNT = 8
+
+
+def reduce_scratch(half_shape, far=False):
+    kept = (4, *half_shape) if far else (1, 8, 128)
+    return [
+        pltpu.VMEM((6, *half_shape), LOW),
+        pltpu.VMEM((2, *half_shape), LOW),
+        pltpu.VMEM(kept, LOW if far else F32),
+    ] + [pltpu.SemaphoreType.DMA((size,)) for size in (3, 3, 3, 3, 4)]
+
+
+def reduce_stages(
+    block, out, received, sums, kept, x_send, x_recv, y_send, y_recv, local_sem
+):
+    b, e, _, _ = place()
+    x_device, y_device = (b ^ 1, e), (b ^ 2, e)
+
+    def over_x(slot):
+        src = (block(b ^ 3, 0), block(b ^ 1, 0), sums.at[1])[slot]
+        return send(src, received.at[slot], x_send.at[slot], x_recv.at[slot], x_device)
+
+    def over_y(slot):
+        src = (block(b ^ 3, 1), block(b ^ 2, 1), sums.at[0])[slot]
+        return send(src, received.at[3 + slot], y_send.at[slot], y_recv.at[slot], y_device)
+
+    far = kept.shape[0] == 4
+
+    def mine(i):
+        return (block(b ^ 2, 0), block(b ^ 1, 1), block(b, 0), block(b, 1))[i]
+
+    def keep(i):
+        return pltpu.make_async_copy(mine(i), kept.at[i], local_sem.at[i])
+
+    def held(i):
+        if not far:
+            return mine(i)
+        keep(i).wait()
+        return kept.at[i]
+
+    def start():
+        for slot in range(2):
+            over_x(slot).start()
+            over_y(slot).start()
+        for i in range(4 if far else 0):
+            keep(i).start()
+
+    def forward():
+        over_x(0).wait_recv()
+        sum_into(sums.at[0], held(0), received.at[0])
+        over_y(2).start()
+        over_y(0).wait_recv()
+        sum_into(sums.at[1], held(1), received.at[3])
+        over_x(2).start()
+
+    def finish():
+        for slot in (1, 2):
+            over_x(slot).wait_recv()
+            over_y(slot).wait_recv()
+        sum_into(out(0), held(2), received.at[1], received.at[5])
+        sum_into(out(1), held(3), received.at[4], received.at[2])
+        for slot in range(3):
+            over_x(slot).wait_send()
+            over_y(slot).wait_send()
+
+    return start, forward, finish
+
+
+def reduce_rows(term, out, scratch):
+    half_rows = out.shape[0] // 2
+
+    def block(owner, half):
+        return term.at[pl.ds((2 * owner + half) * half_rows, half_rows)]
+
+    def out_half(half):
+        return out.at[pl.ds(half * half_rows, half_rows)]
+
+    return reduce_stages(block, out_half, *scratch)
+
+
+def kernel_call(body, outs, args, scratch, collective_id, far_outs=(), far_args=()):
+    near = pl.BlockSpec(memory_space=pltpu.VMEM)
+    far = pl.BlockSpec(memory_space=pl.ANY)
     return pl.pallas_call(
         body,
+        cost_estimate=pl.CostEstimate(flops=COST, bytes_accessed=COST, transcendentals=0),
         out_shape=[jax.ShapeDtypeStruct(shape, dtype) for shape, dtype in outs],
-        in_specs=[vmem] * len(args),
-        out_specs=[vmem] * len(outs),
+        in_specs=[far if i in far_args else near for i in range(len(args))],
+        out_specs=[far if i in far_outs else near for i in range(len(outs))],
         scratch_shapes=scratch,
         compiler_params=pltpu.CompilerParams(
-            collective_id=collective_id, has_side_effects=True, vmem_limit_bytes=48 * 2**20
+            collective_id=collective_id, has_side_effects=True, vmem_limit_bytes=56 * 2**20
         ),
     )(*args)
 
 
+SPREAD_SEMS = [pltpu.SemaphoreType.DMA((2,))] + [pltpu.SemaphoreType.DMA((3,))] * 4
+
+
+def spread_stages(own, whole, local_sem, x_send, x_recv, y_send, y_recv):
+    b, e, _, _ = place()
+    x_device, y_device = (b ^ 1, e), (b ^ 2, e)
+
+    def over_x(slot):
+        src, dst = (
+            (own(0), whole(b, 0)),
+            (own(1), whole(b, 1)),
+            (whole(b ^ 2, 1), whole(b ^ 2, 1)),
+        )[slot]
+        return send(src, dst, x_send.at[slot], x_recv.at[slot], x_device)
+
+    def over_y(slot):
+        src, dst = (
+            (own(1), whole(b, 1)),
+            (own(0), whole(b, 0)),
+            (whole(b ^ 1, 0), whole(b ^ 1, 0)),
+        )[slot]
+        return send(src, dst, y_send.at[slot], y_recv.at[slot], y_device)
+
+    def keep(half):
+        return pltpu.make_async_copy(own(half), whole(b, half), local_sem.at[half])
+
+    def start():
+        for slot in range(2):
+            over_x(slot).start()
+            over_y(slot).start()
+        for half in range(2):
+            keep(half).start()
+
+    def forward():
+        over_x(0).wait_recv()
+        over_y(2).start()
+        over_y(0).wait_recv()
+        over_x(2).start()
+    def finish():
+        for slot in range(3):
+            for over in (over_x, over_y):
+                if slot > 0:
+                    over(slot).wait_recv()
+                over(slot).wait_send()
+        for half in range(2):
+            keep(half).wait()
+
+    return start, forward, finish
+
+
+def spread_rows(own_ref, whole_ref, rows, sems):
+    half_rows = rows // 2
+
+    def own(half):
+        return own_ref.at[pl.ds(half * half_rows, half_rows)]
+
+    def whole(owner, half):
+        return whole_ref.at[pl.ds(owner * rows + half * half_rows, half_rows)]
+
+    return spread_stages(own, whole, *sems)
+
+
 def opening_kernel(
-    rows, small, marks, columns, w_out, n1_all, gains, small_all, marks_all, columns_all, out_all,
-    *sems,
+    rows, small, marks, columns, w_out, up_own, n1_all, gains, small_all, marks_all, columns_all,
+    out_all, up_all, *sems,
 ):
     (
         b_send, b_recv, s_send, s_recv, m_send, m_recv, c_send, c_recv,
@@ -722,11 +764,14 @@
     b, e, z, core = place()
     over = [(b ^ bit, e) for bit in (1, 2, 3)]
     mates = pack_mates()
+    up_start, up_forward, up_finish = spread_rows(
+        up_own.at[0], up_all, up_own.shape[1], sems[18:23]
+    )
     greet(over + mates)
     small_all[e, b] = small[...]
     marks_all[e] = marks[...]
     columns_all[b, e] = columns[e]
-    out_all[core, b, z] = w_out[...]
+    out_all[b, z, core] = w_out[...]
     first = []
     for i, device in enumerate(over):
         first.append(send(small, small_all.at[e, b], b_send.at[i], b_recv.at[i], device))
@@ -741,13 +786,14 @@
     for i in range(3):
         device = (b, lax.rem(e + 2 * i + 2, 8))
         along.append(
-            send(w_out, out_all.at[core, b, z], z_send.at[i], z_recv.at[i], device)
+            send(w_out, out_all.at[b, z, core], z_send.at[i], z_recv.at[i], device)
         )
         along[-1].start()
     rest = []
     for i, device in enumerate(mates):
         rest.append(send(marks, marks_all.at[e], m_send.at[i], m_recv.at[i], device))
         rest[-1].start()
+    up_start()
     values = rows[...]
     inv = lax.rsqrt(jnp.mean(values * values, axis=1, keepdims=True) + EPSILON)
     for copy in first:
@@ -771,7 +817,7 @@
         spread_out = dot(low(pieces), spread)
         gains[i : i + 1, :] = jnp.sum(jnp.where(mine, spread_out, 0.0), axis=0, keepdims=True)
     n1_all[e] = low(values * inv * gains[0:1, :])
-    stages = line_stages(n1_all, *sems[18:])
+    stages = line_stages(n1_all, *sems[23:])
     stages[0]()
 
     def hop(owner, half, sems_out, sems_in, slot, device):
@@ -787,7 +833,7 @@
         return hop(owner, half, y_send, y_recv, slot, over[1])
 
     def out_block(owner):
-        return out_all.at[core, owner]
+        return out_all.at[owner, :, core]
 
     for copy in across:
         copy.wait()
@@ -812,6 +858,7 @@
     over_y(0).wait_recv()
     over_x(2).start()
     stages[2]()
+    up_forward()
     stages[3]()
     for i, copy in enumerate(beyond):
         copy.wait()
@@ -826,9 +873,10 @@
         copy.wait()
     for slot in range(4):
         out_pair(slot).wait()
-
-
-def opening(rows, small, marks, columns, w_out):
+    up_finish()
+
+
+def opening(rows, small, marks, columns, w_out, up_own):
     tokens, width = rows.shape
     sizes = (3, 3, 7, 7, 7, 7, 7, 7, 3, 3, 3, 3, 3, 3, 3, 3, 4, 4)
     return kernel_call(
@@ -839,11 +887,14 @@
             ((8, 4, 8, 128), F32),
             ((8, 8, 128), F32),
             ((4, *columns.shape), LOW),
-            ((2, 4, 4, *w_out.shape), LOW),
+            ((4, 4, 2, *w_out.shape), LOW),
+            ((4 * up_own.shape[1], up_own.shape[2]), LOW),
         ],
-        (rows, small, marks, columns, w_out),
-        [pltpu.SemaphoreType.DMA((size,)) for size in sizes] + GATHER_SEMS,
+        (rows, small, marks, columns, w_out, up_own),
+        [pltpu.SemaphoreType.DMA((size,)) for size in sizes] + SPREAD_SEMS + GATHER_SEMS,
         0,
+        far_outs=(6,),
+        far_args=(5,),
     )
 
 
@@ -851,12 +902,80 @@
     return (lax.rem(e, 2) == 0) | (e == 3), jnp.where(e == 3, 4, e // 2)
 
 
+BLOCK = 256
+
+
+def turned(values, cosine, sine):
+    return values * cosine + pltpu.roll(values, HEAD // 2, 1) * sine
+
+
 def middle_kernel(
-    attended, w_out, rows, gain, attn, resid, n2_all, a_send, a_recv, *sems
+    n1, weights, cosine, sine, ids_row, ids_column, w_out, rows, gain, cot, up_own, down_own, sdown_own,
+    qkv, logsum, attn, resid, n2_all, cot_all, up_all, down_all, sdown_all,
+    attended, a_send, a_recv, *sems,
 ):
     b, e, z, core = place()
-    greet(pack_mates())
+    tokens = rows.shape[0]
+    mates = pack_mates()
+    count = len(SPREAD_SEMS)
+    spreads = [
+        spread_rows(up_own.at[1], up_all, up_own.shape[1], sems[:count]),
+        spread_rows(down_own.at[0], down_all.at[0], down_own.shape[1], sems[count : 2 * count]),
+        spread_rows(down_own.at[1], down_all.at[1], down_own.shape[1], sems[2 * count : 3 * count]),
+        spread_rows(sdown_own, sdown_all, sdown_own.shape[0], sems[3 * count : 4 * count]),
+    ]
+    sems = sems[4 * count :]
+    cot_stages = line_stages(cot_all, *sems[: len(GATHER_SEMS)])
+    n2_stages = line_stages(n2_all, *sems[len(GATHER_SEMS) :])
+    greet([(b ^ 1, e), (b ^ 2, e), *mates])
+    cot_all[e] = cot[...]
+    for start, _, _ in spreads:
+        start()
+    cot_stages[0]()
     holds, pair = holder(e)
+
+    @pl.when(jnp.logical_not(holds))
+    def _():
+        qkv[...] = jnp.zeros_like(qkv)
+        logsum[...] = jnp.zeros_like(logsum)
+
+    @pl.when(holds)
+    def _():
+        @pl.loop(0, n1.shape[0] // BLOCK)
+        def _(i):
+            here = pl.ds(pl.multiple_of(i * BLOCK, BLOCK), BLOCK)
+            projected = dot(n1[here, :], weights[:, : 6 * HEAD])
+            cos_here, sin_here = cosine[here, :], sine[here, :]
+            for part in range(6):
+                piece = projected[:, part * HEAD : (part + 1) * HEAD]
+                if part < 4:
+                    piece = turned(piece, cos_here, sin_here)
+                qkv[part, here, :] = low(piece)
+
+    cot_stages[1]()
+    for head in range(2):
+
+        @pl.when(holds)
+        def _():
+            for i in range(n1.shape[0] // BLOCK):
+                here = pl.ds(i * BLOCK, BLOCK)
+                keys = (i + 1) * BLOCK
+                scores = dot(qkv[head, here, :], qkv[2 + head, :keys, :], ((1,), (1,)))
+                scores = jnp.where(
+                    allowed_here(ids_column, ids_row, i, keys), scores * HEAD ** (-0.5), NEGATIVE
+                )
+                top = jnp.max(scores, axis=1, keepdims=True)
+                weight = jnp.exp(scores - top)
+                total = jnp.sum(weight, axis=1, keepdims=True)
+                out = dot(low(weight / total), qkv[4 + head, :keys, :])
+                logsum[head, here, :] = jnp.broadcast_to(top + jnp.log(total), (BLOCK, HEAD))
+                for j in range(BLOCK // tokens):
+                    attended[i * (BLOCK // tokens) + j, :, head * HEAD : (head + 1) * HEAD] = low(
+                        out[j * tokens : (j + 1) * tokens]
+                    )
+
+        cot_stages[2 + head]()
+        spreads[head][1]()
 
     def give(i):
         other = lax.rem(e + i, 8)
@@ -883,51 +1002,86 @@
     resid[...] = total
     inv = lax.rsqrt(jnp.mean(total * total, axis=1, keepdims=True) + EPSILON)
     n2_all[e] = low(total * inv * gain[...])
-    line_gather(n2_all, *sems)
+    n2_stages[0]()
+    spreads[2][1]()
+    spreads[3][1]()
+    for stage in n2_stages[1:]:
+        stage()
+    cot_stages[4]()
 
     @pl.when(holds)
     def _():
         for i in range(1, 8):
             give(i).wait_send()
 
-
-def middle(attended, w_out, rows, gain):
+    for _, _, finish in spreads:
+        finish()
+
+
+def allowed_here(ids_column, ids_row, i, keys):
+    query = i * BLOCK + lax.broadcasted_iota(jnp.int32, (BLOCK, keys), 0)
+    key = lax.broadcasted_iota(jnp.int32, (BLOCK, keys), 1)
+    same = ids_column[i * BLOCK : (i + 1) * BLOCK, :] == ids_row[:, :keys]
+    return (key <= query) & same
+
+
+def middle(n1, weights, cosine, sine, ids_row, ids_column, w_out, rows, gain, cot, up_own, down_own, sdown_own):
     tokens, width = rows.shape
-    pair = attended.shape[2]
+    length = n1.shape[0]
+    pair = 2 * HEAD
+    count = len(PAIR_OF)
     return kernel_call(
         middle_kernel,
         [
-            ((width // pair, tokens, pair), LOW),
+            ((6, length, HEAD), LOW),
+            ((2, length, HEAD), F32),
+            ((count, tokens, pair), LOW),
             ((tokens, width), F32),
             ((8, tokens, width), LOW),
+            ((8, tokens, width), LOW),
+            ((4 * up_own.shape[1], up_own.shape[2]), LOW),
+            ((2, 4 * down_own.shape[1], width), LOW),
+            ((4 * sdown_own.shape[0], width), LOW),
         ],
-        (attended, w_out, rows, gain),
-        [pltpu.SemaphoreType.DMA((7,)), pltpu.SemaphoreType.DMA((len(PAIR_OF),))] + GATHER_SEMS,
+        (n1, weights, cosine, sine, ids_row, ids_column, w_out, rows, gain, cot, up_own, down_own, sdown_own),
+        [
+            pltpu.VMEM((8, tokens, pair), LOW),
+            pltpu.SemaphoreType.DMA((7,)),
+            pltpu.SemaphoreType.DMA((count,)),
+        ]
+        + SPREAD_SEMS * 4
+        + GATHER_SEMS * 2,
         1,
+        far_outs=(6, 7, 8),
+        far_args=(10, 11, 12),
     )
 
 
 def turn_kernel(
-    part,
-    upstream,
-    gates,
-    w_router,
-    resid,
-    gain,
-    w_out,
-    dresid,
-    dlogits,
-    gain_term,
-    darrived,
-    dattn,
-    a_send,
-    a_recv,
-    *scratch,
+    part, out_part, upstream, gates, w_router, resid, gain, w_out, up_term, down_term,
+    dresid, dlogits, gain_term, darrived, output_rows, up_grad, down_grad,
+    dattn, a_send, a_recv, *scratch,
 ):
     b, e, z, core = place()
-    greet(pack_mates())
+    greet([(b ^ 1, e), (b ^ 2, e), *pack_mates()])
+    reduces = [
+        reduce_rows(up_term, up_grad, scratch[:REDUCE_COUNT]),
+        reduce_rows(down_term, down_grad, scratch[REDUCE_COUNT : 2 * REDUCE_COUNT]),
+    ]
+    scratch = scratch[2 * REDUCE_COUNT :]
+    count = len(scratch) // 2
+    row_stages = line_sum_stages(part, *scratch[:count])
+    out_stages = line_sum_stages(out_part, *scratch[count:])
+    row_stages[0]()
+    for start, _, _ in reduces:
+        start()
     holds, pair = holder(e)
-    total = line_scatter(part, *scratch)
+    row_stages[1]()
+    out_stages[0]()
+    row_stages[2]()
+    reduces[0][1]()
+    row_stages[3]()
+    total = row_stages[4]()
     width = upstream.shape[1]
     experts = gates.shape[1]
     dgate = total[:, width : width + experts] + total[:, width + experts : width + 2 * experts]
@@ -955,6 +1109,11 @@
         def _():
             give(source, index).start()
 
+    out_stages[1]()
+    reduces[1][1]()
+    out_stages[2]()
+    out_stages[3]()
+
     @pl.when(jnp.logical_not(holds))
     def _():
         darrived[...] = jnp.zeros_like(darrived)
@@ -967,6 +1126,9 @@
             block = darrived.at[other]
             send(block, block, a_send.at[0], a_recv.at[other], (b, other)).wait_recv()
 
+    output_rows[...] = resid[...] + out_stages[4]()
+    for _, _, finish in reduces:
+        finish()
     for source, index in PAIR_OF.items():
 
         @pl.when(e != source)
@@ -974,10 +1136,11 @@
             give(source, index).wait_send()
 
 
-def turn(part, upstream, gates, w_router, resid, gain, w_out):
+def turn(part, out_part, upstream, gates, w_router, resid, gain, w_out, up_term, down_term):
     tokens, width = upstream.shape
     pair = 2 * HEAD
     count = len(PAIR_OF)
+    up_rows, down_rows = up_term.shape[0] // 4, down_term.shape[0] // 4
     return kernel_call(
         turn_kernel,
         [
@@ -985,43 +1148,276 @@
             (gates.shape, LOW),
             ((1, width), F32),
             ((8, tokens, pair), LOW),
+            ((tokens, width), F32),
+            ((up_rows, up_term.shape[1]), F32),
+            ((down_rows, down_term.shape[1]), F32),
         ],
-        (part, upstream, gates, w_router, resid, gain, w_out),
+        (part, out_part, upstream, gates, w_router, resid, gain, w_out, up_term, down_term),
         [
             pltpu.VMEM((count, tokens, pair), LOW),
             pltpu.SemaphoreType.DMA((count,)),
             pltpu.SemaphoreType.DMA((8,)),
         ]
+        + reduce_scratch((up_rows // 2, up_term.shape[1]), True)
+        + reduce_scratch((down_rows // 2, down_term.shape[1]), True)
         + scatter_scratch(tokens, part.shape[2])
+        + SCATTER_SEMS
+        + scatter_scratch(tokens, width)
         + SCATTER_SEMS,
         2,
-    )
-
-
-def closing_kernel(part, rows, gain, dresid, input_grad, *scratch):
-    greet_line()
+        far_args=(8, 9),
+    )
+
+
+PARTNERS = ((0, 1), (1, 0), (2, 0), (0, 2), (0, 4))
+
+
+def closing_kernel(
+    dattn, qkv, logsum, n1, weights, cosine, sine, ids_row, ids_column, rows, gain, dresid,
+    up_term, down_term, sdown_term, sup_term, out_term, small,
+    input_grad, columns, out_grad, up_grad, down_grad, sdown_grad, small_sum,
+    dkey, dvalue, dprojected, part, column_term, column_sum, column_low,
+    out_near, out_sum, out_low, out_half, out_got, small_got, small_step,
+    n_send, n_recv, o_send, o_recv, c_send, c_recv, s_send, s_recv, *scratch,
+):
+    b, e, z, core = place()
+    length = n1.shape[0]
+    tokens = rows.shape[0]
+    mates = pack_mates()
+    greet([(b ^ 1, e), (b ^ 2, e), *mates])
+    holds, pair = holder(e)
+
+    def cut():
+        nonlocal scratch
+        mine, scratch = scratch[:REDUCE_COUNT], scratch[REDUCE_COUNT:]
+        return mine
+
+    up = reduce_rows(up_term, up_grad, cut())
+    down = reduce_rows(down_term, down_grad, cut())
+    sdown = reduce_rows(sdown_term, sdown_grad, cut())
+    column = reduce_rows(column_term, column_sum, cut())
+    out = reduce_stages(
+        lambda owner, half: out_sum.at[owner, pl.ds(2 * half, 2)],
+        lambda half: out_half.at[pl.ds(2 * half, 2)],
+        *cut(),
+    )
+    stages = line_sum_stages(part, *scratch)
+
+    def partner(i):
+        batch_bit, expert_bit = PARTNERS[i]
+        src = small if i == 0 else small_step.at[i - 1]
+        device = (b ^ batch_bit, e ^ expert_bit)
+        return send(src, small_got.at[i], s_send.at[i], s_recv.at[i], device)
+
+    def small_round(i):
+        partner(i).wait_recv()
+        before = small[...] if i == 0 else small_step[i - 1]
+        if i < len(PARTNERS) - 1:
+            small_step[i] = before + small_got[i]
+            partner(i + 1).start()
+        else:
+            small_sum[...] = before + small_got[i]
+
+    near = send(
+        out_term.at[:, :, 1 - core], out_near, n_send.at[0], n_recv.at[0], (b, e ^ 1)
+    )
+    near.start()
+    own = pltpu.make_async_copy(out_term.at[:, :, core], out_sum, n_send.at[1])
+    own.start()
+    partner(0).start()
+    up[0]()
+    down[0]()
+    sdown[0]()
+
+    def attend(head):
+        dkey[...] = jnp.zeros_like(dkey)
+        dvalue[...] = jnp.zeros_like(dvalue)
+        lanes = pl.ds(head * HEAD, HEAD)
+        for i in range(length // BLOCK):
+            here = pl.ds(i * BLOCK, BLOCK)
+            keys = (i + 1) * BLOCK
+            count = BLOCK // tokens
+            back = jnp.concatenate(
+                [dattn[count * i + j, :, lanes] for j in range(count)], axis=0
+            )
+            query = qkv[head, here, :]
+            scores = dot(query, qkv[2 + head, :keys, :], ((1,), (1,))) * HEAD ** (-0.5)
+            weight = jnp.where(
+                allowed_here(ids_column, ids_row, i, keys),
+                jnp.exp(scores - logsum[head, here, 0:1]),
+                0.0,
+            )
+            dprob = dot(back, qkv[4 + head, :keys, :], ((1,), (1,)))
+            delta = jnp.sum(weight * dprob, axis=1, keepdims=True)
+            dscore = low(weight * (dprob - delta))
+            dquery = dot(dscore, qkv[2 + head, :keys, :]) * HEAD ** (-0.5)
+            dkey[:keys, :] += dot(dscore, query, ((0,), (0,)))
+            dvalue[:keys, :] += dot(low(weight), back, ((0,), (0,)))
+            dprojected[here, lanes] = low(turned(dquery, cosine[here, :], -sine[here, :]))
+        dprojected[:, (2 + head) * HEAD : (3 + head) * HEAD] = low(
+            turned(dkey[...] * HEAD ** (-0.5), cosine[...], -sine[...])
+        )
+        dprojected[:, (4 + head) * HEAD : (5 + head) * HEAD] = low(dvalue[...])
+
+    @pl.when(holds)
+    def _():
+        attend(0)
+
+    near.wait()
+    own.wait()
+    for owner in range(4):
+        for owner_z in range(4):
+            out_sum[owner, owner_z] = low(
+                out_sum[owner, owner_z].astype(F32) + out_near[owner, owner_z].astype(F32)
+            )
+    out[0]()
+    small_round(0)
+    up[1]()
+
+    @pl.when(holds)
+    def _():
+        attend(1)
+        for i in range(8):
+            part[i] = low(
+                dot(
+                    dprojected[i * tokens : (i + 1) * tokens, :],
+                    weights[:, : 6 * HEAD],
+                    ((1,), (1,)),
+                )
+            )
+
+    @pl.when(jnp.logical_not(holds))
+    def _():
+        part[...] = jnp.zeros_like(part)
+
+    stages[0]()
+    column_term[:, 6 * HEAD :] = sup_term[...]
+
+    @pl.when(holds)
+    def _():
+        for i in range(n1.shape[1] // BLOCK):
+            here = pl.ds(i * BLOCK, BLOCK)
+            column_term[here, : 6 * HEAD] = low(dot(n1[:, here], dprojected[...], ((0,), (0,))))
+
+    @pl.when(jnp.logical_not(holds))
+    def _():
+        column_term[:, : 6 * HEAD] = jnp.zeros((n1.shape[1], 6 * HEAD), LOW)
+
+    column[0]()
+    stages[1]()
+    small_round(1)
+    down[1]()
+    sdown[1]()
+    stages[2]()
+    small_round(2)
+    out[1]()
+    stages[3]()
+    small_round(3)
     values = rows[...]
     inv = lax.rsqrt(jnp.mean(values * values, axis=1, keepdims=True) + EPSILON)
     xhat = values * inv
-    scaled = line_scatter(part, *scratch) * gain[...]
+    scaled = stages[4]() * gain[...]
     input_grad[...] = dresid[...] + inv * (
         scaled - xhat * jnp.mean(scaled * xhat, axis=1, keepdims=True)
     )
-
-
-def closing(part, rows, gain, dresid):
+    column[1]()
+    out[2]()
+    for owner_z in range(4):
+        out_low[owner_z] = low(out_half[owner_z])
+    along = []
+    for i in range(3):
+        device = (b, lax.rem(e + 2 * i + 2, 8))
+        along.append(
+            send(
+                out_low.at[device[1] // 2], out_got.at[i], o_send.at[i], o_recv.at[i], device
+            )
+        )
+        along[-1].start()
+    small_round(4)
+    for i in range(len(PARTNERS)):
+        partner(i).wait_send()
+    up[2]()
+    down[2]()
+    sdown[2]()
+    for copy in along:
+        copy.wait()
+    out_grad[...] = (
+        out_half[z]
+        + out_got[0].astype(F32)
+        + out_got[1].astype(F32)
+        + out_got[2].astype(F32)
+    )
+    column[2]()
+    piece = column_low.shape[1]
+    for i in range(0, 8, 2):
+        two = column_sum[i * piece : (i + 2) * piece, :].astype(F32)
+        column_low[i] = low(two[:piece])
+        column_low[i + 1] = low(two[piece:])
+    columns[e] = column_low[e]
+    across = []
+    for i, device in enumerate(mates):
+        across.append(
+            send(column_low.at[device[1]], columns.at[e], c_send.at[i], c_recv.at[i], device)
+        )
+        across[-1].start()
+    for copy in across:
+        copy.wait()
+
+
+def closing(
+    dattn, qkv, logsum, n1, weights, cosine, sine, ids_row, ids_column, rows, gain, dresid,
+    up_term, down_term, sdown_term, sup_term, out_term, small,
+):
     tokens, width = rows.shape
+    length = n1.shape[0]
+    rows_w = out_term.shape[3]
+    wide = weights.shape[1]
+    up_rows, down_rows, sdown_rows = (
+        term.shape[0] // 4 for term in (up_term, down_term, sdown_term)
+    )
+    dma = pltpu.SemaphoreType.DMA
     return kernel_call(
         closing_kernel,
-        [((tokens, width), F32)],
-        (part, rows, gain, dresid),
-        scatter_scratch(tokens, width) + SCATTER_SEMS,
+        [
+            ((tokens, width), F32),
+            ((8, rows_w, wide), LOW),
+            ((rows_w, width), F32),
+            ((up_rows, up_term.shape[1]), F32),
+            ((down_rows, width), F32),
+            ((sdown_rows, width), F32),
+            (small.shape, F32),
+        ],
+        (
+            dattn, qkv, logsum, n1, weights, cosine, sine, ids_row, ids_column, rows, gain, dresid,
+            up_term, down_term, sdown_term, sup_term, out_term, small,
+        ),
+        [
+            pltpu.VMEM((length, HEAD), F32),
+            pltpu.VMEM((length, HEAD), F32),
+            pltpu.VMEM((length, 6 * HEAD), LOW),
+            pltpu.VMEM((8, tokens, width), LOW),
+            pltpu.VMEM((width, wide), LOW),
+            pltpu.VMEM((width // 4, wide), LOW),
+            pltpu.VMEM((8, rows_w, wide), LOW),
+            pltpu.VMEM((4, 4, rows_w, width), LOW),
+            pltpu.VMEM((4, 4, rows_w, width), LOW),
+            pltpu.VMEM((4, rows_w, width), LOW),
+            pltpu.VMEM((4, rows_w, width), F32),
+            pltpu.VMEM((3, rows_w, width), LOW),
+            pltpu.VMEM((5, *small.shape), F32),
+            pltpu.VMEM((4, *small.shape), F32),
+            dma((2,)), dma((1,)), dma((3,)), dma((3,)), dma((7,)), dma((7,)), dma((5,)), dma((5,)),
+        ]
+        + reduce_scratch((up_rows // 2, up_term.shape[1]), True)
+        + reduce_scratch((down_rows // 2, width), True)
+        + reduce_scratch((sdown_rows // 2, width))
+        + reduce_scratch((width // 8, wide))
+        + reduce_scratch((2, rows_w, width))
+        + scatter_scratch(tokens, width)
+        + SCATTER_SEMS,
         3,
-    )[0]
-
-
-def exchange(values):
-    return lax.all_to_all(values, "expert", split_axis=0, concat_axis=0, tiled=True)
+        far_args=(12, 13, 16),
+    )
 
 
 def silu_parts(gate, up):
@@ -1056,22 +1452,19 @@
     hidden = expert_up.shape[2] // 2
     experts = expert_up.shape[0] * 8
     s_rows = shared_down.shape[0]
-    s_own = 4 * s_rows
-    s_pad = -(-s_own // 128) * 128
-    scale = HEAD ** (-0.5)
+    s_each = -(-s_rows // 32) * 32
+    s_pad = 4 * s_each
 
     qkv_low = low(qkv_weight).reshape(rows_w, 3, pairs_of_heads, pair)
     nothing = jnp.zeros((rows_w, 3, pair), LOW)
     columns = [qkv_low[:, :, PAIR_OF[i]] if i in PAIR_OF else nothing for i in range(8)]
     columns = jnp.stack(columns).reshape(8, rows_w, 3 * pair)
-    sup_low = low(shared_up).reshape(rows_w, 2, 4, 8, s_rows).transpose(3, 0, 1, 2, 4)
-    sup_low = jnp.pad(
-        sup_low.reshape(8, rows_w, 2, s_own), ((0, 0), (0, 0), (0, 0), (0, s_pad - s_own))
-    )
+    sup_low = low(shared_up).reshape(rows_w, 2, 4, 8, s_rows)
+    sup_low = jnp.pad(sup_low, ((0, 0),) * 4 + ((0, s_each - s_rows),)).transpose(3, 0, 1, 2, 4)
     columns = jnp.concatenate([columns, sup_low.reshape(8, rows_w, 2 * s_pad)], axis=2)
-    up_near = gather_near(low(expert_up))
-    down_near = gather_near(low(expert_down))
-    sdown_near = gather_near(low(shared_down))
+    up_own = low(expert_up)
+    down_own = low(expert_down)
+    sdown_own = jnp.pad(low(shared_down), ((0, s_each - s_rows), (0, 0)))
     core = lax.rem(e, 2)
 
     small = jnp.concatenate(
@@ -1085,14 +1478,14 @@
     small = low(small).astype(F32)
     marks = jnp.concatenate([routes[0].T, seq_ids], axis=0).astype(F32)
     marks = jnp.pad(marks, ((0, 7 - TOP), (0, 0)))
-    n1_all, gains, small, marks, columns, w_out = opening(
-        rows_in, small, marks, columns, low(out_weight)
+    n1_all, gains, small, marks, columns, w_out, up_first = opening(
+        rows_in, small, marks, columns, low(out_weight), up_own
     )
     n1_all = n1_all.reshape(length, width)
     columns = columns.reshape(width, 3 * pair + 2 * s_pad)
     w_qkv = columns[:, : 3 * pair]
     w_sup = columns[:, 3 * pair :]
-    w_out = w_out.transpose(1, 2, 0, 3, 4).reshape(width, width)
+    w_out = w_out.reshape(width, width)
     router_rows = rows_w * experts // 128
     w_router = low(small[:, :, :router_rows].transpose(1, 0, 2, 3).reshape(width, experts))
     gain_first = gains[0:1]
@@ -1100,34 +1493,34 @@
     marks = marks.astype(jnp.int32).transpose(0, 2, 1).reshape(length, 8)
     route_all = marks[:, :TOP]
     ids_all = marks[:, TOP]
-    cot_all = gather_pack(after(low(upstream), n1_all)).reshape(length, width)
-
     positions = jnp.arange(length, dtype=jnp.int32)
-    projected = dot(n1_all, w_qkv)
-    queries = low(rotate(projected[:, :pair].reshape(length, 2, HEAD), positions, 1.0))
-    keys = low(rotate(projected[:, pair : 2 * pair].reshape(length, 2, HEAD), positions, 1.0))
-    values = low(projected[:, 2 * pair :].reshape(length, 2, HEAD))
-    allowed = (positions[None, :] <= positions[:, None]) & (ids_all[None, :] == ids_all[:, None])
-    scores = jnp.einsum("qhd,khd->hqk", queries, keys, preferred_element_type=F32) * scale
-    scores = jnp.where(allowed[None], scores, NEGATIVE)
-    top = jnp.max(scores, axis=2, keepdims=True)
-    attn_p = jnp.exp(scores - top)
-    total = jnp.sum(attn_p, axis=2, keepdims=True)
-    attn_p = attn_p / total
-    attn_low = low(attn_p)
-    attended = jnp.einsum("hqk,khd->qhd", attn_low, values, preferred_element_type=F32)
-    attended_low = low(attended)
-    up_low = gather_far(after(up_near, attended_low), 1, 1)
-    attn, resid, n2_all = middle(
-        attended_low.reshape(8, tokens, pair), w_out, rows_in, gain_second
-    )
+    ids_row = ids_all[None, :]
+    ids_column = ids_all[:, None]
+    frequency = 10000.0 ** (-jnp.arange(HEAD // 2, dtype=jnp.float32) / (HEAD // 2))
+    angle = positions.astype(F32)[:, None] * frequency[None, :]
+    cosine = jnp.concatenate([jnp.cos(angle)] * 2, axis=1)
+    sine = jnp.concatenate([-jnp.sin(angle), jnp.sin(angle)], axis=1)
+    qkv, logsum, attn, resid, n2_all, cot_all, up_second, down_low, w_sdown = middle(
+        n1_all,
+        columns,
+        cosine,
+        sine,
+        ids_row,
+        ids_column,
+        w_out,
+        rows_in,
+        gain_second,
+        low(upstream),
+        up_own,
+        down_own,
+        sdown_own,
+    )
+    up_low = (up_first, up_second)
     attn = attn.transpose(1, 0, 2).reshape(tokens, width)
+    cot_all = cot_all.reshape(length, width)
 
     n2 = lax.dynamic_index_in_dim(n2_all, e, 0, False)
     n2_all = n2_all.reshape(length, width)
-    down_low = gather_far(after(down_near, n2_all), 1, 1)
-    w_sdown = gather_far(after(sdown_near, n2_all), 0, 1)
-    w_sdown = jnp.pad(w_sdown, ((0, s_pad - s_own), (0, 0)))
     logits = dot(n2_all, w_router)
     hot = route_all[:, :, None] == jnp.arange(experts, dtype=jnp.int32)[None, None, :]
     routed_to = jnp.any(hot, axis=1)
@@ -1160,72 +1553,67 @@
     hid_low = low(silu * pre[:, s_pad:])
     back = dot(cot_all, w_sdown, ((1,), (1,)))
     output_part = output_part + dot(hid_low, w_sdown)
-    sdown_term = dot(hid_low, cot_all, ((0,), (0,)))[:s_own]
+    sdown_term = dot(hid_low, cot_all, ((0,), (0,)))
     dpre = low(jnp.concatenate([back * slope, back * silu], axis=1))
     sup_term = dot(n2_all, dpre, ((0,), (0,)))
     drow_part = drow_part + dot(dpre, w_sup, ((1,), (1,)))
-    expert_up_grad = scatter_batch(low(jnp.stack(up_terms)), 1, 1)
-    expert_down_grad = scatter_batch(low(jnp.stack(down_terms)), 1, 1)
-    shared_down_grad = scatter_batch(low(sdown_term), 0, 1)
-
     lane = jnp.arange(experts, dtype=jnp.int32)[None, :] - 2 * e
     dgate = jnp.where(lane == 0, dgates[0], 0.0) + jnp.where(lane == 1, dgates[1], 0.0)
     dgate_high = low(dgate)
     dgate_rest = low(dgate - dgate_high.astype(F32))
     spare = jnp.zeros((length, 128 - 2 * experts), LOW)
     part = jnp.concatenate([low(drow_part), dgate_high, dgate_rest, spare], axis=1)
+    up_terms = [low(term) for term in up_terms]
+    down_terms = [low(term) for term in down_terms]
     own_gates = lax.dynamic_slice_in_dim(gates, e * tokens, tokens, 0)
-    dresid, dlogits, gain_ffn_term, dattn = turn(
+    dresid, dlogits, gain_ffn_term, dattn, output_rows, up_grad_first, down_grad_first = turn(
         part.reshape(8, tokens, part.shape[1]),
+        low(output_part).reshape(8, tokens, width),
         upstream,
         own_gates,
         w_router.T,
         resid,
         gain_second,
         w_out,
-    )
-    dattn = dattn.reshape(length, 2, HEAD)
-    output_part = after(low(output_part), dresid).reshape(8, tokens, width)
-    output_rows = resid + scatter_pack(output_part)
+        up_terms[0],
+        down_terms[0],
+    )
     router_term = dot(dlogits, n2, ((0,), (0,)))
-    small = total_all(jnp.concatenate([router_term, gain_ffn_term], axis=0))
+    small = jnp.concatenate(
+        [router_term, gain_ffn_term, jnp.zeros((7, width), F32)], axis=0
+    )
+    out_term = low(dot(attn, low(dresid), ((0,), (0,)))).reshape(4, 4, 2, rows_w, width)
+    input_grad, columns, out_grad, up_grad_second, down_grad_second, sdown_grad, small = closing(
+        dattn,
+        qkv,
+        logsum,
+        n1_all,
+        columns,
+        cosine,
+        sine,
+        ids_row,
+        ids_column,
+        rows_in,
+        gain_first,
+        dresid,
+        up_terms[1],
+        down_terms[1],
+        low(sdown_term),
+        low(sup_term),
+        out_term,
+        small,
+    )
+    expert_up_grad = jnp.stack([up_grad_first, up_grad_second])
+    expert_down_grad = jnp.stack([down_grad_first, down_grad_second])
+    shared_down_grad = sdown_grad[:s_rows]
     small = lax.dynamic_slice_in_dim(small, (b * 8 + e) * rows_w, rows_w, 1)
-    dproj = low(dresid)
-    out_term = dot(attn, dproj, ((0,), (0,))).reshape(4, 4, 2, rows_w, width)
-    out_away = swap(low(lax.dynamic_index_in_dim(out_term, 1 - core, 2, False)), 0, 1)
-    out_term = lax.dynamic_index_in_dim(out_term, core, 2, False) + out_away
-    out_term = scatter_batch(low(out_term).reshape(16 * rows_w, width), 0, 1)
-    out_grad = scatter_z(out_term.reshape(4, rows_w, width))
-
-    delta = jnp.sum(dattn.astype(F32) * attended, axis=2).T[:, :, None]
-    dprob = jnp.einsum("qhd,khd->hqk", dattn, values, preferred_element_type=F32)
-    dscore = low(attn_p * (dprob - delta))
-    dquery = jnp.einsum("hqk,khd->qhd", dscore, keys, preferred_element_type=F32)
-    dkey = jnp.einsum("hqk,qhd->khd", dscore, queries, preferred_element_type=F32)
-    dvalue = jnp.einsum("hqk,qhd->khd", attn_low, dattn, preferred_element_type=F32)
-    dprojected = low(
-        jnp.concatenate(
-            [
-                rotate(dquery * scale, positions, -1.0).reshape(length, pair),
-                rotate(dkey * scale, positions, -1.0).reshape(length, pair),
-                dvalue.reshape(length, pair),
-            ],
-            axis=1,
-        )
-    )
-    qkv_term = dot(n1_all, dprojected, ((0,), (0,)))
-    dn1 = low(dot(dprojected, w_qkv, ((1,), (1,))))
-    input_grad = closing(dn1.reshape(8, tokens, width), rows_in, gain_first, dresid)
-
-    columns = scatter_batch(low(jnp.concatenate([qkv_term, sup_term], axis=1)), 0, 0)
-    columns = exchange(low(columns).reshape(8, rows_w, 3 * pair + 2 * s_pad)).astype(F32)
+    columns = columns.astype(F32)
     qkv_grad = jnp.stack([columns[i, :, : 3 * pair] for i in PAIR_OF])
     qkv_grad = qkv_grad.reshape(pairs_of_heads, rows_w, 3, pair).transpose(1, 2, 0, 3)
     qkv_grad = qkv_grad.reshape(rows_w, 3 * width)
-    sup_grad = columns[:, :, 3 * pair :].reshape(8, rows_w, 2, s_pad)[..., :s_own]
-    sup_grad = sup_grad.reshape(8, rows_w, 2, 4, s_rows).transpose(1, 2, 3, 0, 4)
+    sup_grad = columns[:, :, 3 * pair :].reshape(8, rows_w, 2, 4, s_each)[..., :s_rows]
+    sup_grad = sup_grad.transpose(1, 2, 3, 0, 4)
     sup_grad = sup_grad.reshape(rows_w, shared_up.shape[1])
-
     own_first = low(gain_attn).astype(F32)
     gain_attn_grad = jnp.sum(low(qkv_weight).astype(F32) * qkv_grad, axis=1) / own_first
     return (

time: 768 us -> 569 us (0.74)
  the two profiles are of different devices: /device:TPU:0 before, /device:TPU:25 now
where the time goes in v3:
time: 569 us; the launch traced here: 561 us
  Pallas kernels  395 us (69%)
  matrix products  108 us (19%)
  local copies, waits for them, and re-layouts  29.6 us (5%)
  other arithmetic  26.5 us (5%)
    pallas_call x4, Pallas kernels, kernel_call(): pl.pallas_call(body, cost_estimate=pl.CostEstimate(flops=COST, bytes_acce...  395 us
    dot_general x21, matrix products, dot(): lax.dot_general(left, right, (dims, ((), ())), preferred_element_type=F32)  108 us

profile of v3, /device:TPU:25, one launch (start us, length us, event | category | flops | bytes accessed | tf_op | source)
XLA Modules:
  0.0 560.7 jit_solution(10992739337543487051)
XLA Ops:
  6.0 1.7 reshape.121
  8.9 1.5 slice_reduce_fusion
  12.5 3.9 convert_element_type.131.up_own
  16.4 89.5 %shard_map.212 = (bf16[8,128,1280]{2,1,0:T(8,128)(2,1)}, f32[2,1280]{1,0:T(2,128)}, f32[8,4,8,128]{3,2,1,0:T(8,128)}, f32[8,8,128]{2,1,0:T(8,128)}, bf16[4,8,40,...) custom-call(f32[128,1280]{1,0:T(8,128)} %bitcast.105, ...), custom_call_target="tpu_custom_call" | custom-call | flops 1000000000 | bytes 1000000000 | tf_op jit(solution)/shard_map/pallas_call | solution.py:681
  106.0 1.9 fusion.28
  109.4 1.6 fusion.47
  114.2 88.7 %shard_map.213 = (bf16[6,1024,128]{2,1,0:T(8,128)(2,1)}, f32[2,1024,128]{2,1,0:T(8,128)}, bf16[5,128,256]{2,1,0:T(8,128)(2,1)}, f32[128,1280]{1,0:T(8,128)}, bf1...) custom-call(bf16[1024,1280]{1,0:T(8,128)(2,1)} %bitcast.103, ...), custom_call_target="tpu_custom_call" | custom-call | flops 1000000000 | bytes 1000000000 | tf_op jit(solution)/shard_map/pallas_call | solution.py:681
  203.0 8.8 %fusion.50 = f32[1024,1792]{0,1:T(8,128)} fusion(bf16[1024,1280]{1,0:T(8,128)(2,1)} %bitcast.128, bf16[1280,1792]{1,0:T(8,128)(2,1)S(1)} %bitcast.141), kind=kOutput, calls=%fused_computation.133 | convolution fusion | flops 4697620480 | bytes 14548992 | tf_op jit(solution)/shard_map/dot_general | solution.py:344
  212.6 2.7 fusion.49
  215.7 1.4 fusion.22
  217.8 8.3 %multiply_convert_fusion.5 = (bf16[1024,896]{0,1:T(8,128)(2,1)S(1)}, bf16[1024,896]{0,1:T(8,128)(2,1)S(1)}, f32[1024]{0:T(1024)S(1)}, bf16[1024,896]{0,1:T(8,128)(2,1)}) fusion(f32[1024,1792]{0,1:T(8,128)} %fusion.50, f32[1024]{0:T(1024)S(1)} %get-tuple-element.72, bf16[1024,1280]{1,0:T(8,128)(2,1)S(1)} %bitcast.112, ...), kind=kOutput, calls=%fused_computation.17 | convolution fusion | flops 2366241792 | bytes 17768448 | tf_op jit(solution)/shard_map/dot_general | solution.py:344
  226.1 8.8 %fusion.3 = f32[1024,1280]{1,0:T(8,128)S(1)} fusion(bf16[1280,1792]{1,0:T(8,128)(2,1)} %get-tuple-element.50, bf16[1024,896]{0,1:T(8,128)(2,1)S(1)} %get-tuple-element.81, bf16[1024,896]{0,1:T(8,128)(2,1)S(1)} %get-tuple-element.80), kind=kOutput, calls=%fused_computation.27 | convolution fusion | flops 4704960512 | bytes 13500416 | tf_op jit(solution)/shard_map/dot_general | solution.py:344
  235.0 15.5 %fusion.51 = f32[1024,1792]{0,1:T(8,128)S(1)} fusion(bf16[1024,1280]{1,0:T(8,128)(2,1)S(1)} %bitcast.131, bf16[1280,1792]{1,0:T(8,128)(2,1)} %get-tuple-element.51), kind=kOutput, calls=%fused_computation.134 | convolution fusion | flops 4697620480 | bytes 14548992 | tf_op jit(solution)/shard_map/dot_general | solution.py:344
  250.5 5.7 %multiply_convert_fusion.3 = (bf16[1024,896]{0,1:T(8,128)(2,1)S(1)}, bf16[1024,896]{0,1:T(8,128)(2,1)}, f32[1024]{0:T(1024)S(1)}, bf16[1024,896]{0,1:T(8,128)(2,1)}) fusion(f32[1024,1792]{0,1:T(8,128)S(1)} %fusion.51, f32[1024]{0:T(1024)S(1)} %get-tuple-element.71, bf16[1024,1280]{1,0:T(8,128)(2,1)S(1)} %bitcast.113, bf16[2,896,1280]{2,1,0:T(8,128)(2,1)S(1)} %bitcast.139), kind=kOutput, calls=%fused_computation.13 | convolution fusion | flops 2366241792 | bytes 17768448 | tf_op jit(solution)/shard_map/dot_general | solution.py:344
  256.2 8.7 %fusion.2 = f32[1024,1280]{1,0:T(8,128)S(1)} fusion(bf16[1280,1792]{1,0:T(8,128)(2,1)} %get-tuple-element.51, bf16[1024,896]{0,1:T(8,128)(2,1)} %get-tuple-element.79, bf16[1024,896]{0,1:T(8,128)(2,1)S(1)} %get-tuple-element.78), kind=kOutput, calls=%fused_computation.26 | convolution fusion | flops 4704960512 | bytes 13500416 | tf_op jit(solution)/shard_map/dot_general | solution.py:344
  265.9 1.8 multiply_convert_fusion.8
  270.5 5.5 concatenate.43
  276.0 5.3 fusion.8
  281.4 4.7 fusion.4
  286.1 2.4 add_convert_fusion
  289.9 10.1 %convolution_convert_fusion.1.up_term = bf16[1280,1792]{1,0:T(8,128)(2,1)} fusion(bf16[1024,1280]{1,0:T(8,128)(2,1)} %bitcast.130, bf16[1024,896]{0,1:T(8,128)(2,1)} %copy-done.40, bf16[1024,896]{0,1:T(8,128)(2,1)} %copy-done.39), kind=kOutput, calls=%fused_computation.1 | convolution fusion | flops 4707254272 | bytes 10878976 | tf_op jit(solution)/shard_map/dot_general | solution.py:344
  300.0 4.1 convolution_convert_fusion.4.down_term
  304.1 69.8 %shard_map.214 = (f32[128,1280]{1,0:T(8,128)}, bf16[128,16]{1,0:T(8,128)(2,1)}, f32[1,1280]{1,0:T(1,128)}, bf16[8,128,256]{2,1,0:T(8,128)(2,1)}, f32[128,1280]{1...) custom-call(bf16[8,128,1408]{2,1,0:T(8,128)(2,1)} %bitcast.101, bf16[8,128,1280]{2,1,0:T(8,128)(2,1)} %bitcast.102, ...), custom_call_target="tpu_custom_call" | custom-call | flops 1000000000 | bytes 1000000000 | tf_op jit(solution)/shard_map/pallas_call | solution.py:681
  373.9 8.7 %convolution_convert_fusion.up_term = bf16[1280,1792]{1,0:T(8,128)(2,1)} fusion(bf16[1024,1280]{1,0:T(8,128)(2,1)S(1)} %bitcast.133, bf16[1024,896]{0,1:T(8,128)(2,1)} %get-tuple-element.79, bf16[1024,896]{0,1:T(8,128)(2,1)} %copy-done.38), kind=kOutput, calls=%fused_computation | convolution fusion | flops 4707254272 | bytes 10878976 | tf_op jit(solution)/shard_map/dot_general | solution.py:344
  382.7 3.9 convolution_convert_fusion.3.down_term
  388.6 1.7 convolution_convert_fusion.5.sup_term
  390.6 2.7 convolution_convert_fusion.2
  395.2 146.6 %shard_map.215 = (f32[128,1280]{1,0:T(8,128)}, bf16[8,40,1024]{2,1,0:T(8,128)(2,1)}, f32[40,1280]{1,0:T(8,128)}, f32[320,1792]{1,0:T(8,128)}, f32[224,1280]{1,0:...) custom-call(bf16[8,128,256]{2,1,0:T(8,128)(2,1)} %get-tuple-element.55.dattn, ...), custom_call_target="tpu_custom_call" | custom-call | flops 1000000000 | bytes 1000000000 | tf_op jit(solution)/shard_map/pallas_call | solution.py:681
  545.8 1.6 reshape.136
  547.4 1.4 dynamic-slice_bitcast_fusion
  550.8 4.9 pad_maximum_fusion
  555.7 1.5 pad_maximum_fusion.7
  (173 shorter events, 33.4 us)
Async XLA Ops:
  0.6 7.9 %copy-start.6 = (f32[40,3840]{1,0:T(8,128)S(1)}, f32[40,3840]{1,0:T(8,128)}, u32[]{:S(2)}) copy-start(f32[40,3840]{1,0:T(8,128)} %param.17) | copy-start | bytes 1843204
  8.5 3.4 copy-start.23
  105.9 3.3 copy-start.31
  106.0 5.1 copy-start.33
  106.0 5.7 %copy-start.1 = (f32[1,128,1280]{2,1,0:T(8,128)S(1)}, f32[1,128,1280]{2,1,0:T(8,128)}, u32[]{:S(2)}) copy-start(f32[1,128,1280]{2,1,0:T(8,128)} %param.16) | copy-start | bytes 1966084
  107.9 4.5 copy-start.8
  109.4 4.1 copy-start.26
  113.5 89.4 %slice-start.2 = ((s8[4587520]{0:T(1024)(128)(4,1)}), s8[4194304]{0:T(1024)(128)(4,1)S(1)}, s32[]{:S(2)}) async-start(s8[4587520]{0:T(1024)(128)(4,1)} %bitcast.140), calls=%async_computation.2 | async-start | bytes 8388608
  114.2 88.7 %slice-start.3 = ((s8[4587520]{0:T(1024)(128)(4,1)}), s8[393216]{0:T(1024)(128)(4,1)S(1)}, s32[]{:S(2)}) async-start(s8[4587520]{0:T(1024)(128)(4,1)} %bitcast.140), calls=%async_computation.3 | async-start | bytes 786432
  203.0 9.3 %copy-start.30 = (f32[8,4,8,128]{3,2,1,0:T(8,128)S(1)}, f32[8,4,8,128]{3,2,1,0:T(8,128)}, u32[]{:S(2)}) copy-start(f32[8,4,8,128]{3,2,1,0:T(8,128)} %get-tuple-element.49) | copy-start | bytes 393220
  212.3 3.0 copy-start.10
  226.1 8.8 %copy-start.39 = (bf16[1024,896]{0,1:T(8,128)(2,1)}, bf16[1024,896]{0,1:T(8,128)(2,1)S(1)}, u32[]{:S(2)}) copy-start(bf16[1024,896]{0,1:T(8,128)(2,1)S(1)} %get-tuple-element.80) | copy-start | bytes 5505028
  226.1 8.8 %copy-start.40 = (bf16[1024,896]{0,1:T(8,128)(2,1)}, bf16[1024,896]{0,1:T(8,128)(2,1)S(1)}, u32[]{:S(2)}) copy-start(bf16[1024,896]{0,1:T(8,128)(2,1)S(1)} %get-tuple-element.81) | copy-start | bytes 5505028
  226.1 8.8 %copy-start.27 = (bf16[8,128,1280]{2,1,0:T(8,128)(2,1)S(1)}, bf16[8,128,1280]{2,1,0:T(8,128)(2,1)}, u32[]{:S(2)}) copy-start(bf16[8,128,1280]{2,1,0:T(8,128)(2,1)} %get-tuple-element.48) | copy-start | bytes 7864324
  226.1 24.4 %slice-start = ((s8[4587520]{0:T(1024)(128)(4,1)}), s8[4194304]{0:T(1024)(128)(4,1)S(1)}, s32[]{:S(2)}) async-start(s8[4587520]{0:T(1024)(128)(4,1)} %bitcast.138), calls=%async_computation | async-start | bytes 8388608
  234.9 15.6 %slice-start.1 = ((s8[4587520]{0:T(1024)(128)(4,1)}), s8[393216]{0:T(1024)(128)(4,1)S(1)}, s32[]{:S(2)}) async-start(s8[4587520]{0:T(1024)(128)(4,1)} %bitcast.138), calls=%async_computation.1 | async-start | bytes 786432
  256.2 8.7 %copy-start.38 = (bf16[1024,896]{0,1:T(8,128)(2,1)}, bf16[1024,896]{0,1:T(8,128)(2,1)S(1)}, u32[]{:S(2)}) copy-start(bf16[1024,896]{0,1:T(8,128)(2,1)S(1)} %get-tuple-element.78) | copy-start | bytes 5505028
  256.2 8.7 %copy-start = (bf16[4,8,40,1024]{3,2,1,0:T(8,128)(2,1)S(1)}, bf16[4,8,40,1024]{3,2,1,0:T(8,128)(2,1)}, u32[]{:S(2)}) copy-start(bf16[4,8,40,1024]{3,2,1,0:T(8,128)(2,1)} %get-tuple-element.42) | copy-start | bytes 7864324
  276.0 5.3 copy-start.36
  281.3 4.7 copy-start.13
  281.4 4.7 copy-start.18
  289.9 10.1 %copy-start.4 = (bf16[8,128,1280]{2,1,0:T(8,128)(2,1)S(1)}, bf16[8,128,1280]{2,1,0:T(8,128)(2,1)}, u32[]{:S(2)}) copy-start(bf16[8,128,1280]{2,1,0:T(8,128)(2,1)} %get-tuple-element.46) | copy-start | bytes 7864324
  289.9 10.1 %copy-start.37 = (bf16[1024,896]{0,1:T(8,128)(2,1)S(1)}, bf16[1024,896]{0,1:T(8,128)(2,1)}, u32[]{:S(2)}) copy-start(bf16[1024,896]{0,1:T(8,128)(2,1)} %get-tuple-element.85) | copy-start | bytes 5505028
  304.1 69.8 %copy-start.28 = (bf16[8,128,1280]{2,1,0:T(8,128)(2,1)S(1)}, bf16[8,128,1280]{2,1,0:T(8,128)(2,1)}, u32[]{:S(2)}) copy-start(bf16[8,128,1280]{2,1,0:T(8,128)(2,1)} %get-tuple-element.48) | copy-start | bytes 7864324
  390.3 2.9 copy-start.32
  390.4 4.1 copy-start.34
  544.1 4.7 copy-start.5
  545.1 3.7 copy-start.7
  545.1 3.9 copy-start.35
  550.8 4.9 copy-start.11
  550.8 4.9 copy-start.12
  555.7 3.2 copy-start.24
  (13 other events, 21.1 us)

commit v4 on v3

--- a/solution.py
+++ b/solution.py
@@ -2,6 +2,7 @@
 
 import jax
 import jax.numpy as jnp
+import numpy as np
 from jax import lax
 from jax.experimental import pallas as pl
 from jax.experimental.pallas import tpu as pltpu
@@ -353,6 +354,23 @@
     return b, e, e // 2, lax.rem(e, 2)
 
 
+def greet_line():
+    b, e, z, core = place()
+    barrier = pltpu.get_barrier_semaphore()
+    pl.semaphore_signal(barrier, inc=1, device_id=(b, e ^ 1), device_id_type=MESH_ID)
+
+    @pl.when(z > 0)
+    def _():
+        pl.semaphore_signal(barrier, inc=1, device_id=(b, e - 2), device_id_type=MESH_ID)
+
+    @pl.when(z < 3)
+    def _():
+        pl.semaphore_signal(barrier, inc=1, device_id=(b, e + 2), device_id_type=MESH_ID)
+
+    ends = jnp.where((z == 0) | (z == 3), 1, 0)
+    pl.semaphore_wait(barrier, 3 - ends)
+
+
 def greet(devices):
     barrier = pltpu.get_barrier_semaphore()
     for device in devices:
@@ -508,37 +526,57 @@
         for target in (3, 0, 2, 1):
             to_core(target).start()
 
-    def advance(step):
-        top = 3 - step
-        if step == 0:
-            for target in range(4):
-                to_core(target).wait()
-
-        @pl.when(z < top)
-        def _():
-            @pl.when(z > 0)
-            def _():
-                up(step).wait_recv()
-                up_out[step] = low(chip_sum(top) + up_in[step].astype(F32))
-
-            @pl.when(z == 0)
-            def _():
-                up_out[step] = low(chip_sum(top))
-
-            up(step).start()
-
-        @pl.when(z > step)
-        def _():
-            @pl.when(z < 3)
-            def _():
-                down(step).wait_recv()
-                down_out[step] = low(chip_sum(step) + down_in[step].astype(F32))
-
-            @pl.when(z == 3)
-            def _():
-                down_out[step] = low(chip_sum(step))
-
-            down(step).start()
+    def send_up(step):
+        up_out[step] = low(chip_sum(3 - step))
+        up(step).start()
+
+    def send_down(step):
+        down_out[step] = low(chip_sum(step))
+        down(step).start()
+
+    def pass_up(step):
+        up(step).wait_recv()
+        up_out[step] = low(chip_sum(3 - step) + up_in[step].astype(F32))
+        up(step).start()
+
+    def pass_down(step):
+        down(step).wait_recv()
+        down_out[step] = low(chip_sum(step) + down_in[step].astype(F32))
+        down(step).start()
+
+    def ends():
+        for target in range(4):
+            to_core(target).wait()
+
+        @pl.when(z == 0)
+        def _():
+            for step in range(3):
+                send_up(step)
+
+        @pl.when(z == 3)
+        def _():
+            for step in range(3):
+                send_down(step)
+
+    def near():
+        @pl.when(z == 1)
+        def _():
+            pass_up(0)
+
+        @pl.when(z == 2)
+        def _():
+            pass_down(0)
+
+    def far():
+        @pl.when(z == 1)
+        def _():
+            pass_up(1)
+            pass_down(0)
+
+        @pl.when(z == 2)
+        def _():
+            pass_down(1)
+            pass_up(0)
 
     def finish():
         @pl.when(z == 0)
@@ -573,7 +611,7 @@
 
         return total
 
-    return [start] + [functools.partial(advance, i) for i in range(3)] + [finish]
+    return [start, ends, near, far, finish]
 
 
 def sum_into(out, *terms):
@@ -636,17 +674,18 @@
         return kept.at[i]
 
     def start():
-        for slot in range(2):
-            over_x(slot).start()
-            over_y(slot).start()
+        over_x(0).start()
+        over_y(0).start()
         for i in range(4 if far else 0):
             keep(i).start()
 
     def forward():
         over_x(0).wait_recv()
+        over_x(1).start()
         sum_into(sums.at[0], held(0), received.at[0])
         over_y(2).start()
         over_y(0).wait_recv()
+        over_y(1).start()
         sum_into(sums.at[1], held(1), received.at[3])
         over_x(2).start()
 
@@ -718,17 +757,18 @@
         return pltpu.make_async_copy(own(half), whole(b, half), local_sem.at[half])
 
     def start():
-        for slot in range(2):
-            over_x(slot).start()
-            over_y(slot).start()
+        over_x(0).start()
+        over_y(0).start()
         for half in range(2):
             keep(half).start()
 
     def forward():
         over_x(0).wait_recv()
         over_y(2).start()
+        over_x(1).start()
         over_y(0).wait_recv()
         over_x(2).start()
+        over_y(1).start()
     def finish():
         for slot in range(3):
             for over in (over_x, over_y):
@@ -754,8 +794,9 @@
 
 
 def opening_kernel(
-    rows, small, marks, columns, w_out, up_own, n1_all, gains, small_all, marks_all, columns_all,
-    out_all, up_all, *sems,
+    rows, router, first_gain, second_gain, routes, ids, qkv, sup, out_weight, up_weight,
+    n1_all, gains, small_all, marks_all, columns_all, out_all, up_all,
+    small, marks, columns, w_out, up_own, up_wide, up_sem, *sems,
 ):
     (
         b_send, b_recv, s_send, s_recv, m_send, m_recv, c_send, c_recv,
@@ -764,10 +805,35 @@
     b, e, z, core = place()
     over = [(b ^ bit, e) for bit in (1, 2, 3)]
     mates = pack_mates()
-    up_start, up_forward, up_finish = spread_rows(
-        up_own.at[0], up_all, up_own.shape[1], sems[18:23]
-    )
+    up_start, up_forward, up_finish = spread_rows(up_own, up_all, up_own.shape[0], sems[18:23])
+    bring = pltpu.make_async_copy(up_weight.at[0], up_wide, up_sem.at[0])
+    bring.start()
     greet(over + mates)
+    bring.wait()
+    up_own[...] = low(up_wide[...])
+    up_start()
+    rows_w = router.shape[0]
+    small[...] = jnp.zeros_like(small)
+    small[:rows_w] = router[...]
+    small[rows_w : rows_w + 1, : first_gain.shape[1]] = first_gain[...]
+    small[rows_w + 1 : rows_w + 2, : second_gain.shape[1]] = second_gain[...]
+    chosen = routes[0].astype(F32)
+    chosen = jnp.concatenate([chosen, jnp.zeros((128, 128 - TOP), F32)], axis=1).T
+    marks[...] = jnp.concatenate(
+        [chosen[:TOP], ids[...].astype(F32), jnp.zeros((7 - TOP, 128), F32)], axis=0
+    )
+    pair = 2 * HEAD
+    width = rows.shape[1]
+    for i in range(8):
+        for part in range(3):
+            lanes = slice(part * pair, (part + 1) * pair)
+            if i in PAIR_OF:
+                start = part * width + PAIR_OF[i] * pair
+                columns[i, :, lanes] = low(qkv[:, start : start + pair])
+            else:
+                columns[i, :, lanes] = jnp.zeros((columns.shape[1], pair), LOW)
+        columns[i, :, 3 * pair :] = sup[i]
+    w_out[...] = low(out_weight[...])
     small_all[e, b] = small[...]
     marks_all[e] = marks[...]
     columns_all[b, e] = columns[e]
@@ -782,18 +848,16 @@
             send(columns.at[device[1]], columns_all.at[b, e], c_send.at[i], c_recv.at[i], device)
         )
         across[-1].start()
-    along = []
-    for i in range(3):
-        device = (b, lax.rem(e + 2 * i + 2, 8))
-        along.append(
-            send(w_out, out_all.at[b, z, core], z_send.at[i], z_recv.at[i], device)
+    beyond = []
+    for i, device in enumerate(over):
+        beyond.append(
+            send(w_out, out_all.at[b, z, core], o_send.at[i], o_recv.at[i], device)
         )
-        along[-1].start()
+        beyond[-1].start()
     rest = []
     for i, device in enumerate(mates):
         rest.append(send(marks, marks_all.at[e], m_send.at[i], m_recv.at[i], device))
         rest[-1].start()
-    up_start()
     values = rows[...]
     inv = lax.rsqrt(jnp.mean(values * values, axis=1, keepdims=True) + EPSILON)
     for copy in first:
@@ -805,7 +869,6 @@
     for copy in second:
         copy.wait()
 
-    width = rows.shape[1]
     piece = width // 32
     lane = lax.broadcasted_iota(jnp.int32, (128, width), 1)
     spread = low(jnp.where(lax.rem(lane, piece) == lax.broadcasted_iota(jnp.int32, (128, width), 0), 1.0, 0.0))
@@ -832,35 +895,36 @@
         owner, half = ((b, 1), (b, 0), (b ^ 1, 0))[slot]
         return hop(owner, half, y_send, y_recv, slot, over[1])
 
-    def out_block(owner):
-        return out_all.at[owner, :, core]
+    def out_block(owner_z):
+        return out_all.at[:, owner_z, core]
+
+    def out_pair(slot):
+        block = out_block(lax.rem(z + 4 - slot, 4))
+        return send(block, block, p_send.at[slot], p_recv.at[slot], (b, e ^ 1))
 
     for copy in across:
         copy.wait()
-    for slot in range(2):
-        over_x(slot).start()
-        over_y(slot).start()
-    for copy in along:
-        copy.wait()
-    beyond = []
-    for i, device in enumerate(over):
-        beyond.append(send(out_block(b), out_block(b), o_send.at[i], o_recv.at[i], device))
-        beyond[-1].start()
-
-    def out_pair(slot):
-        block = out_block(b ^ slot)
-        return send(block, block, p_send.at[slot], p_recv.at[slot], (b, e ^ 1))
-
-    out_pair(0).start()
+    over_x(0).start()
+    over_y(0).start()
+    up_forward()
+    over_x(1).start()
+    over_y(1).start()
     stages[1]()
     over_x(0).wait_recv()
     over_y(2).start()
     over_y(0).wait_recv()
     over_x(2).start()
     stages[2]()
-    up_forward()
+    for copy in beyond:
+        copy.wait()
+    along = []
+    for i in range(3):
+        device = (b, lax.rem(e + 2 * i + 2, 8))
+        along.append(send(out_block(z), out_block(z), z_send.at[i], z_recv.at[i], device))
+        along[-1].start()
+    out_pair(0).start()
     stages[3]()
-    for i, copy in enumerate(beyond):
+    for i, copy in enumerate(along):
         copy.wait()
         out_pair(i + 1).start()
     stages[4]()
@@ -876,8 +940,11 @@
     up_finish()
 
 
-def opening(rows, small, marks, columns, w_out, up_own):
+def opening(rows, router, first_gain, second_gain, routes, ids, qkv, sup, out_weight, up_weight):
     tokens, width = rows.shape
+    _, up_rows, up_width = up_weight.shape
+    rows_w = out_weight.shape[0]
+    wide = 6 * HEAD + sup.shape[2]
     sizes = (3, 3, 7, 7, 7, 7, 7, 7, 3, 3, 3, 3, 3, 3, 3, 3, 4, 4)
     return kernel_call(
         opening_kernel,
@@ -886,15 +953,26 @@
             ((2, width), F32),
             ((8, 4, 8, 128), F32),
             ((8, 8, 128), F32),
-            ((4, *columns.shape), LOW),
-            ((4, 4, 2, *w_out.shape), LOW),
-            ((4 * up_own.shape[1], up_own.shape[2]), LOW),
+            ((4, 8, rows_w, wide), LOW),
+            ((4, 4, 2, rows_w, width), LOW),
+            ((4 * up_rows, up_width), LOW),
         ],
-        (rows, small, marks, columns, w_out, up_own),
-        [pltpu.SemaphoreType.DMA((size,)) for size in sizes] + SPREAD_SEMS + GATHER_SEMS,
+        (rows, router, first_gain, second_gain, routes, ids, qkv, sup, out_weight, up_weight),
+        [
+            pltpu.VMEM((8, 128), F32),
+            pltpu.VMEM((8, 128), F32),
+            pltpu.VMEM((8, rows_w, wide), LOW),
+            pltpu.VMEM((rows_w, width), LOW),
+            pltpu.VMEM((up_rows, up_width), LOW),
+            pltpu.VMEM((up_rows, up_width), F32),
+            pltpu.SemaphoreType.DMA((1,)),
+        ]
+        + [pltpu.SemaphoreType.DMA((size,)) for size in sizes]
+        + SPREAD_SEMS
+        + GATHER_SEMS,
         0,
         far_outs=(6,),
-        far_args=(5,),
+        far_args=(9,),
     )
 
 
@@ -910,16 +988,16 @@
 
 
 def middle_kernel(
-    n1, weights, cosine, sine, ids_row, ids_column, w_out, rows, gain, cot, up_own, down_own, sdown_own,
+    n1, weights, cosine, sine, ids_row, ids_column, w_out, rows, gain, cot, up_weight, down_weight, sdown_weight,
     qkv, logsum, attn, resid, n2_all, cot_all, up_all, down_all, sdown_all,
-    attended, a_send, a_recv, *sems,
+    attended, up_own, up_wide, down_own, sdown_own, up_sem, a_send, a_recv, *sems,
 ):
     b, e, z, core = place()
     tokens = rows.shape[0]
     mates = pack_mates()
     count = len(SPREAD_SEMS)
     spreads = [
-        spread_rows(up_own.at[1], up_all, up_own.shape[1], sems[:count]),
+        spread_rows(up_own, up_all, up_own.shape[0], sems[:count]),
         spread_rows(down_own.at[0], down_all.at[0], down_own.shape[1], sems[count : 2 * count]),
         spread_rows(down_own.at[1], down_all.at[1], down_own.shape[1], sems[2 * count : 3 * count]),
         spread_rows(sdown_own, sdown_all, sdown_own.shape[0], sems[3 * count : 4 * count]),
@@ -927,11 +1005,21 @@
     sems = sems[4 * count :]
     cot_stages = line_stages(cot_all, *sems[: len(GATHER_SEMS)])
     n2_stages = line_stages(n2_all, *sems[len(GATHER_SEMS) :])
+    cot_all[e] = low(cot[0])
+    bring = pltpu.make_async_copy(up_weight.at[1], up_wide, up_sem.at[0])
+    bring.start()
     greet([(b ^ 1, e), (b ^ 2, e), *mates])
-    cot_all[e] = cot[...]
-    for start, _, _ in spreads:
+    bring.wait()
+    up_own[...] = low(up_wide[...])
+    spreads[0][0]()
+    cot_stages[0]()
+    down_own[...] = low(down_weight[...])
+    short = sdown_own.shape[0] - sdown_weight.shape[0]
+    sdown_own[...] = low(
+        jnp.concatenate([sdown_weight[...], jnp.zeros((short, cot.shape[2]), F32)], axis=0)
+    )
+    for start, _, _ in spreads[1:]:
         start()
-    cot_stages[0]()
     holds, pair = holder(e)
 
     @pl.when(jnp.logical_not(holds))
@@ -1025,11 +1113,14 @@
     return (key <= query) & same
 
 
-def middle(n1, weights, cosine, sine, ids_row, ids_column, w_out, rows, gain, cot, up_own, down_own, sdown_own):
+def middle(n1, weights, cosine, sine, ids_row, ids_column, w_out, rows, gain, cot, up_weight, down_weight, sdown_weight):
     tokens, width = rows.shape
     length = n1.shape[0]
     pair = 2 * HEAD
     count = len(PAIR_OF)
+    _, up_rows, up_width = up_weight.shape
+    down_rows = down_weight.shape[1]
+    sdown_rows = -(-sdown_weight.shape[0] // 32) * 32
     return kernel_call(
         middle_kernel,
         [
@@ -1039,13 +1130,18 @@
             ((tokens, width), F32),
             ((8, tokens, width), LOW),
             ((8, tokens, width), LOW),
-            ((4 * up_own.shape[1], up_own.shape[2]), LOW),
-            ((2, 4 * down_own.shape[1], width), LOW),
-            ((4 * sdown_own.shape[0], width), LOW),
+            ((4 * up_rows, up_width), LOW),
+            ((2, 4 * down_rows, width), LOW),
+            ((4 * sdown_rows, width), LOW),
         ],
-        (n1, weights, cosine, sine, ids_row, ids_column, w_out, rows, gain, cot, up_own, down_own, sdown_own),
+        (n1, weights, cosine, sine, ids_row, ids_column, w_out, rows, gain, cot, up_weight, down_weight, sdown_weight),
         [
             pltpu.VMEM((8, tokens, pair), LOW),
+            pltpu.VMEM((up_rows, up_width), LOW),
+            pltpu.VMEM((up_rows, up_width), F32),
+            pltpu.VMEM((2, down_rows, width), LOW),
+            pltpu.VMEM((sdown_rows, width), LOW),
+            pltpu.SemaphoreType.DMA((1,)),
             pltpu.SemaphoreType.DMA((7,)),
             pltpu.SemaphoreType.DMA((count,)),
         ]
@@ -1053,12 +1149,156 @@
         + GATHER_SEMS * 2,
         1,
         far_outs=(6, 7, 8),
-        far_args=(10, 11, 12),
+        far_args=(10,),
+    )
+
+
+def experts_kernel(
+    n2, cot, w_sup, w_sdown, gates, up_first, up_second, w_down,
+    out_part, row_sum, sdown_term, sup_term, up_term_first, up_term_second, down_term_first, down_term_second,
+    part, up_w, down_w, hid, dpre, hid_shared, dpre_shared, load_sem, store_sem, *scratch,
+):
+    e = lax.axis_index("expert")
+    greet_line()
+    stages = line_sum_stages(part, *scratch)
+    tokens = part.shape[1]
+    length, width = n2.shape
+    hidden = down_w.shape[1]
+    pad = w_sdown.shape[0]
+    loads = []
+    for k, up_ref in enumerate((up_first, up_second)):
+        loads.append(pltpu.make_async_copy(up_ref, up_w.at[k], load_sem.at[2 * k]))
+        loads.append(pltpu.make_async_copy(w_down.at[k], down_w.at[k], load_sem.at[2 * k + 1]))
+    for copy in loads:
+        copy.start()
+    for copy in loads:
+        copy.wait()
+    lane = lax.broadcasted_iota(jnp.int32, (ROWS, 128), 1)
+
+    @pl.loop(0, length // ROWS)
+    def _(i):
+        here = pl.ds(pl.multiple_of(i * ROWS, ROWS), ROWS)
+        x = n2[here, :]
+        c = cot[here, :]
+        marks = jnp.zeros((ROWS, 128), F32)
+        gate_part = dot(x, w_sup[:, :pad])
+        up_part = dot(x, w_sup[:, pad:])
+        back = dot(c, w_sdown[...], ((1,), (1,)))
+        silu, slope = silu_parts(gate_part, up_part)
+        hid_shared[here, :] = low(silu * up_part)
+        dpre_shared[here, :pad] = low(back * slope)
+        dpre_shared[here, pad:] = low(back * silu)
+        out = dot(hid_shared[here, :], w_sdown[...])
+        drow = dot(dpre_shared[here, :], w_sup[...], ((1,), (1,)))
+        for k in range(2):
+            gate = gates[here, k : k + 1]
+            gate_part = dot(x, up_w[k, :, :hidden])
+            up_part = dot(x, up_w[k, :, hidden:])
+            back = dot(c, down_w[k], ((1,), (1,)))
+            silu, slope = silu_parts(gate_part, up_part)
+            value = silu * up_part
+            dgate = jnp.sum(back * value, axis=1, keepdims=True)
+            hid[k, here, :] = low(value * gate)
+            back = back * gate
+            dpre[k, here, :hidden] = low(back * slope)
+            dpre[k, here, hidden:] = low(back * silu)
+            out = out + dot(hid[k, here, :], down_w[k])
+            drow = drow + dot(dpre[k, here, :], up_w[k], ((1,), (1,)))
+            high = low(dgate).astype(F32)
+            marks = jnp.where(lane == 2 * e + k, high, marks)
+            marks = jnp.where(lane == 2 * e + k + 16, dgate - high, marks)
+        out_part[here, :] = low(out)
+        for j in range(ROWS // tokens):
+            rows = slice(j * tokens, (j + 1) * tokens)
+            part[i * (ROWS // tokens) + j, :, :width] = low(drow[rows])
+            part[i * (ROWS // tokens) + j, :, width:] = low(marks[rows])
+
+    stages[0]()
+    stores = []
+    for k, (up_ref, down_ref) in enumerate(
+        ((up_term_first, down_term_first), (up_term_second, down_term_second))
+    ):
+
+        if k == 0:
+            stages[1]()
+
+        @pl.loop(0, width // COLS)
+        def _(i):
+            here = pl.ds(pl.multiple_of(i * COLS, COLS), COLS)
+            up_w[k, here, :] = low(dot(n2[:, here], dpre[k], ((0,), (0,))))
+
+        if k == 0:
+            stages[2]()
+
+        stores.append(pltpu.make_async_copy(up_w.at[k], up_ref, store_sem.at[2 * k]))
+        stores[-1].start()
+
+        @pl.loop(0, hidden // 128)
+        def _(i):
+            here = pl.ds(pl.multiple_of(i * 128, 128), 128)
+            down_w[k, here, :] = low(dot(hid[k, :, here], cot[...], ((0,), (0,))))
+
+        stores.append(pltpu.make_async_copy(down_w.at[k], down_ref, store_sem.at[2 * k + 1]))
+        stores[-1].start()
+        if k == 0:
+            stages[3]()
+
+    sdown_term[...] = low(dot(hid_shared[...], cot[...], ((0,), (0,))))
+
+    @pl.loop(0, width // COLS)
+    def _(i):
+        here = pl.ds(pl.multiple_of(i * COLS, COLS), COLS)
+        sup_term[here, :] = low(dot(n2[:, here], dpre_shared[...], ((0,), (0,))))
+
+    row_sum[...] = stages[4]()
+    for copy in stores:
+        copy.wait()
+
+
+ROWS = 256
+COLS = 256
+
+
+def experts_phase(n2, cot, w_sup, w_sdown, gates, up_first, up_second, w_down):
+    length, width = n2.shape
+    _, hidden, _ = w_down.shape
+    pad = w_sdown.shape[0]
+    tokens = length // 8
+    wide = width + 128
+    return kernel_call(
+        experts_kernel,
+        [
+            ((length, width), LOW),
+            ((tokens, wide), F32),
+            ((pad, width), LOW),
+            ((width, 2 * pad), LOW),
+            (up_first.shape, LOW),
+            (up_first.shape, LOW),
+            ((hidden, width), LOW),
+            ((hidden, width), LOW),
+        ],
+        (n2, cot, w_sup, w_sdown, gates, up_first, up_second, w_down),
+        [
+            pltpu.VMEM((8, tokens, wide), LOW),
+            pltpu.VMEM((2, *up_first.shape), LOW),
+            pltpu.VMEM(w_down.shape, LOW),
+            pltpu.VMEM((2, length, hidden), LOW),
+            pltpu.VMEM((2, length, 2 * hidden), LOW),
+            pltpu.VMEM((length, pad), LOW),
+            pltpu.VMEM((length, 2 * pad), LOW),
+            pltpu.SemaphoreType.DMA((4,)),
+            pltpu.SemaphoreType.DMA((4,)),
+        ]
+        + scatter_scratch(tokens, wide)
+        + SCATTER_SEMS,
+        4,
+        far_outs=(4, 5, 6, 7),
+        far_args=(5, 6, 7),
     )
 
 
 def turn_kernel(
-    part, out_part, upstream, gates, w_router, resid, gain, w_out, up_term, down_term,
+    row_sum, out_part, upstream, gates, w_router, resid, gain, w_out, up_term, down_term,
     dresid, dlogits, gain_term, darrived, output_rows, up_grad, down_grad,
     dattn, a_send, a_recv, *scratch,
 ):
@@ -1069,19 +1309,12 @@
         reduce_rows(down_term, down_grad, scratch[REDUCE_COUNT : 2 * REDUCE_COUNT]),
     ]
     scratch = scratch[2 * REDUCE_COUNT :]
-    count = len(scratch) // 2
-    row_stages = line_sum_stages(part, *scratch[:count])
-    out_stages = line_sum_stages(out_part, *scratch[count:])
-    row_stages[0]()
+    out_stages = line_sum_stages(out_part, *scratch)
+    out_stages[0]()
     for start, _, _ in reduces:
         start()
     holds, pair = holder(e)
-    row_stages[1]()
-    out_stages[0]()
-    row_stages[2]()
-    reduces[0][1]()
-    row_stages[3]()
-    total = row_stages[4]()
+    total = row_sum[...]
     width = upstream.shape[1]
     experts = gates.shape[1]
     dgate = total[:, width : width + experts] + total[:, width + experts : width + 2 * experts]
@@ -1110,8 +1343,9 @@
             give(source, index).start()
 
     out_stages[1]()
+    reduces[0][1]()
+    out_stages[2]()
     reduces[1][1]()
-    out_stages[2]()
     out_stages[3]()
 
     @pl.when(jnp.logical_not(holds))
@@ -1136,7 +1370,7 @@
             give(source, index).wait_send()
 
 
-def turn(part, out_part, upstream, gates, w_router, resid, gain, w_out, up_term, down_term):
+def turn(row_sum, out_part, upstream, gates, w_router, resid, gain, w_out, up_term, down_term):
     tokens, width = upstream.shape
     pair = 2 * HEAD
     count = len(PAIR_OF)
@@ -1152,7 +1386,7 @@
             ((up_rows, up_term.shape[1]), F32),
             ((down_rows, down_term.shape[1]), F32),
         ],
-        (part, out_part, upstream, gates, w_router, resid, gain, w_out, up_term, down_term),
+        (row_sum, out_part, upstream, gates, w_router, resid, gain, w_out, up_term, down_term),
         [
             pltpu.VMEM((count, tokens, pair), LOW),
             pltpu.SemaphoreType.DMA((count,)),
@@ -1160,8 +1394,6 @@
         ]
         + reduce_scratch((up_rows // 2, up_term.shape[1]), True)
         + reduce_scratch((down_rows // 2, down_term.shape[1]), True)
-        + scatter_scratch(tokens, part.shape[2])
-        + SCATTER_SEMS
         + scatter_scratch(tokens, width)
         + SCATTER_SEMS,
         2,
@@ -1226,8 +1458,6 @@
     own.start()
     partner(0).start()
     up[0]()
-    down[0]()
-    sdown[0]()
 
     def attend(head):
         dkey[...] = jnp.zeros_like(dkey)
@@ -1270,7 +1500,6 @@
             out_sum[owner, owner_z] = low(
                 out_sum[owner, owner_z].astype(F32) + out_near[owner, owner_z].astype(F32)
             )
-    out[0]()
     small_round(0)
     up[1]()
 
@@ -1305,13 +1534,15 @@
 
     column[0]()
     stages[1]()
+    out[0]()
     small_round(1)
-    down[1]()
-    sdown[1]()
     stages[2]()
+    column[1]()
+    down[0]()
+    sdown[0]()
+    stages[3]()
     small_round(2)
     out[1]()
-    stages[3]()
     small_round(3)
     values = rows[...]
     inv = lax.rsqrt(jnp.mean(values * values, axis=1, keepdims=True) + EPSILON)
@@ -1319,33 +1550,6 @@
     scaled = stages[4]() * gain[...]
     input_grad[...] = dresid[...] + inv * (
         scaled - xhat * jnp.mean(scaled * xhat, axis=1, keepdims=True)
-    )
-    column[1]()
-    out[2]()
-    for owner_z in range(4):
-        out_low[owner_z] = low(out_half[owner_z])
-    along = []
-    for i in range(3):
-        device = (b, lax.rem(e + 2 * i + 2, 8))
-        along.append(
-            send(
-                out_low.at[device[1] // 2], out_got.at[i], o_send.at[i], o_recv.at[i], device
-            )
-        )
-        along[-1].start()
-    small_round(4)
-    for i in range(len(PARTNERS)):
-        partner(i).wait_send()
-    up[2]()
-    down[2]()
-    sdown[2]()
-    for copy in along:
-        copy.wait()
-    out_grad[...] = (
-        out_half[z]
-        + out_got[0].astype(F32)
-        + out_got[1].astype(F32)
-        + out_got[2].astype(F32)
     )
     column[2]()
     piece = column_low.shape[1]
@@ -1360,6 +1564,34 @@
             send(column_low.at[device[1]], columns.at[e], c_send.at[i], c_recv.at[i], device)
         )
         across[-1].start()
+    down[1]()
+    sdown[1]()
+    small_round(4)
+    for i in range(len(PARTNERS)):
+        partner(i).wait_send()
+    out[2]()
+    for owner_z in range(4):
+        out_low[owner_z] = low(out_half[owner_z])
+    along = []
+    for i in range(3):
+        device = (b, lax.rem(e + 2 * i + 2, 8))
+        along.append(
+            send(
+                out_low.at[device[1] // 2], out_got.at[i], o_send.at[i], o_recv.at[i], device
+            )
+        )
+        along[-1].start()
+    up[2]()
+    for copy in along:
+        copy.wait()
+    out_grad[...] = (
+        out_half[z]
+        + out_got[0].astype(F32)
+        + out_got[1].astype(F32)
+        + out_got[2].astype(F32)
+    )
+    down[2]()
+    sdown[2]()
     for copy in across:
         copy.wait()
 
@@ -1425,6 +1657,12 @@
     return gate * sigma, up * sigma * (1.0 + gate * (1.0 - sigma))
 
 
+def rotary_angles(length):
+    half = HEAD // 2
+    frequency = np.float32(10000.0) ** (-np.arange(half, dtype=np.float32) / np.float32(half))
+    return np.arange(length, dtype=np.float32)[:, None] * frequency[None, :]
+
+
 def pack_device(
     block_input,
     seq_ids,
@@ -1455,36 +1693,22 @@
     s_each = -(-s_rows // 32) * 32
     s_pad = 4 * s_each
 
-    qkv_low = low(qkv_weight).reshape(rows_w, 3, pairs_of_heads, pair)
-    nothing = jnp.zeros((rows_w, 3, pair), LOW)
-    columns = [qkv_low[:, :, PAIR_OF[i]] if i in PAIR_OF else nothing for i in range(8)]
-    columns = jnp.stack(columns).reshape(8, rows_w, 3 * pair)
     sup_low = low(shared_up).reshape(rows_w, 2, 4, 8, s_rows)
     sup_low = jnp.pad(sup_low, ((0, 0),) * 4 + ((0, s_each - s_rows),)).transpose(3, 0, 1, 2, 4)
-    columns = jnp.concatenate([columns, sup_low.reshape(8, rows_w, 2 * s_pad)], axis=2)
-    up_own = low(expert_up)
-    down_own = low(expert_down)
-    sdown_own = jnp.pad(low(shared_down), ((0, s_each - s_rows), (0, 0)))
-    core = lax.rem(e, 2)
-
-    small = jnp.concatenate(
-        [
-            router_weight.reshape(-1, 128),
-            jnp.pad(gain_attn[None], ((0, 0), (0, 128 - rows_w))),
-            jnp.pad(gain_ffn[None], ((0, 0), (0, 128 - rows_w))),
-            jnp.zeros((1, 128), F32),
-        ]
-    )
-    small = low(small).astype(F32)
-    marks = jnp.concatenate([routes[0].T, seq_ids], axis=0).astype(F32)
-    marks = jnp.pad(marks, ((0, 7 - TOP), (0, 0)))
     n1_all, gains, small, marks, columns, w_out, up_first = opening(
-        rows_in, small, marks, columns, low(out_weight), up_own
+        rows_in,
+        router_weight.reshape(-1, 128),
+        gain_attn[None],
+        gain_ffn[None],
+        routes,
+        seq_ids,
+        qkv_weight,
+        sup_low.reshape(8, rows_w, 2 * s_pad),
+        out_weight,
+        expert_up,
     )
     n1_all = n1_all.reshape(length, width)
     columns = columns.reshape(width, 3 * pair + 2 * s_pad)
-    w_qkv = columns[:, : 3 * pair]
-    w_sup = columns[:, 3 * pair :]
     w_out = w_out.reshape(width, width)
     router_rows = rows_w * experts // 128
     w_router = low(small[:, :, :router_rows].transpose(1, 0, 2, 3).reshape(width, experts))
@@ -1496,26 +1720,24 @@
     positions = jnp.arange(length, dtype=jnp.int32)
     ids_row = ids_all[None, :]
     ids_column = ids_all[:, None]
-    frequency = 10000.0 ** (-jnp.arange(HEAD // 2, dtype=jnp.float32) / (HEAD // 2))
-    angle = positions.astype(F32)[:, None] * frequency[None, :]
-    cosine = jnp.concatenate([jnp.cos(angle)] * 2, axis=1)
-    sine = jnp.concatenate([-jnp.sin(angle), jnp.sin(angle)], axis=1)
+    angle = rotary_angles(length)
+    cosine = np.concatenate([np.cos(angle)] * 2, axis=1)
+    sine = np.concatenate([-np.sin(angle), np.sin(angle)], axis=1)
     qkv, logsum, attn, resid, n2_all, cot_all, up_second, down_low, w_sdown = middle(
         n1_all,
         columns,
-        cosine,
-        sine,
+        jnp.asarray(cosine),
+        jnp.asarray(sine),
         ids_row,
         ids_column,
         w_out,
         rows_in,
         gain_second,
-        low(upstream),
-        up_own,
-        down_own,
-        sdown_own,
-    )
-    up_low = (up_first, up_second)
+        cotangent,
+        expert_up,
+        expert_down,
+        shared_down,
+    )
     attn = attn.transpose(1, 0, 2).reshape(tokens, width)
     cot_all = cot_all.reshape(length, width)
 
@@ -1529,46 +1751,21 @@
     gates = gates / jnp.sum(gates, axis=1, keepdims=True)
     mine = lax.dynamic_slice_in_dim(gates, 2 * e, 2, 1)
 
-    output_part = 0.0
-    drow_part = 0.0
-    dgates = []
-    up_terms = []
-    down_terms = []
-    for k in range(2):
-        gate = mine[:, k : k + 1]
-        pre = dot(n2_all, up_low[k])
-        silu, slope = silu_parts(pre[:, :hidden], pre[:, hidden:])
-        hid = silu * pre[:, hidden:]
-        back = dot(cot_all, down_low[k], ((1,), (1,)))
-        dgates.append(jnp.sum(back * hid, axis=1, keepdims=True))
-        hid_low = low(hid * gate)
-        output_part = output_part + dot(hid_low, down_low[k])
-        down_terms.append(dot(hid_low, cot_all, ((0,), (0,))))
-        back = back * gate
-        dpre = low(jnp.concatenate([back * slope, back * silu], axis=1))
-        up_terms.append(dot(n2_all, dpre, ((0,), (0,))))
-        drow_part = drow_part + dot(dpre, up_low[k], ((1,), (1,)))
-    pre = dot(n2_all, w_sup)
-    silu, slope = silu_parts(pre[:, :s_pad], pre[:, s_pad:])
-    hid_low = low(silu * pre[:, s_pad:])
-    back = dot(cot_all, w_sdown, ((1,), (1,)))
-    output_part = output_part + dot(hid_low, w_sdown)
-    sdown_term = dot(hid_low, cot_all, ((0,), (0,)))
-    dpre = low(jnp.concatenate([back * slope, back * silu], axis=1))
-    sup_term = dot(n2_all, dpre, ((0,), (0,)))
-    drow_part = drow_part + dot(dpre, w_sup, ((1,), (1,)))
-    lane = jnp.arange(experts, dtype=jnp.int32)[None, :] - 2 * e
-    dgate = jnp.where(lane == 0, dgates[0], 0.0) + jnp.where(lane == 1, dgates[1], 0.0)
-    dgate_high = low(dgate)
-    dgate_rest = low(dgate - dgate_high.astype(F32))
-    spare = jnp.zeros((length, 128 - 2 * experts), LOW)
-    part = jnp.concatenate([low(drow_part), dgate_high, dgate_rest, spare], axis=1)
-    up_terms = [low(term) for term in up_terms]
-    down_terms = [low(term) for term in down_terms]
+    output_part, row_sum, sdown_term, sup_term, *terms = experts_phase(
+        n2_all,
+        cot_all,
+        columns[:, 3 * pair :],
+        w_sdown,
+        mine,
+        up_first,
+        up_second,
+        down_low,
+    )
+    up_terms, down_terms = terms[:2], terms[2:]
     own_gates = lax.dynamic_slice_in_dim(gates, e * tokens, tokens, 0)
     dresid, dlogits, gain_ffn_term, dattn, output_rows, up_grad_first, down_grad_first = turn(
-        part.reshape(8, tokens, part.shape[1]),
-        low(output_part).reshape(8, tokens, width),
+        row_sum,
+        output_part.reshape(8, tokens, width),
         upstream,
         own_gates,
         w_router.T,
@@ -1589,8 +1786,8 @@
         logsum,
         n1_all,
         columns,
-        cosine,
-        sine,
+        jnp.asarray(cosine),
+        jnp.asarray(sine),
         ids_row,
         ids_column,
         rows_in,
@@ -1598,8 +1795,8 @@
         dresid,
         up_terms[1],
         down_terms[1],
-        low(sdown_term),
-        low(sup_term),
+        sdown_term,
+        sup_term,
         out_term,
         small,
     )

time: 569 us -> 489 us (0.86)
  the two profiles are of different devices: /device:TPU:25 before, /device:TPU:0 now
where the time goes in v4:
time: 489 us; the launch traced here: 481 us
  Pallas kernels  434 us (89%)
  local copies, waits for them, and re-layouts  26.3 us (5%)
  other arithmetic  11.4 us (2%)
  matrix products  7.65 us (2%)
    pallas_call x5, Pallas kernels, kernel_call(): pl.pallas_call(body, cost_estimate=pl.CostEstimate(flops=COST, bytes_acce...  434 us

profile of v4, /device:TPU:0, one launch (start us, length us, event | category | flops | bytes accessed | tf_op | source)
XLA Modules:
  0.0 481.0 jit_solution(2456174508727965737)
XLA Ops:
  0.7 0.8 copy.43
  2.2 1.4 copy.45.routes
  3.6 1.0 convert_element_type.40
  4.6 1.7 reshape.77
  6.7 1.1 reshape.78.sup
  7.8 85.0 %shard_map.230 = (bf16[8,128,1280]{2,1,0:T(8,128)(2,1)}, f32[2,1280]{1,0:T(2,128)}, f32[8,4,8,128]{3,2,1,0:T(8,128)}, f32[8,8,128]{2,1,0:T(8,128)}, bf16[4,8,40,...) custom-call(f32[128,1280]{1,0:T(8,128)} %bitcast.54, ...), custom_call_target="tpu_custom_call" | custom-call | flops 1000000000 | bytes 1000000000 | tf_op jit(solution)/shard_map/pallas_call | solution.py:720
  92.8 1.4 fusion.10
  94.1 0.8 convert_bitcast_fusion
  94.9 0.9 fusion.7
  96.1 0.8 copy.52
  97.5 1.6 fusion.9
  99.1 2.0 slice.65.w_sup
  101.1 92.7 %shard_map.231 = (bf16[6,1024,128]{2,1,0:T(8,128)(2,1)}, f32[2,1024,128]{2,1,0:T(8,128)}, bf16[5,128,256]{2,1,0:T(8,128)(2,1)}, f32[128,1280]{1,0:T(8,128)}, bf1...) custom-call(bf16[1024,1280]{1,0:T(8,128)(2,1)} %bitcast.52, ...), custom_call_target="tpu_custom_call" | custom-call | flops 1000000000 | bytes 1000000000 | tf_op jit(solution)/shard_map/pallas_call | solution.py:720
  193.8 2.7 fusion.11
  197.8 1.0 constant_dynamic-slice_fusion.1.gates
  198.8 77.8 %shard_map.232 = (bf16[1024,1280]{1,0:T(8,128)(2,1)}, f32[128,1408]{1,0:T(8,128)}, bf16[128,1280]{1,0:T(8,128)(2,1)}, bf16[1280,256]{1,0:T(8,128)(2,1)}, bf16[12...) custom-call(bf16[1024,1280]{1,0:T(8,128)(2,1)} %bitcast.60, ...), custom_call_target="tpu_custom_call" | custom-call | flops 1000000000 | bytes 1000000000 | tf_op jit(solution)/shard_map/pallas_call | solution.py:720
  276.7 70.5 %shard_map.233 = (f32[128,1280]{1,0:T(8,128)}, bf16[128,16]{1,0:T(8,128)(2,1)}, f32[1,1280]{1,0:T(1,128)}, bf16[8,128,256]{2,1,0:T(8,128)(2,1)}, f32[128,1280]{1...) custom-call(f32[128,1408]{1,0:T(8,128)} %get-tuple-element.61.row_sum, bf16[8,128,1280]{2,1,0:T(8,128)(2,1)} %bitcast.64, ...), custom_call_target="tpu_custom_call" | custom-call | flops 1000000000 | bytes 1000000000 | tf_op jit(solution)/shard_map/pallas_call | solution.py:720
  347.2 1.2 fusion.3
  348.4 1.4 maximum_maximum_fusion.small
  350.0 3.8 convolution_convert_fusion
  353.8 108.2 %shard_map.234 = (f32[128,1280]{1,0:T(8,128)}, bf16[8,40,1024]{2,1,0:T(8,128)(2,1)}, f32[40,1280]{1,0:T(8,128)}, f32[320,1792]{1,0:T(8,128)}, f32[224,1280]{1,0:...) custom-call(bf16[8,128,256]{2,1,0:T(8,128)(2,1)} %get-tuple-element.67.dattn, ...), custom_call_target="tpu_custom_call" | custom-call | flops 1000000000 | bytes 1000000000 | tf_op jit(solution)/shard_map/pallas_call | solution.py:720
  462.1 1.3 dynamic-slice_bitcast_fusion.1
  463.4 1.4 dynamic-slice_bitcast_fusion
  464.8 0.9 slice.72
  465.7 1.2 convert_element_type.47
  469.6 0.8 copy.55
  470.4 1.6 reshape.91
  472.0 3.1 pad_maximum_fusion.1
  475.1 2.4 pad_maximum_fusion
  477.5 0.8 copy.68
  478.3 0.8 copy.69
  479.2 0.7 copy.70
  (50 shorter events, 7.0 us)
Async XLA Ops:
  276.7 73.1 %copy-start.7 = (bf16[5,128,256]{2,1,0:T(8,128)(2,1)S(1)}, bf16[5,128,256]{2,1,0:T(8,128)(2,1)}, u32[]{:S(2)}) copy-start(bf16[5,128,256]{2,1,0:T(8,128)(2,1)} %get-tuple-element.75) | copy-start | bytes 983044
  467.0 1.1 copy-start.1
  467.4 0.9 copy-start.10
  468.1 1.5 copy-start
  469.6 2.3 copy-start.4
  472.0 3.1 copy-start.2
  472.0 3.1 copy-start.3
  475.0 2.4 copy-start.5
  475.0 3.3 copy-start.6
  477.5 1.7 copy-start.8
  477.5 2.4 copy-start.9

commit v5 on v4

--- a/solution.py
+++ b/solution.py
@@ -354,10 +354,11 @@
     return b, e, e // 2, lax.rem(e, 2)
 
 
-def greet_line():
+def greet_near():
     b, e, z, core = place()
     barrier = pltpu.get_barrier_semaphore()
-    pl.semaphore_signal(barrier, inc=1, device_id=(b, e ^ 1), device_id_type=MESH_ID)
+    for device in ((b ^ 1, e), (b ^ 2, e), (b, e ^ 1)):
+        pl.semaphore_signal(barrier, inc=1, device_id=device, device_id_type=MESH_ID)
 
     @pl.when(z > 0)
     def _():
@@ -368,7 +369,7 @@
         pl.semaphore_signal(barrier, inc=1, device_id=(b, e + 2), device_id_type=MESH_ID)
 
     ends = jnp.where((z == 0) | (z == 3), 1, 0)
-    pl.semaphore_wait(barrier, 3 - ends)
+    pl.semaphore_wait(barrier, 5 - ends)
 
 
 def greet(devices):
@@ -989,7 +990,7 @@
 
 def middle_kernel(
     n1, weights, cosine, sine, ids_row, ids_column, w_out, rows, gain, cot, up_weight, down_weight, sdown_weight,
-    qkv, logsum, attn, resid, n2_all, cot_all, up_all, down_all, sdown_all,
+    qkv, logsum, attn, resid, n2_all, cot_all, up_all, down_all, sdown_all, down_second,
     attended, up_own, up_wide, down_own, sdown_own, up_sem, a_send, a_recv, *sems,
 ):
     b, e, z, core = place()
@@ -998,11 +999,10 @@
     count = len(SPREAD_SEMS)
     spreads = [
         spread_rows(up_own, up_all, up_own.shape[0], sems[:count]),
-        spread_rows(down_own.at[0], down_all.at[0], down_own.shape[1], sems[count : 2 * count]),
-        spread_rows(down_own.at[1], down_all.at[1], down_own.shape[1], sems[2 * count : 3 * count]),
-        spread_rows(sdown_own, sdown_all, sdown_own.shape[0], sems[3 * count : 4 * count]),
+        spread_rows(down_own, down_all, down_own.shape[0], sems[count : 2 * count]),
+        spread_rows(sdown_own, sdown_all, sdown_own.shape[0], sems[2 * count : 3 * count]),
     ]
-    sems = sems[4 * count :]
+    sems = sems[3 * count :]
     cot_stages = line_stages(cot_all, *sems[: len(GATHER_SEMS)])
     n2_stages = line_stages(n2_all, *sems[len(GATHER_SEMS) :])
     cot_all[e] = low(cot[0])
@@ -1013,7 +1013,8 @@
     up_own[...] = low(up_wide[...])
     spreads[0][0]()
     cot_stages[0]()
-    down_own[...] = low(down_weight[...])
+    down_own[...] = low(down_weight[0])
+    down_second[...] = low(down_weight[1])
     short = sdown_own.shape[0] - sdown_weight.shape[0]
     sdown_own[...] = low(
         jnp.concatenate([sdown_weight[...], jnp.zeros((short, cot.shape[2]), F32)], axis=0)
@@ -1062,7 +1063,8 @@
                         out[j * tokens : (j + 1) * tokens]
                     )
 
-        cot_stages[2 + head]()
+        if head == 0:
+            cot_stages[2]()
         spreads[head][1]()
 
     def give(i):
@@ -1091,8 +1093,8 @@
     inv = lax.rsqrt(jnp.mean(total * total, axis=1, keepdims=True) + EPSILON)
     n2_all[e] = low(total * inv * gain[...])
     n2_stages[0]()
+    cot_stages[3]()
     spreads[2][1]()
-    spreads[3][1]()
     for stage in n2_stages[1:]:
         stage()
     cot_stages[4]()
@@ -1131,21 +1133,22 @@
             ((8, tokens, width), LOW),
             ((8, tokens, width), LOW),
             ((4 * up_rows, up_width), LOW),
-            ((2, 4 * down_rows, width), LOW),
+            ((4 * down_rows, width), LOW),
             ((4 * sdown_rows, width), LOW),
+            ((down_rows, width), LOW),
         ],
         (n1, weights, cosine, sine, ids_row, ids_column, w_out, rows, gain, cot, up_weight, down_weight, sdown_weight),
         [
             pltpu.VMEM((8, tokens, pair), LOW),
             pltpu.VMEM((up_rows, up_width), LOW),
             pltpu.VMEM((up_rows, up_width), F32),
-            pltpu.VMEM((2, down_rows, width), LOW),
+            pltpu.VMEM((down_rows, width), LOW),
             pltpu.VMEM((sdown_rows, width), LOW),
             pltpu.SemaphoreType.DMA((1,)),
             pltpu.SemaphoreType.DMA((7,)),
             pltpu.SemaphoreType.DMA((count,)),
         ]
-        + SPREAD_SEMS * 4
+        + SPREAD_SEMS * 3
         + GATHER_SEMS * 2,
         1,
         far_outs=(6, 7, 8),
@@ -1154,33 +1157,57 @@
 
 
 def experts_kernel(
-    n2, cot, w_sup, w_sdown, gates, up_first, up_second, w_down,
-    out_part, row_sum, sdown_term, sup_term, up_term_first, up_term_second, down_term_first, down_term_second,
+    n2, cot, w_sup, w_sdown, gates, down_second, up_first, up_second, down_first,
+    out_part, row_sum, sdown_term, sup_term, down_grad, up_term_first, up_term_second, down_term_second,
     part, up_w, down_w, hid, dpre, hid_shared, dpre_shared, load_sem, store_sem, *scratch,
 ):
     e = lax.axis_index("expert")
-    greet_line()
-    stages = line_sum_stages(part, *scratch)
-    tokens = part.shape[1]
     length, width = n2.shape
     hidden = down_w.shape[1]
     pad = w_sdown.shape[0]
-    loads = []
-    for k, up_ref in enumerate((up_first, up_second)):
-        loads.append(pltpu.make_async_copy(up_ref, up_w.at[k], load_sem.at[2 * k]))
-        loads.append(pltpu.make_async_copy(w_down.at[k], down_w.at[k], load_sem.at[2 * k + 1]))
+    loads = [
+        pltpu.make_async_copy(up_first, up_w.at[0], load_sem.at[0]),
+        pltpu.make_async_copy(down_first, down_w.at[0], load_sem.at[1]),
+        pltpu.make_async_copy(up_second, up_w.at[1], load_sem.at[2]),
+    ]
     for copy in loads:
         copy.start()
-    for copy in loads:
+    count = len(SPREAD_SEMS)
+    arrive = spread_rows(down_second, down_w.at[1], down_second.shape[0], scratch[:count])
+    reduce = reduce_rows(down_w.at[0], down_grad, scratch[count : count + REDUCE_COUNT])
+    stages = line_sum_stages(part, *scratch[count + REDUCE_COUNT :])
+    tokens = part.shape[1]
+    greet_near()
+    arrive[0]()
+    for copy in loads[:2]:
         copy.wait()
     lane = lax.broadcasted_iota(jnp.int32, (ROWS, 128), 1)
 
-    @pl.loop(0, length // ROWS)
-    def _(i):
+    def routed(k, here, x, c):
+        gate = gates[here, k : k + 1]
+        gate_part = dot(x, up_w[k, :, :hidden])
+        up_part = dot(x, up_w[k, :, hidden:])
+        back = dot(c, down_w[k], ((1,), (1,)))
+        silu, slope = silu_parts(gate_part, up_part)
+        value = silu * up_part
+        dgate = jnp.sum(back * value, axis=1, keepdims=True)
+        hid[k, here, :] = low(value * gate)
+        back = back * gate
+        dpre[k, here, :hidden] = low(back * slope)
+        dpre[k, here, hidden:] = low(back * silu)
+        out = dot(hid[k, here, :], down_w[k])
+        drow = dot(dpre[k, here, :], up_w[k], ((1,), (1,)))
+        return out, drow, dgate
+
+    def mark(k, dgate, marks):
+        high = low(dgate).astype(F32)
+        marks = jnp.where(lane == 2 * e + k, high, marks)
+        return jnp.where(lane == 2 * e + k + 16, dgate - high, marks)
+
+    def first_pass(i):
         here = pl.ds(pl.multiple_of(i * ROWS, ROWS), ROWS)
         x = n2[here, :]
         c = cot[here, :]
-        marks = jnp.zeros((ROWS, 128), F32)
         gate_part = dot(x, w_sup[:, :pad])
         up_part = dot(x, w_sup[:, pad:])
         back = dot(c, w_sdown[...], ((1,), (1,)))
@@ -1188,61 +1215,75 @@
         hid_shared[here, :] = low(silu * up_part)
         dpre_shared[here, :pad] = low(back * slope)
         dpre_shared[here, pad:] = low(back * silu)
-        out = dot(hid_shared[here, :], w_sdown[...])
-        drow = dot(dpre_shared[here, :], w_sup[...], ((1,), (1,)))
-        for k in range(2):
-            gate = gates[here, k : k + 1]
-            gate_part = dot(x, up_w[k, :, :hidden])
-            up_part = dot(x, up_w[k, :, hidden:])
-            back = dot(c, down_w[k], ((1,), (1,)))
-            silu, slope = silu_parts(gate_part, up_part)
-            value = silu * up_part
-            dgate = jnp.sum(back * value, axis=1, keepdims=True)
-            hid[k, here, :] = low(value * gate)
-            back = back * gate
-            dpre[k, here, :hidden] = low(back * slope)
-            dpre[k, here, hidden:] = low(back * silu)
-            out = out + dot(hid[k, here, :], down_w[k])
-            drow = drow + dot(dpre[k, here, :], up_w[k], ((1,), (1,)))
-            high = low(dgate).astype(F32)
-            marks = jnp.where(lane == 2 * e + k, high, marks)
-            marks = jnp.where(lane == 2 * e + k + 16, dgate - high, marks)
+        out, drow, dgate = routed(0, here, x, c)
+        out = out + dot(hid_shared[here, :], w_sdown[...])
+        drow = drow + dot(dpre_shared[here, :], w_sup[...], ((1,), (1,)))
+        marks = mark(0, dgate, jnp.zeros((ROWS, 128), F32))
         out_part[here, :] = low(out)
         for j in range(ROWS // tokens):
             rows = slice(j * tokens, (j + 1) * tokens)
             part[i * (ROWS // tokens) + j, :, :width] = low(drow[rows])
             part[i * (ROWS // tokens) + j, :, width:] = low(marks[rows])
 
+    half = length // ROWS // 2
+
+    @pl.loop(0, half)
+    def _(i):
+        first_pass(i)
+
+    arrive[1]()
+
+    @pl.loop(half, 2 * half)
+    def _(i):
+        first_pass(i)
+
+    loads[2].wait()
+    arrive[2]()
+
+    @pl.loop(0, length // ROWS)
+    def _(i):
+        here = pl.ds(pl.multiple_of(i * ROWS, ROWS), ROWS)
+        out, drow, dgate = routed(1, here, n2[here, :], cot[here, :])
+        out_part[here, :] = low(out_part[here, :].astype(F32) + out)
+        for j in range(ROWS // tokens):
+            rows = slice(j * tokens, (j + 1) * tokens)
+            block = i * (ROWS // tokens) + j
+            part[block, :, :width] = low(part[block, :, :width].astype(F32) + drow[rows])
+            marks = part[block, :, width:].astype(F32)
+            high = low(dgate[rows]).astype(F32)
+            marks = jnp.where(lane[rows] == 2 * e + 1, high, marks)
+            marks = jnp.where(lane[rows] == 2 * e + 17, dgate[rows] - high, marks)
+            part[block, :, width:] = low(marks)
+
     stages[0]()
-    stores = []
-    for k, (up_ref, down_ref) in enumerate(
-        ((up_term_first, down_term_first), (up_term_second, down_term_second))
-    ):
-
-        if k == 0:
-            stages[1]()
-
+
+    def up_gradient(k, up_ref):
         @pl.loop(0, width // COLS)
         def _(i):
             here = pl.ds(pl.multiple_of(i * COLS, COLS), COLS)
             up_w[k, here, :] = low(dot(n2[:, here], dpre[k], ((0,), (0,))))
 
-        if k == 0:
-            stages[2]()
-
-        stores.append(pltpu.make_async_copy(up_w.at[k], up_ref, store_sem.at[2 * k]))
-        stores[-1].start()
-
+        store = pltpu.make_async_copy(up_w.at[k], up_ref, store_sem.at[k])
+        store.start()
+        return store
+
+    def down_gradient(k):
         @pl.loop(0, hidden // 128)
         def _(i):
             here = pl.ds(pl.multiple_of(i * 128, 128), 128)
             down_w[k, here, :] = low(dot(hid[k, :, here], cot[...], ((0,), (0,))))
 
-        stores.append(pltpu.make_async_copy(down_w.at[k], down_ref, store_sem.at[2 * k + 1]))
-        stores[-1].start()
-        if k == 0:
-            stages[3]()
-
+    down_gradient(0)
+    reduce[0]()
+    stages[1]()
+    stores = [up_gradient(0, up_term_first)]
+    stages[2]()
+    reduce[1]()
+    down_gradient(1)
+    stores.append(pltpu.make_async_copy(down_w.at[1], down_term_second, store_sem.at[2]))
+    stores[-1].start()
+    stages[3]()
+    stores.append(up_gradient(1, up_term_second))
     sdown_term[...] = low(dot(hid_shared[...], cot[...], ((0,), (0,))))
 
     @pl.loop(0, width // COLS)
@@ -1251,6 +1292,7 @@
         sup_term[here, :] = low(dot(n2[:, here], dpre_shared[...], ((0,), (0,))))
 
     row_sum[...] = stages[4]()
+    reduce[2]()
     for copy in stores:
         copy.wait()
 
@@ -1259,9 +1301,9 @@
 COLS = 256
 
 
-def experts_phase(n2, cot, w_sup, w_sdown, gates, up_first, up_second, w_down):
+def experts_phase(n2, cot, w_sup, w_sdown, gates, down_second, up_first, up_second, down_first):
     length, width = n2.shape
-    _, hidden, _ = w_down.shape
+    hidden = down_first.shape[0]
     pad = w_sdown.shape[0]
     tokens = length // 8
     wide = width + 128
@@ -1272,34 +1314,36 @@
             ((tokens, wide), F32),
             ((pad, width), LOW),
             ((width, 2 * pad), LOW),
+            ((hidden // 4, width), F32),
             (up_first.shape, LOW),
             (up_first.shape, LOW),
             ((hidden, width), LOW),
-            ((hidden, width), LOW),
         ],
-        (n2, cot, w_sup, w_sdown, gates, up_first, up_second, w_down),
+        (n2, cot, w_sup, w_sdown, gates, down_second, up_first, up_second, down_first),
         [
             pltpu.VMEM((8, tokens, wide), LOW),
             pltpu.VMEM((2, *up_first.shape), LOW),
-            pltpu.VMEM(w_down.shape, LOW),
+            pltpu.VMEM((2, hidden, width), LOW),
             pltpu.VMEM((2, length, hidden), LOW),
             pltpu.VMEM((2, length, 2 * hidden), LOW),
             pltpu.VMEM((length, pad), LOW),
             pltpu.VMEM((length, 2 * pad), LOW),
-            pltpu.SemaphoreType.DMA((4,)),
-            pltpu.SemaphoreType.DMA((4,)),
+            pltpu.SemaphoreType.DMA((3,)),
+            pltpu.SemaphoreType.DMA((3,)),
         ]
+        + SPREAD_SEMS
+        + reduce_scratch((hidden // 8, width))
         + scatter_scratch(tokens, wide)
         + SCATTER_SEMS,
         4,
-        far_outs=(4, 5, 6, 7),
-        far_args=(5, 6, 7),
+        far_outs=(5, 6, 7),
+        far_args=(6, 7, 8),
     )
 
 
 def turn_kernel(
-    row_sum, out_part, upstream, gates, w_router, resid, gain, w_out, up_term, down_term,
-    dresid, dlogits, gain_term, darrived, output_rows, up_grad, down_grad,
+    row_sum, out_part, upstream, gates, w_router, resid, gain, w_out, attn, n2, up_term, down_term,
+    dresid, small, out_term, darrived, output_rows, up_grad, down_grad,
     dattn, a_send, a_recv, *scratch,
 ):
     b, e, z, core = place()
@@ -1320,12 +1364,11 @@
     dgate = total[:, width : width + experts] + total[:, width + experts : width + 2 * experts]
     own = gates[...]
     dlog = low(own * (dgate - jnp.sum(own * dgate, axis=1, keepdims=True)))
-    dlogits[...] = dlog
     dn2 = total[:, :width] + dot(dlog, w_router[...])
     rows = resid[...]
     inv = lax.rsqrt(jnp.mean(rows * rows, axis=1, keepdims=True) + EPSILON)
     xhat = rows * inv
-    gain_term[...] = jnp.sum(dn2 * xhat, axis=0, keepdims=True)
+    small[experts : experts + 1, :] = jnp.sum(dn2 * xhat, axis=0, keepdims=True)
     scaled = dn2 * gain[...]
     grad = upstream[...] + inv * (scaled - xhat * jnp.mean(scaled * xhat, axis=1, keepdims=True))
     dresid[...] = grad
@@ -1344,7 +1387,14 @@
 
     out_stages[1]()
     reduces[0][1]()
+    small[:experts, :] = dot(dlog, n2[...], ((0,), (0,)))
+    small[experts + 1 :, :] = jnp.zeros((small.shape[0] - experts - 1, width), F32)
     out_stages[2]()
+    grad_low = low(dresid[...])
+    for index in range(len(PAIR_OF)):
+        out_term[index * size : (index + 1) * size, :] = low(
+            dot(attn[index], grad_low, ((0,), (0,)))
+        )
     reduces[1][1]()
     out_stages[3]()
 
@@ -1370,7 +1420,7 @@
             give(source, index).wait_send()
 
 
-def turn(row_sum, out_part, upstream, gates, w_router, resid, gain, w_out, up_term, down_term):
+def turn(row_sum, out_part, upstream, gates, w_router, resid, gain, w_out, attn, n2, up_term, down_term):
     tokens, width = upstream.shape
     pair = 2 * HEAD
     count = len(PAIR_OF)
@@ -1379,14 +1429,14 @@
         turn_kernel,
         [
             ((tokens, width), F32),
-            (gates.shape, LOW),
-            ((1, width), F32),
+            ((gates.shape[1] + 8, width), F32),
+            ((width, width), LOW),
             ((8, tokens, pair), LOW),
             ((tokens, width), F32),
             ((up_rows, up_term.shape[1]), F32),
             ((down_rows, down_term.shape[1]), F32),
         ],
-        (row_sum, out_part, upstream, gates, w_router, resid, gain, w_out, up_term, down_term),
+        (row_sum, out_part, upstream, gates, w_router, resid, gain, w_out, attn, n2, up_term, down_term),
         [
             pltpu.VMEM((count, tokens, pair), LOW),
             pltpu.SemaphoreType.DMA((count,)),
@@ -1397,7 +1447,7 @@
         + scatter_scratch(tokens, width)
         + SCATTER_SEMS,
         2,
-        far_args=(8, 9),
+        far_args=(10, 11),
     )
 
 
@@ -1406,8 +1456,8 @@
 
 def closing_kernel(
     dattn, qkv, logsum, n1, weights, cosine, sine, ids_row, ids_column, rows, gain, dresid,
-    up_term, down_term, sdown_term, sup_term, out_term, small,
-    input_grad, columns, out_grad, up_grad, down_grad, sdown_grad, small_sum,
+    up_term, sdown_term, sup_term, out_term, small,
+    input_grad, columns, out_grad, up_grad, sdown_grad, small_sum,
     dkey, dvalue, dprojected, part, column_term, column_sum, column_low,
     out_near, out_sum, out_low, out_half, out_got, small_got, small_step,
     n_send, n_recv, o_send, o_recv, c_send, c_recv, s_send, s_recv, *scratch,
@@ -1425,7 +1475,6 @@
         return mine
 
     up = reduce_rows(up_term, up_grad, cut())
-    down = reduce_rows(down_term, down_grad, cut())
     sdown = reduce_rows(sdown_term, sdown_grad, cut())
     column = reduce_rows(column_term, column_sum, cut())
     out = reduce_stages(
@@ -1538,7 +1587,6 @@
     small_round(1)
     stages[2]()
     column[1]()
-    down[0]()
     sdown[0]()
     stages[3]()
     small_round(2)
@@ -1564,7 +1612,6 @@
             send(column_low.at[device[1]], columns.at[e], c_send.at[i], c_recv.at[i], device)
         )
         across[-1].start()
-    down[1]()
     sdown[1]()
     small_round(4)
     for i in range(len(PARTNERS)):
@@ -1590,7 +1637,6 @@
         + out_got[1].astype(F32)
         + out_got[2].astype(F32)
     )
-    down[2]()
     sdown[2]()
     for copy in across:
         copy.wait()
@@ -1598,15 +1644,13 @@
 
 def closing(
     dattn, qkv, logsum, n1, weights, cosine, sine, ids_row, ids_column, rows, gain, dresid,
-    up_term, down_term, sdown_term, sup_term, out_term, small,
+    up_term, sdown_term, sup_term, out_term, small,
 ):
     tokens, width = rows.shape
     length = n1.shape[0]
     rows_w = out_term.shape[3]
     wide = weights.shape[1]
-    up_rows, down_rows, sdown_rows = (
-        term.shape[0] // 4 for term in (up_term, down_term, sdown_term)
-    )
+    up_rows, sdown_rows = up_term.shape[0] // 4, sdown_term.shape[0] // 4
     dma = pltpu.SemaphoreType.DMA
     return kernel_call(
         closing_kernel,
@@ -1615,13 +1659,12 @@
             ((8, rows_w, wide), LOW),
             ((rows_w, width), F32),
             ((up_rows, up_term.shape[1]), F32),
-            ((down_rows, width), F32),
             ((sdown_rows, width), F32),
             (small.shape, F32),
         ],
         (
             dattn, qkv, logsum, n1, weights, cosine, sine, ids_row, ids_column, rows, gain, dresid,
-            up_term, down_term, sdown_term, sup_term, out_term, small,
+            up_term, sdown_term, sup_term, out_term, small,
         ),
         [
             pltpu.VMEM((length, HEAD), F32),
@@ -1641,14 +1684,13 @@
             dma((2,)), dma((1,)), dma((3,)), dma((3,)), dma((7,)), dma((7,)), dma((5,)), dma((5,)),
         ]
         + reduce_scratch((up_rows // 2, up_term.shape[1]), True)
-        + reduce_scratch((down_rows // 2, width), True)
         + reduce_scratch((sdown_rows // 2, width))
         + reduce_scratch((width // 8, wide))
         + reduce_scratch((2, rows_w, width))
         + scatter_scratch(tokens, width)
         + SCATTER_SEMS,
         3,
-        far_args=(12, 13, 16),
+        far_args=(12, 15),
     )
 
 
@@ -1723,7 +1765,7 @@
     angle = rotary_angles(length)
     cosine = np.concatenate([np.cos(angle)] * 2, axis=1)
     sine = np.concatenate([-np.sin(angle), np.sin(angle)], axis=1)
-    qkv, logsum, attn, resid, n2_all, cot_all, up_second, down_low, w_sdown = middle(
+    qkv, logsum, attn, resid, n2_all, cot_all, up_second, down_low, w_sdown, down_second = middle(
         n1_all,
         columns,
         jnp.asarray(cosine),
@@ -1738,7 +1780,6 @@
         expert_down,
         shared_down,
     )
-    attn = attn.transpose(1, 0, 2).reshape(tokens, width)
     cot_all = cot_all.reshape(length, width)
 
     n2 = lax.dynamic_index_in_dim(n2_all, e, 0, False)
@@ -1751,19 +1792,20 @@
     gates = gates / jnp.sum(gates, axis=1, keepdims=True)
     mine = lax.dynamic_slice_in_dim(gates, 2 * e, 2, 1)
 
-    output_part, row_sum, sdown_term, sup_term, *terms = experts_phase(
+    output_part, row_sum, sdown_term, sup_term, down_grad_first, *terms = experts_phase(
         n2_all,
         cot_all,
         columns[:, 3 * pair :],
         w_sdown,
         mine,
+        down_second,
         up_first,
         up_second,
         down_low,
     )
-    up_terms, down_terms = terms[:2], terms[2:]
+    up_terms, down_term_second = terms[:2], terms[2]
     own_gates = lax.dynamic_slice_in_dim(gates, e * tokens, tokens, 0)
-    dresid, dlogits, gain_ffn_term, dattn, output_rows, up_grad_first, down_grad_first = turn(
+    dresid, small, out_term, dattn, output_rows, up_grad_first, down_grad_second = turn(
         row_sum,
         output_part.reshape(8, tokens, width),
         upstream,
@@ -1772,15 +1814,13 @@
         resid,
         gain_second,
         w_out,
+        attn,
+        n2,
         up_terms[0],
-        down_terms[0],
-    )
-    router_term = dot(dlogits, n2, ((0,), (0,)))
-    small = jnp.concatenate(
-        [router_term, gain_ffn_term, jnp.zeros((7, width), F32)], axis=0
-    )
-    out_term = low(dot(attn, low(dresid), ((0,), (0,)))).reshape(4, 4, 2, rows_w, width)
-    input_grad, columns, out_grad, up_grad_second, down_grad_second, sdown_grad, small = closing(
+        down_term_second,
+    )
+    out_term = out_term.reshape(4, 4, 2, rows_w, width)
+    input_grad, columns, out_grad, up_grad_second, sdown_grad, small = closing(
         dattn,
         qkv,
         logsum,
@@ -1794,7 +1834,6 @@
         gain_first,
         dresid,
         up_terms[1],
-        down_terms[1],
         sdown_term,
         sup_term,
         out_term,

time: 489 us -> 463 us (0.947)
  Pallas kernels: 434 us -> 413 us
  matrix products: 7.65 us -> 2.66 us
    pallas_call x5, Pallas kernels: 434 us -> 413 us  [kernel_call(): pl.pallas_call(body, cost_estimate=pl.CostEstimate(flops=COST, bytes_acce...]
    dot_general x3 -> x1, matrix products: 7.65 us -> 2.66 us  [dot(): lax.dot_general(left, right, (dims, ((), ())), preferred_element_type=F32)]
where the time goes in v5:
time: 463 us; the launch traced here: 455 us
  Pallas kernels  413 us (89%)
  local copies, waits for them, and re-layouts  27.8 us (6%)
  other arithmetic  9.96 us (2%)
    pallas_call x5, Pallas kernels, kernel_call(): pl.pallas_call(body, cost_estimate=pl.CostEstimate(flops=COST, bytes_acce...  413 us

profile of v5, /device:TPU:0, one launch (start us, length us, event | category | flops | bytes accessed | tf_op | source)
XLA Modules:
  0.0 455.2 jit_solution(14120745139672634240)
XLA Ops:
  0.7 0.8 copy.42
  1.4 0.7 reshape.73.router
  2.1 1.4 copy.44.routes
  3.5 1.0 convert_element_type.34
  4.5 1.7 reshape.74
  6.6 1.1 reshape.75.sup
  7.7 85.0 %shard_map.230 = (bf16[8,128,1280]{2,1,0:T(8,128)(2,1)}, f32[2,1280]{1,0:T(2,128)}, f32[8,4,8,128]{3,2,1,0:T(8,128)}, f32[8,8,128]{2,1,0:T(8,128)}, bf16[4,8,40,...) custom-call(f32[128,1280]{1,0:T(8,128)} %bitcast.48, ...), custom_call_target="tpu_custom_call" | custom-call | flops 1000000000 | bytes 1000000000 | tf_op jit(solution)/shard_map/pallas_call | solution.py:721
  92.8 1.4 fusion.5
  94.1 0.8 convert_bitcast_fusion
  94.9 0.9 fusion.3
  96.1 0.8 copy.51
  97.5 1.6 fusion.4
  99.1 2.0 slice.65.w_sup
  101.1 75.4 %shard_map.231 = (bf16[6,1024,128]{2,1,0:T(8,128)(2,1)}, f32[2,1024,128]{2,1,0:T(8,128)}, bf16[5,128,256]{2,1,0:T(8,128)(2,1)}, f32[128,1280]{1,0:T(8,128)}, bf1...) custom-call(bf16[1024,1280]{1,0:T(8,128)(2,1)} %bitcast.46, ...), custom_call_target="tpu_custom_call" | custom-call | flops 1000000000 | bytes 1000000000 | tf_op jit(solution)/shard_map/pallas_call | solution.py:721
  176.5 2.7 fusion.6
  180.5 1.0 constant_dynamic-slice_fusion.1.gates
  181.5 1.7 dynamic-slice_bitcast_fusion.n2
  183.3 83.5 %shard_map.232 = (bf16[1024,1280]{1,0:T(8,128)(2,1)}, f32[128,1408]{1,0:T(8,128)}, bf16[128,1280]{1,0:T(8,128)(2,1)}, bf16[1280,256]{1,0:T(8,128)(2,1)}, f32[224...) custom-call(bf16[1024,1280]{1,0:T(8,128)(2,1)} %bitcast.54, ...), custom_call_target="tpu_custom_call" | custom-call | flops 1000000000 | bytes 1000000000 | tf_op jit(solution)/shard_map/pallas_call | solution.py:721
  266.8 68.4 %shard_map.233 = (f32[128,1280]{1,0:T(8,128)}, f32[24,1280]{1,0:T(8,128)}, bf16[1280,1280]{1,0:T(8,128)(2,1)}, bf16[8,128,256]{2,1,0:T(8,128)(2,1)}, f32[128,128...) custom-call(f32[128,1408]{1,0:T(8,128)} %get-tuple-element.62.row_sum, bf16[8,128,1280]{2,1,0:T(8,128)(2,1)} %bitcast.58, ...), custom_call_target="tpu_custom_call" | custom-call | flops 1000000000 | bytes 1000000000 | tf_op jit(solution)/shard_map/pallas_call | solution.py:721
  335.2 101.1 %shard_map.234 = (f32[128,1280]{1,0:T(8,128)}, bf16[8,40,1024]{2,1,0:T(8,128)(2,1)}, f32[40,1280]{1,0:T(8,128)}, f32[320,1792]{1,0:T(8,128)}, f32[32,1280]{1,0:T(8,128)}, /*index=5*/f32[24,1280]{1,0:T(8,128)}) custom-call(bf16[8,128,256]{2,1,0:T(8,128)(2,1)} %get-tuple-element.69.dattn, bf16[6,1024,128]{2,1,0:T(8,128)(2,1)} %get-tuple-element.70.qkv, ...), custom_call_target="tpu_custom_call" | custom-call | flops 1000000000 | bytes 1000000000 | tf_op jit(solution)/shard_map/pallas_call | solution.py:721
  436.3 1.3 dynamic-slice_bitcast_fusion.2
  437.6 1.4 dynamic-slice_bitcast_fusion.1
  439.0 0.9 slice.72
  439.9 1.2 convert_element_type.39
  443.9 0.8 copy.53
  444.6 1.6 reshape.87
  446.2 3.1 pad_maximum_fusion.1
  449.3 2.4 pad_maximum_fusion
  451.7 0.8 copy.66
  452.6 0.8 copy.67
  453.4 0.7 copy.68
  454.1 0.7 copy.69
  (43 shorter events, 5.3 us)
Async XLA Ops:
  441.2 1.1 copy-start.1
  441.6 0.9 copy-start.9
  442.3 1.5 copy-start
  443.9 2.3 copy-start.4
  446.2 3.1 copy-start.2
  446.2 3.1 copy-start.3
  449.3 2.4 copy-start.5
  449.3 3.3 copy-start.6
  451.7 1.7 copy-start.7
  451.7 2.4 copy-start.8

commit v6 on v5

--- a/solution.py
+++ b/solution.py
@@ -713,6 +713,16 @@
         return out.at[pl.ds(half * half_rows, half_rows)]
 
     return reduce_stages(block, out_half, *scratch)
+
+
+def bring_all(far_refs, near_refs, sem):
+    copies = [
+        pltpu.make_async_copy(far, near, sem.at[i])
+        for i, (far, near) in enumerate(zip(far_refs, near_refs))
+    ]
+    for copy in copies:
+        copy.start()
+    return copies
 
 
 def kernel_call(body, outs, args, scratch, collective_id, far_outs=(), far_args=()):
@@ -989,8 +999,10 @@
 
 
 def middle_kernel(
-    n1, weights, cosine, sine, ids_row, ids_column, w_out, rows, gain, cot, up_weight, down_weight, sdown_weight,
-    qkv, logsum, attn, resid, n2_all, cot_all, up_all, down_all, sdown_all, down_second,
+    n1_far, weights_far, cosine_far, sine_far, ids_row, ids_column, w_out_far, rows, gain, cot, up_weight, down_weight,
+    sdown_weight,
+    qkv, logsum, attn, resid, n2_all, cot_all, up_all, down_all, sdown_all, down_second, n2_own,
+    n1, weights, cosine, sine, w_out, bring_sem,
     attended, up_own, up_wide, down_own, sdown_own, up_sem, a_send, a_recv, *sems,
 ):
     b, e, z, core = place()
@@ -1008,6 +1020,11 @@
     cot_all[e] = low(cot[0])
     bring = pltpu.make_async_copy(up_weight.at[1], up_wide, up_sem.at[0])
     bring.start()
+    brought = bring_all(
+        (n1_far, weights_far, cosine_far, sine_far, w_out_far),
+        (n1, weights, cosine, sine, w_out),
+        bring_sem,
+    )
     greet([(b ^ 1, e), (b ^ 2, e), *mates])
     bring.wait()
     up_own[...] = low(up_wide[...])
@@ -1022,6 +1039,8 @@
     for start, _, _ in spreads[1:]:
         start()
     holds, pair = holder(e)
+    for copy in brought:
+        copy.wait()
 
     @pl.when(jnp.logical_not(holds))
     def _():
@@ -1092,6 +1111,7 @@
     resid[...] = total
     inv = lax.rsqrt(jnp.mean(total * total, axis=1, keepdims=True) + EPSILON)
     n2_all[e] = low(total * inv * gain[...])
+    n2_own[...] = n2_all[e]
     n2_stages[0]()
     cot_stages[3]()
     spreads[2][1]()
@@ -1136,9 +1156,16 @@
             ((4 * down_rows, width), LOW),
             ((4 * sdown_rows, width), LOW),
             ((down_rows, width), LOW),
+            ((tokens, width), LOW),
         ],
         (n1, weights, cosine, sine, ids_row, ids_column, w_out, rows, gain, cot, up_weight, down_weight, sdown_weight),
         [
+            pltpu.VMEM(n1.shape, LOW),
+            pltpu.VMEM(weights.shape, LOW),
+            pltpu.VMEM(cosine.shape, F32),
+            pltpu.VMEM(sine.shape, F32),
+            pltpu.VMEM(w_out.shape, LOW),
+            pltpu.SemaphoreType.DMA((5,)),
             pltpu.VMEM((8, tokens, pair), LOW),
             pltpu.VMEM((up_rows, up_width), LOW),
             pltpu.VMEM((up_rows, up_width), F32),
@@ -1152,14 +1179,14 @@
         + GATHER_SEMS * 2,
         1,
         far_outs=(6, 7, 8),
-        far_args=(10,),
+        far_args=(0, 1, 2, 3, 6, 10),
     )
 
 
 def experts_kernel(
-    n2, cot, w_sup, w_sdown, gates, down_second, up_first, up_second, down_first,
+    n2, cot, columns, w_sdown, gates, down_second, up_first, up_second, down_first,
     out_part, row_sum, sdown_term, sup_term, down_grad, up_term_first, up_term_second, down_term_second,
-    part, up_w, down_w, hid, dpre, hid_shared, dpre_shared, load_sem, store_sem, *scratch,
+    part, w_sup, up_w, down_w, hid, dpre, hid_shared, dpre_shared, load_sem, store_sem, *scratch,
 ):
     e = lax.axis_index("expert")
     length, width = n2.shape
@@ -1168,6 +1195,7 @@
     loads = [
         pltpu.make_async_copy(up_first, up_w.at[0], load_sem.at[0]),
         pltpu.make_async_copy(down_first, down_w.at[0], load_sem.at[1]),
+        pltpu.make_async_copy(columns.at[:, pl.ds(6 * HEAD, 2 * pad)], w_sup, load_sem.at[3]),
         pltpu.make_async_copy(up_second, up_w.at[1], load_sem.at[2]),
     ]
     for copy in loads:
@@ -1179,7 +1207,7 @@
     tokens = part.shape[1]
     greet_near()
     arrive[0]()
-    for copy in loads[:2]:
+    for copy in loads[:3]:
         copy.wait()
     lane = lax.broadcasted_iota(jnp.int32, (ROWS, 128), 1)
 
@@ -1237,7 +1265,7 @@
     def _(i):
         first_pass(i)
 
-    loads[2].wait()
+    loads[3].wait()
     arrive[2]()
 
     @pl.loop(0, length // ROWS)
@@ -1301,7 +1329,7 @@
 COLS = 256
 
 
-def experts_phase(n2, cot, w_sup, w_sdown, gates, down_second, up_first, up_second, down_first):
+def experts_phase(n2, cot, columns, w_sdown, gates, down_second, up_first, up_second, down_first):
     length, width = n2.shape
     hidden = down_first.shape[0]
     pad = w_sdown.shape[0]
@@ -1319,16 +1347,17 @@
             (up_first.shape, LOW),
             ((hidden, width), LOW),
         ],
-        (n2, cot, w_sup, w_sdown, gates, down_second, up_first, up_second, down_first),
+        (n2, cot, columns, w_sdown, gates, down_second, up_first, up_second, down_first),
         [
             pltpu.VMEM((8, tokens, wide), LOW),
+            pltpu.VMEM((width, 2 * pad), LOW),
             pltpu.VMEM((2, *up_first.shape), LOW),
             pltpu.VMEM((2, hidden, width), LOW),
             pltpu.VMEM((2, length, hidden), LOW),
             pltpu.VMEM((2, length, 2 * hidden), LOW),
             pltpu.VMEM((length, pad), LOW),
             pltpu.VMEM((length, 2 * pad), LOW),
-            pltpu.SemaphoreType.DMA((3,)),
+            pltpu.SemaphoreType.DMA((4,)),
             pltpu.SemaphoreType.DMA((3,)),
         ]
         + SPREAD_SEMS
@@ -1337,7 +1366,7 @@
         + SCATTER_SEMS,
         4,
         far_outs=(5, 6, 7),
-        far_args=(6, 7, 8),
+        far_args=(2, 6, 7, 8),
     )
 
 
@@ -1455,9 +1484,10 @@
 
 
 def closing_kernel(
-    dattn, qkv, logsum, n1, weights, cosine, sine, ids_row, ids_column, rows, gain, dresid,
+    dattn, qkv_far, logsum_far, n1_far, weights_far, cosine_far, sine_far, ids_row, ids_column, rows, gain, dresid,
     up_term, sdown_term, sup_term, out_term, small,
     input_grad, columns, out_grad, up_grad, sdown_grad, small_sum,
+    qkv, logsum, n1, weights, cosine, sine, bring_sem,
     dkey, dvalue, dprojected, part, column_term, column_sum, column_low,
     out_near, out_sum, out_low, out_half, out_got, small_got, small_step,
     n_send, n_recv, o_send, o_recv, c_send, c_recv, s_send, s_recv, *scratch,
@@ -1502,11 +1532,16 @@
     near = send(
         out_term.at[:, :, 1 - core], out_near, n_send.at[0], n_recv.at[0], (b, e ^ 1)
     )
+    up[0]()
     near.start()
+    brought = bring_all(
+        (qkv_far, logsum_far, n1_far, weights_far, cosine_far, sine_far),
+        (qkv, logsum, n1, weights, cosine, sine),
+        bring_sem,
+    )
     own = pltpu.make_async_copy(out_term.at[:, :, core], out_sum, n_send.at[1])
     own.start()
     partner(0).start()
-    up[0]()
 
     def attend(head):
         dkey[...] = jnp.zeros_like(dkey)
@@ -1537,6 +1572,9 @@
             turned(dkey[...] * HEAD ** (-0.5), cosine[...], -sine[...])
         )
         dprojected[:, (4 + head) * HEAD : (5 + head) * HEAD] = low(dvalue[...])
+
+    for copy in brought:
+        copy.wait()
 
     @pl.when(holds)
     def _():
@@ -1667,6 +1705,13 @@
             up_term, sdown_term, sup_term, out_term, small,
         ),
         [
+            pltpu.VMEM(qkv.shape, LOW),
+            pltpu.VMEM(logsum.shape, F32),
+            pltpu.VMEM(n1.shape, LOW),
+            pltpu.VMEM(weights.shape, LOW),
+            pltpu.VMEM(cosine.shape, F32),
+            pltpu.VMEM(sine.shape, F32),
+            pltpu.SemaphoreType.DMA((6,)),
             pltpu.VMEM((length, HEAD), F32),
             pltpu.VMEM((length, HEAD), F32),
             pltpu.VMEM((length, 6 * HEAD), LOW),
@@ -1690,7 +1735,7 @@
         + scatter_scratch(tokens, width)
         + SCATTER_SEMS,
         3,
-        far_args=(12, 15),
+        far_args=(1, 2, 3, 4, 5, 6, 12, 15),
     )
 
 
@@ -1765,7 +1810,7 @@
     angle = rotary_angles(length)
     cosine = np.concatenate([np.cos(angle)] * 2, axis=1)
     sine = np.concatenate([-np.sin(angle), np.sin(angle)], axis=1)
-    qkv, logsum, attn, resid, n2_all, cot_all, up_second, down_low, w_sdown, down_second = middle(
+    qkv, logsum, attn, resid, n2_all, cot_all, up_second, down_low, w_sdown, down_second, n2 = middle(
         n1_all,
         columns,
         jnp.asarray(cosine),
@@ -1782,7 +1827,6 @@
     )
     cot_all = cot_all.reshape(length, width)
 
-    n2 = lax.dynamic_index_in_dim(n2_all, e, 0, False)
     n2_all = n2_all.reshape(length, width)
     logits = dot(n2_all, w_router)
     hot = route_all[:, :, None] == jnp.arange(experts, dtype=jnp.int32)[None, None, :]
@@ -1795,7 +1839,7 @@
     output_part, row_sum, sdown_term, sup_term, down_grad_first, *terms = experts_phase(
         n2_all,
         cot_all,
-        columns[:, 3 * pair :],
+        columns,
         w_sdown,
         mine,
         down_second,

time: 463 us -> 456 us (0.985)
  no operation moved by 1% of the time
where the time goes in v6:
time: 456 us; the launch traced here: 449 us
  Pallas kernels  411 us (90%)
  local copies, waits for them, and re-layouts  24.1 us (5%)
  other arithmetic  9.96 us (2%)
    pallas_call x5, Pallas kernels, kernel_call(): pl.pallas_call(body, cost_estimate=pl.CostEstimate(flops=COST, bytes_acce...  411 us

profile of v6, /device:TPU:0, one launch (start us, length us, event | category | flops | bytes accessed | tf_op | source)
XLA Modules:
  0.0 448.6 jit_solution(12482050697348649943)
XLA Ops:
  0.7 0.8 copy.42
  1.4 0.7 reshape.73.router
  2.1 1.4 copy.44.routes
  3.5 1.0 convert_element_type.34
  4.5 1.7 reshape.74
  6.6 1.1 reshape.75.sup
  7.7 85.0 %shard_map.230 = (bf16[8,128,1280]{2,1,0:T(8,128)(2,1)}, f32[2,1280]{1,0:T(2,128)}, f32[8,4,8,128]{3,2,1,0:T(8,128)}, f32[8,8,128]{2,1,0:T(8,128)}, bf16[4,8,40,...) custom-call(f32[128,1280]{1,0:T(8,128)} %bitcast.46, ...), custom_call_target="tpu_custom_call" | custom-call | flops 1000000000 | bytes 1000000000 | tf_op jit(solution)/shard_map/pallas_call | solution.py:731
  92.8 1.4 fusion.5
  94.1 0.8 convert_bitcast_fusion
  94.9 0.9 fusion.3
  96.1 0.8 copy.51
  97.5 1.6 fusion.4
  99.1 73.9 %shard_map.231 = (bf16[6,1024,128]{2,1,0:T(8,128)(2,1)}, f32[2,1024,128]{2,1,0:T(8,128)}, bf16[5,128,256]{2,1,0:T(8,128)(2,1)}, f32[128,1280]{1,0:T(8,128)}, bf1...) custom-call(bf16[1024,1280]{1,0:T(8,128)(2,1)} %bitcast.44, ...), custom_call_target="tpu_custom_call" | custom-call | flops 1000000000 | bytes 1000000000 | tf_op jit(solution)/shard_map/pallas_call | solution.py:731
  173.1 2.7 fusion.6
  176.5 0.6 constant_dynamic-slice_fusion.gates
  177.1 1.0 constant_dynamic-slice_fusion.1.gates
  178.1 84.7 %shard_map.232 = (bf16[1024,1280]{1,0:T(8,128)(2,1)}, f32[128,1408]{1,0:T(8,128)}, bf16[128,1280]{1,0:T(8,128)(2,1)}, bf16[1280,256]{1,0:T(8,128)(2,1)}, f32[224...) custom-call(bf16[1024,1280]{1,0:T(8,128)(2,1)} %bitcast.56, ...), custom_call_target="tpu_custom_call" | custom-call | flops 1000000000 | bytes 1000000000 | tf_op jit(solution)/shard_map/pallas_call | solution.py:731
  262.8 68.3 %shard_map.233 = (f32[128,1280]{1,0:T(8,128)}, f32[24,1280]{1,0:T(8,128)}, bf16[1280,1280]{1,0:T(8,128)(2,1)}, bf16[8,128,256]{2,1,0:T(8,128)(2,1)}, f32[128,128...) custom-call(f32[128,1408]{1,0:T(8,128)} %get-tuple-element.63.row_sum, bf16[8,128,1280]{2,1,0:T(8,128)(2,1)} %bitcast.54, ...), custom_call_target="tpu_custom_call" | custom-call | flops 1000000000 | bytes 1000000000 | tf_op jit(solution)/shard_map/pallas_call | solution.py:731
  331.2 98.5 %shard_map.234 = (f32[128,1280]{1,0:T(8,128)}, bf16[8,40,1024]{2,1,0:T(8,128)(2,1)}, f32[40,1280]{1,0:T(8,128)}, f32[320,1792]{1,0:T(8,128)}, f32[32,1280]{1,0:T(8,128)}, /*index=5*/f32[24,1280]{1,0:T(8,128)}) custom-call(bf16[8,128,256]{2,1,0:T(8,128)(2,1)} %get-tuple-element.71.dattn, bf16[6,1024,128]{2,1,0:T(8,128)(2,1)} %get-tuple-element.72.qkv_far, ...), custom_call_target="tpu_custom_call" | custom-call | flops 1000000000 | bytes 1000000000 | tf_op jit(solution)/shard_map/pallas_call | solution.py:731
  429.7 1.3 dynamic-slice_bitcast_fusion.1
  431.0 1.4 dynamic-slice_bitcast_fusion
  432.4 0.9 slice.67
  433.3 1.2 convert_element_type.39
  436.4 0.6 reshape.86
  437.3 0.8 copy.53
  438.1 1.6 reshape.87
  439.6 3.1 pad_maximum_fusion.1
  442.7 2.4 pad_maximum_fusion
  445.1 0.8 copy.66
  446.0 0.8 copy.67
  446.8 0.7 copy.68
  447.5 0.7 copy.69
  (41 shorter events, 4.1 us)
Async XLA Ops:
  434.7 1.1 copy-start.1
  435.0 0.9 copy-start.9
  435.7 1.5 copy-start
  437.3 2.3 copy-start.4
  439.6 3.1 copy-start.2
  439.6 3.1 copy-start.3
  442.7 2.4 copy-start.5
  442.7 3.3 copy-start.6
  445.1 1.7 copy-start.7
  445.1 2.4 copy-start.8

commit v7 on v6

--- a/solution.py
+++ b/solution.py
@@ -1184,8 +1184,8 @@
 
 
 def experts_kernel(
-    n2, cot, columns, w_sdown, gates, down_second, up_first, up_second, down_first,
-    out_part, row_sum, sdown_term, sup_term, down_grad, up_term_first, up_term_second, down_term_second,
+    n2, cot, columns, w_sdown, w_router, marks_all, down_second, up_first, up_second, down_first,
+    gates, out_part, row_sum, sdown_term, sup_term, down_grad, up_term_first, up_term_second, down_term_second,
     part, w_sup, up_w, down_w, hid, dpre, hid_shared, dpre_shared, load_sem, store_sem, *scratch,
 ):
     e = lax.axis_index("expert")
@@ -1210,9 +1210,19 @@
     for copy in loads[:3]:
         copy.wait()
     lane = lax.broadcasted_iota(jnp.int32, (ROWS, 128), 1)
+    number = lax.broadcasted_iota(jnp.int32, (ROWS, w_router.shape[1]), 1)
+
+    def weigh(here, x):
+        chosen = number == marks_all[here, 0:1]
+        for j in range(1, TOP):
+            chosen = chosen | (number == marks_all[here, j : j + 1])
+        logits = jnp.where(chosen, dot(x, w_router[...]), NEGATIVE)
+        weight = jnp.exp(logits - jnp.max(logits, axis=1, keepdims=True))
+        weight = jnp.where(chosen, weight, 0.0)
+        gates[here, :] = weight / jnp.sum(weight, axis=1, keepdims=True)
 
     def routed(k, here, x, c):
-        gate = gates[here, k : k + 1]
+        gate = jnp.sum(jnp.where(number == 2 * e + k, gates[here, :], 0.0), axis=1, keepdims=True)
         gate_part = dot(x, up_w[k, :, :hidden])
         up_part = dot(x, up_w[k, :, hidden:])
         back = dot(c, down_w[k], ((1,), (1,)))
@@ -1236,6 +1246,7 @@
         here = pl.ds(pl.multiple_of(i * ROWS, ROWS), ROWS)
         x = n2[here, :]
         c = cot[here, :]
+        weigh(here, x)
         gate_part = dot(x, w_sup[:, :pad])
         up_part = dot(x, w_sup[:, pad:])
         back = dot(c, w_sdown[...], ((1,), (1,)))
@@ -1329,7 +1340,9 @@
 COLS = 256
 
 
-def experts_phase(n2, cot, columns, w_sdown, gates, down_second, up_first, up_second, down_first):
+def experts_phase(
+    n2, cot, columns, w_sdown, w_router, marks, down_second, up_first, up_second, down_first
+):
     length, width = n2.shape
     hidden = down_first.shape[0]
     pad = w_sdown.shape[0]
@@ -1338,6 +1351,7 @@
     return kernel_call(
         experts_kernel,
         [
+            ((length, w_router.shape[1]), F32),
             ((length, width), LOW),
             ((tokens, wide), F32),
             ((pad, width), LOW),
@@ -1347,7 +1361,7 @@
             (up_first.shape, LOW),
             ((hidden, width), LOW),
         ],
-        (n2, cot, columns, w_sdown, gates, down_second, up_first, up_second, down_first),
+        (n2, cot, columns, w_sdown, w_router, marks, down_second, up_first, up_second, down_first),
         [
             pltpu.VMEM((8, tokens, wide), LOW),
             pltpu.VMEM((width, 2 * pad), LOW),
@@ -1365,8 +1379,8 @@
         + scatter_scratch(tokens, wide)
         + SCATTER_SEMS,
         4,
-        far_outs=(5, 6, 7),
-        far_args=(2, 6, 7, 8),
+        far_outs=(6, 7, 8),
+        far_args=(2, 7, 8, 9),
     )
 
 
@@ -1391,7 +1405,7 @@
     width = upstream.shape[1]
     experts = gates.shape[1]
     dgate = total[:, width : width + experts] + total[:, width + experts : width + 2 * experts]
-    own = gates[...]
+    own = gates[pl.ds(pl.multiple_of(e * upstream.shape[0], 128), upstream.shape[0]), :]
     dlog = low(own * (dgate - jnp.sum(own * dgate, axis=1, keepdims=True)))
     dn2 = total[:, :width] + dot(dlog, w_router[...])
     rows = resid[...]
@@ -1802,7 +1816,6 @@
     gain_first = gains[0:1]
     gain_second = gains[1:2]
     marks = marks.astype(jnp.int32).transpose(0, 2, 1).reshape(length, 8)
-    route_all = marks[:, :TOP]
     ids_all = marks[:, TOP]
     positions = jnp.arange(length, dtype=jnp.int32)
     ids_row = ids_all[None, :]
@@ -1828,32 +1841,24 @@
     cot_all = cot_all.reshape(length, width)
 
     n2_all = n2_all.reshape(length, width)
-    logits = dot(n2_all, w_router)
-    hot = route_all[:, :, None] == jnp.arange(experts, dtype=jnp.int32)[None, None, :]
-    routed_to = jnp.any(hot, axis=1)
-    logits = jnp.where(routed_to, logits, NEGATIVE)
-    gates = jnp.where(routed_to, jnp.exp(logits - jnp.max(logits, axis=1, keepdims=True)), 0.0)
-    gates = gates / jnp.sum(gates, axis=1, keepdims=True)
-    mine = lax.dynamic_slice_in_dim(gates, 2 * e, 2, 1)
-
-    output_part, row_sum, sdown_term, sup_term, down_grad_first, *terms = experts_phase(
+    gates, output_part, row_sum, sdown_term, sup_term, down_grad_first, *terms = experts_phase(
         n2_all,
         cot_all,
         columns,
         w_sdown,
-        mine,
+        w_router,
+        marks,
         down_second,
         up_first,
         up_second,
         down_low,
     )
     up_terms, down_term_second = terms[:2], terms[2]
-    own_gates = lax.dynamic_slice_in_dim(gates, e * tokens, tokens, 0)
     dresid, small, out_term, dattn, output_rows, up_grad_first, down_grad_second = turn(
         row_sum,
         output_part.reshape(8, tokens, width),
         upstream,
-        own_gates,
+        gates,
         w_router.T,
         resid,
         gain_second,

time: 456 us -> 450 us (0.987)
  no operation moved by 1% of the time
where the time goes in v7:
time: 450 us; the launch traced here: 442 us
  Pallas kernels  411 us (91%)
  local copies, waits for them, and re-layouts  19.6 us (4%)
  other arithmetic  9.53 us (2%)
    pallas_call x5, Pallas kernels, kernel_call(): pl.pallas_call(body, cost_estimate=pl.CostEstimate(flops=COST, bytes_acce...  411 us

profile of v7, /device:TPU:0, one launch (start us, length us, event | category | flops | bytes accessed | tf_op | source)
XLA Modules:
  0.0 442.0 jit_solution(8649822268828972550)
XLA Ops:
  0.7 1.0 convert_element_type.28
  1.7 1.7 reshape.70
  3.5 0.3 copy.34
  3.8 1.1 reshape.71.sup
  4.9 0.7 copy.35.routes
  5.7 0.7 reshape.69.router
  6.4 85.1 %shard_map.230 = (bf16[8,128,1280]{2,1,0:T(8,128)(2,1)}, f32[2,1280]{1,0:T(2,128)}, f32[8,4,8,128]{3,2,1,0:T(8,128)}, f32[8,8,128]{2,1,0:T(8,128)}, bf16[4,8,40,...) custom-call(f32[128,1280]{1,0:T(8,128)} %bitcast.43, ...), custom_call_target="tpu_custom_call" | custom-call | flops 1000000000 | bytes 1000000000 | tf_op jit(solution)/shard_map/pallas_call | solution.py:731
  91.4 0.8 convert_bitcast_fusion
  92.4 1.6 fusion.1
  94.0 1.4 fusion.2
  95.4 74.0 %shard_map.231 = (bf16[6,1024,128]{2,1,0:T(8,128)(2,1)}, f32[2,1024,128]{2,1,0:T(8,128)}, bf16[5,128,256]{2,1,0:T(8,128)(2,1)}, f32[128,1280]{1,0:T(8,128)}, bf1...) custom-call(bf16[1024,1280]{1,0:T(8,128)(2,1)} %bitcast.41, ...), custom_call_target="tpu_custom_call" | custom-call | flops 1000000000 | bytes 1000000000 | tf_op jit(solution)/shard_map/pallas_call | solution.py:731
  169.5 1.0 convert_element_type.31.w_router
  170.4 85.7 %shard_map.232 = (f32[1024,16]{1,0:T(8,128)}, bf16[1024,1280]{1,0:T(8,128)(2,1)}, f32[128,1408]{1,0:T(8,128)}, bf16[128,1280]{1,0:T(8,128)(2,1)}, bf16[1280,256]...) custom-call(bf16[1024,1280]{1,0:T(8,128)(2,1)} %bitcast.52, ...), custom_call_target="tpu_custom_call" | custom-call | flops 1000000000 | bytes 1000000000 | tf_op jit(solution)/shard_map/pallas_call | solution.py:731
  256.1 0.8 copy.38
  256.9 68.1 %shard_map.233 = (f32[128,1280]{1,0:T(8,128)}, f32[24,1280]{1,0:T(8,128)}, bf16[1280,1280]{1,0:T(8,128)(2,1)}, bf16[8,128,256]{2,1,0:T(8,128)(2,1)}, f32[128,128...) custom-call(f32[128,1408]{1,0:T(8,128)} %get-tuple-element.64.row_sum, bf16[8,128,1280]{2,1,0:T(8,128)(2,1)} %bitcast.51, ...), custom_call_target="tpu_custom_call" | custom-call | flops 1000000000 | bytes 1000000000 | tf_op jit(solution)/shard_map/pallas_call | solution.py:731
  325.0 2.8 pad_maximum_fusion.1
  327.8 98.6 %shard_map.234 = (f32[128,1280]{1,0:T(8,128)}, bf16[8,40,1024]{2,1,0:T(8,128)(2,1)}, f32[40,1280]{1,0:T(8,128)}, f32[320,1792]{1,0:T(8,128)}, f32[32,1280]{1,0:T(8,128)}, /*index=5*/f32[24,1280]{1,0:T(8,128)}) custom-call(bf16[8,128,256]{2,1,0:T(8,128)(2,1)} %get-tuple-element.73.dattn, bf16[6,1024,128]{2,1,0:T(8,128)(2,1)} %get-tuple-element.74.qkv_far, ...), custom_call_target="tpu_custom_call" | custom-call | flops 1000000000 | bytes 1000000000 | tf_op jit(solution)/shard_map/pallas_call | solution.py:731
  426.5 4.2 pad_maximum_fusion
  430.9 0.3 reshape.80
  431.2 0.4 copy.39
  431.6 0.2 reshape.81
  432.1 0.5 convert_divide_fusion
  432.7 0.6 reshape.82
  433.2 0.2 slice_bitcast_fusion
  433.5 0.8 copy.40
  434.3 1.6 reshape.83
  435.9 1.4 dynamic-slice_bitcast_fusion
  437.2 1.3 dynamic-slice_bitcast_fusion.1
  438.5 0.8 copy.49
  439.4 0.8 copy.50
  440.2 0.7 copy.51
  440.9 0.7 copy.52
  (43 shorter events, 1.0 us)
Async XLA Ops:
  0.6 4.2 copy-start.13
  0.7 5.0 %copy-start.12 = (f32[40,16]{0,1:T(8,128)S(1)}, f32[40,16]{0,1:T(8,128)}, u32[]{:S(2)}) copy-start(f32[40,16]{0,1:T(8,128)} %param.23) | copy-start | bytes 7684
  92.4 77.0 %copy-start = (s32[8,128,8]{2,1,0:T(8,128)}, s32[8,128,8]{2,1,0:T(8,128)S(1)}, u32[]{:S(2)}) copy-start(s32[8,128,8]{2,1,0:T(8,128)S(1)} %copy.36) | copy-start | bytes 98308
  95.4 74.0 %copy-start.11 = (f32[8,4,8,128]{3,2,1,0:T(8,128)S(1)}, f32[8,4,8,128]{3,2,1,0:T(8,128)}, u32[]{:S(2)}) copy-start(f32[8,4,8,128]{3,2,1,0:T(8,128)} %get-tuple-element.59) | copy-start | bytes 393220
  170.4 85.7 %copy-start.1 = (bf16[1280,16]{1,0:T(8,128)(2,1)S(1)}, bf16[1280,16]{1,0:T(8,128)(2,1)}, u32[]{:S(2)}) copy-start(bf16[1280,16]{1,0:T(8,128)(2,1)} %convert_element_type.31.w_router) | copy-start | bytes 122884
  256.9 68.1 %copy-start.6 = (f32[224,1280]{1,0:T(8,128)S(1)}, f32[224,1280]{1,0:T(8,128)}, u32[]{:S(2)}) copy-start(f32[224,1280]{1,0:T(8,128)} %get-tuple-element.89) | copy-start | bytes 3440644
  327.8 98.7 %copy-start.4 = (f32[320,1792]{1,0:T(8,128)S(1)}, f32[320,1792]{1,0:T(8,128)}, u32[]{:S(2)}) copy-start(f32[320,1792]{1,0:T(8,128)} %get-tuple-element.87) | copy-start | bytes 6881284
  426.5 4.2 copy-start.5
  430.9 1.1 copy-start.3
  431.2 0.9 copy-start.14
  431.9 1.6 copy-start.2
  433.5 5.0 %copy-start.7 = (f32[128,1280]{1,0:T(8,128)S(1)}, f32[128,1280]{1,0:T(8,128)}, u32[]{:S(2)}) copy-start(f32[128,1280]{1,0:T(8,128)} %get-tuple-element.72) | copy-start | bytes 1966084
  433.5 5.9 %copy-start.8 = (f32[128,1280]{1,0:T(8,128)S(1)}, f32[128,1280]{1,0:T(8,128)}, u32[]{:S(2)}) copy-start(f32[128,1280]{1,0:T(8,128)} %get-tuple-element.82) | copy-start | bytes 1966084
  434.3 5.9 %copy-start.9 = (f32[40,1280]{1,0:T(8,128)S(1)}, f32[40,1280]{1,0:T(8,128)}, u32[]{:S(2)}) copy-start(f32[40,1280]{1,0:T(8,128)} %get-tuple-element.109) | copy-start | bytes 614404
  434.3 6.6 %copy-start.10 = (f32[32,1280]{1,0:T(8,128)S(1)}, f32[32,1280]{1,0:T(8,128)}, u32[]{:S(2)}) copy-start(f32[32,1280]{1,0:T(8,128)} %get-tuple-element.85) | copy-start | bytes 491524
